TPU v7x, 512 devices: a whole 4x8x8 slice. The times are simulated.
512 devices in a mesh: clip: 16 (over x_lo, y), act: 32 (over z, x_hi, core).
Axes of the slice: x: 4 (x_hi: 2, x_lo: 2; x = x_hi * 2 + x_lo), y: 8, z: 8, core: 2. Of those that a mesh axis runs over, the one named last changes fastest.
Arguments:
- clips: float32 [1024, 8192], P('act', 'clip'), may hold values from -6 to 6
- actions: float32 [1024, 16384], P('clip', 'act'), may hold values from -6 to 6
- positive_ids: int32 [8192], P('clip'), may hold values from 0 to 16383
- robot_ids: int32 [16384], P('act'), may hold values from 0 to 15
- robot_bias: float32 [16], replicated, may hold values from -4 to 0
Outputs:
- clip_grad: float32 [1024, 8192], P('act', 'clip')
- action_grad: float32 [1024, 16384], P('clip', 'act')
- loss: float32 [], replicated
All inputs are finite; a program needn't handle non-finite values.
Results may differ from a plain program's by a relative error of at most 0.019.
Values may be sent and summed in bfloat16 or wider, within the bound.
No kernel may reach another device: no remote copies, remote signals or barrier semaphores. Data moves between devices by JAX's collectives and lax.ppermute only.
A program may use at most 64 MiB of HBM per device.

v0:
```python
import math

import jax
import jax.numpy as jnp
from jax import lax
from jax.sharding import PartitionSpec as P


def shards(clips, actions, positive_ids, robot_ids, robot_bias):
    clip_full = lax.all_gather(clips.astype(jnp.bfloat16), "act", axis=0, tiled=True)
    action_full = lax.all_gather(actions.astype(jnp.bfloat16), "clip", axis=0, tiled=True)
    width = clip_full.shape[0]
    clip_rows_dev = clip_full.shape[1]
    action_rows_dev = action_full.shape[1]
    total_actions = action_rows_dev * lax.axis_size("act")
    total_clips = clip_rows_dev * lax.axis_size("clip")
    onehot = (
        robot_ids[:, None] == jnp.arange(robot_bias.shape[0], dtype=jnp.int32)[None, :]
    ).astype(jnp.float32)
    bias_row = jnp.dot(onehot, robot_bias, precision=lax.Precision.HIGHEST)
    logits = lax.dot_general(
        clip_full, action_full, (((0,), (0,)), ((), ())), preferred_element_type=jnp.float32
    )
    logits = logits * (2.0 / math.sqrt(width)) + bias_row[None, :]
    columns = lax.axis_index("act") * action_rows_dev + jnp.arange(action_rows_dev, dtype=jnp.int32)
    sign = jnp.where(positive_ids[:, None] == columns[None, :], 1.0, -1.0).astype(jnp.float32)
    margin = -sign * logits
    loss_part = jnp.sum(jnp.logaddexp(jnp.float32(0.0), margin))
    weights = (-sign * jax.nn.sigmoid(margin)).astype(jnp.bfloat16)
    partial_rows = lax.dot_general(
        action_full, weights, (((1,), (1,)), ((), ())), preferred_element_type=jnp.float32
    )
    clip_part = lax.psum_scatter(
        partial_rows.astype(jnp.bfloat16), "act", scatter_dimension=0, tiled=True
    ).astype(jnp.float32)
    clip_grad = clip_part / math.sqrt(total_actions)
    action_partial = jnp.dot(clip_full, weights, preferred_element_type=jnp.float32)
    action_grad = lax.psum_scatter(
        action_partial.astype(jnp.bfloat16), "clip", scatter_dimension=0, tiled=True
    ).astype(jnp.float32) / math.sqrt(total_clips)
    loss = lax.psum(loss_part, ("clip", "act")) / (total_clips * total_actions)
    return (clip_grad, action_grad, loss)


def solution(mesh):
    return jax.shard_map(
        shards,
        mesh=mesh,
        in_specs=(P("act", "clip"), P("clip", "act"), P("clip"), P("act"), P()),
        out_specs=(P("act", "clip"), P("clip", "act"), P()),
        check_vma=False,
    )
```

profile of v0, /device:TPU:4, one launch (start us, length us, event | category | flops | bytes accessed | tf_op | source)
XLA Modules:
  0.0 382.6 jit_solution(10988881435882111706)
XLA Ops:
  7.2 0.0 all-gather.5.cloned.1.call-start
  7.2 1.5 convert_element_type.29
  8.8 0.0 all-gather.5.cloned.1.call-update
  8.8 0.0 all-gather.3.cloned.1.call-start
  8.8 1.5 convert_element_type.28
  10.3 0.0 all-gather.3.cloned.1.call-update
  10.3 0.0 reduce-scatter.7.cloned.1.call-start
  10.4 1.0 fusion.4
  11.4 75.3 %all-gather.5.cloned.1.call-done = bf16[1024,512]{1,0:T(8,128)(2,1)} async-done(((bf16[64,512]{1,0:T(8,128)(2,1)}), bf16[1024,512]{1,0:T(8,128)(2,1)}) %all-gather.5.cloned.1.call-update) | async-done | bytes 1048592 | tf_op jit(solution)/shard_map/all_gather | solution.py:11
  86.7 83.9 %all-gather.3.cloned.1.call-done = bf16[1024,512]{1,0:T(8,128)(2,1)} async-done(((bf16[32,512]{1,0:T(8,128)(2,1)}), bf16[1024,512]{1,0:T(8,128)(2,1)}) %all-gather.3.cloned.1.call-update) | async-done | bytes 1048592 | tf_op jit(solution)/shard_map/all_gather | solution.py:10
  170.6 3.7 select_reduce_fusion
  174.4 0.9 fusion.2
  175.3 1.3 copy.12
  176.6 0.0 reduce-scatter.9.cloned.1.call-start
  176.7 1.1 copy-done.1
  177.8 1.0 fusion.3
  178.8 1.3 copy.14
  180.1 96.8 %psum.7 = f32[]{:T(128)} all-reduce(f32[]{:T(128)} %get-tuple-element.9), channel_id=1, replica_groups=mesh['clip'=16,'act'=32] {'clip','act'}, use_global_device_ids=true, to_apply=%region_3.4 | all-reduce | flops 1 | bytes 8 | tf_op jit(solution)/shard_map/psum | solution.py:41
  277.6 20.5 %reduce-scatter.7.cloned.1.call-done = bf16[32,512]{1,0:T(8,128)(2,1)} async-done(((bf16[1024,512]{1,0:T(8,128)(2,1)}), bf16[32,512]{1,0:T(8,128)(2,1)}) %reduce-scatter.7.cloned.1.call-update) | async-done | bytes 32784
  298.1 0.9 copy.13
  299.0 0.7 copy.10
  299.8 73.4 %reduce-scatter.9.cloned.1.call-done = bf16[64,512]{1,0:T(8,128)(2,1)} async-done(((bf16[1024,512]{1,0:T(8,128)(2,1)}), bf16[64,512]{1,0:T(8,128)(2,1)}) %reduce-scatter.9.cloned.1.call-update) | async-done | bytes 65552
  373.2 1.0 copy.15
  374.2 0.8 copy.11
  (12 shorter events, 0.1 us)
Async XLA Ops:
  7.2 3.2 copy-start
  7.2 79.5 %all-gather.5.cloned.1.call-start = ((), (), s32[]{:S(2)}) async-start(), calls=%async_computation.3 | async-start | bytes 1114112 | tf_op jit(solution)/shard_map/all_gather | solution.py:11
  8.8 161.8 %all-gather.3.cloned.1.call-start = ((), (), s32[]{:S(2)}) async-start(), calls=%async_computation.2 | async-start | bytes 1081344 | tf_op jit(solution)/shard_map/all_gather | solution.py:10
  10.3 287.8 %reduce-scatter.7.cloned.1.call-start = ((), (), s32[]{:S(2)}) async-start(), calls=%async_computation.4 | async-start | bytes 1081344
  170.6 3.7 copy-start.2
  170.6 3.7 copy-start.3
  176.6 1.2 copy-start.1
  176.6 196.6 %reduce-scatter.9.cloned.1.call-start = ((), (), s32[]{:S(2)}) async-start(), calls=%async_computation.5 | async-start | bytes 1114112
Sparse Core Ops, SparseCore 0:
  10.7 75.9 all-gather.4
  90.6 79.9 all-gather.2
  176.7 121.3 reduce-scatter.6
  301.0 72.1 reduce-scatter.8
where the time goes:
time: 383 us
  waiting for transfers between devices  253 us (66%)
  blocking collectives  96.8 us (25%)
  between operations  15.6 us (4%)
  local copies, waits for them, and re-layouts  7.16 us (2%)
  matrix products  6.59 us (2%)
    psum x1, blocking collectives, shards(): loss = lax.psum(loss_part, ('clip', 'act')) / (total_clips * total_actions)  96.8 us
    unnamed x6, waiting for transfers between devices  94 us
    all_gather x1, waiting for transfers between devices, shards(): lax.all_gather(clips.astype(jnp.bfloat16), 'act', axis=0, tiled=True)  83.9 us
    all_gather x1, waiting for transfers between devices, shards(): lax.all_gather(actions.astype(jnp.bfloat16), 'clip', axis=0, tiled=True)  75.3 us
  transfers between devices with their start and end apart: 4, of which 4 were waited for; matrix products, arithmetic and copies ran while one was open for 2% of the time, Pallas kernels for 0%

commit v1 on v0

v1 whole, which is shorter than its diff:
```python
import functools
import math

import jax
import jax.numpy as jnp
from jax import lax
from jax.experimental import pallas as pl
from jax.experimental.pallas import tpu as pltpu
from jax.sharding import PartitionSpec as P

BF16 = jnp.bfloat16
F32 = jnp.float32
LANES = 128
EXTRA = 16
VMEM = pl.BlockSpec(memory_space=pltpu.VMEM)
SMEM = pl.BlockSpec(memory_space=pltpu.SMEM)


def pieces(value):
    high = value.astype(BF16).astype(F32)
    middle = (value - high).astype(BF16).astype(F32)
    low = (value - high - middle).astype(BF16).astype(F32)
    return high, middle, low


def loss_rows(value, shape):
    high, middle, low = pieces(value)
    row = lax.broadcasted_iota(jnp.int32, shape, len(shape) - 2)
    rows = jnp.where(row < 4, high, jnp.where(row < 8, middle, jnp.where(row < 12, low, 0.0)))
    return rows.astype(BF16)


def store_blocks(out_ref, values, first_column):
    blocks = out_ref.shape[0]
    rows = values.shape[0] // blocks
    for part in range(values.shape[1] // LANES):
        at = (first_column // LANES + part) * rows
        columns = values[:, part * LANES : (part + 1) * LANES]
        out_ref[:, at : at + rows, :] = columns.reshape(blocks, rows, LANES).astype(BF16)


def logits_kernel(scale, step, core_ref, own_ref, got_ref, row_bias_ref, column_bias_ref, row_key_ref, column_key_ref,
                  weights_ref, grad_ref, loss_ref):
    core = core_ref[0]
    blocks, _, rows, count = own_ref.shape
    width = blocks * rows
    own = own_ref[:, core].reshape(width, count)
    own_t = own.T
    total = jnp.zeros((1, 1), F32)
    for start in range(0, got_ref.shape[1], step):
        got = got_ref[:, start : start + step]
        logits = jnp.dot(own_t, got, preferred_element_type=F32) * scale
        logits = logits + row_bias_ref[...] + column_bias_ref[:, start : start + step]
        positive = row_key_ref[...] == column_key_ref[:, start : start + step]
        margin = jnp.where(positive, -logits, logits)
        small = jnp.exp(-jnp.abs(margin))
        loss = jnp.maximum(margin, 0.0) + jnp.log1p(small)
        sigmoid = jnp.where(margin >= 0.0, 1.0, small) / (1.0 + small)
        weights = jnp.where(positive, -sigmoid, sigmoid).astype(BF16)
        weights_ref[:, start : start + step] = weights
        total = total + jnp.sum(loss, keepdims=True)
        store_blocks(grad_ref, jnp.dot(own, weights, preferred_element_type=F32), start)
    shape = (grad_ref.shape[0], EXTRA, LANES)
    grad_ref[:, grad_ref.shape[1] - EXTRA :, :] = loss_rows(jnp.broadcast_to(total.reshape(1, 1, 1), shape), shape)
    loss_ref[...] = total


def second_kernel(step, got_ref, weights_ref, grad_ref):
    for start in range(0, weights_ref.shape[0], step):
        weights = weights_ref[start : start + step, :]
        grad = lax.dot_general(got_ref[...], weights, (((1,), (1,)), ((), ())), preferred_element_type=F32)
        store_blocks(grad_ref, grad, start)


def vmem_call(kernel, out_shape, in_specs, flops=0, moved=0):
    return pl.pallas_call(
        kernel,
        out_shape=out_shape,
        in_specs=in_specs,
        out_specs=jax.tree.map(lambda _: VMEM, out_shape),
        compiler_params=pltpu.CompilerParams(vmem_limit_bytes=40 * 1024 * 1024),
        cost_estimate=pl.CostEstimate(flops=flops, bytes_accessed=moved, transcendentals=0),
    )


def summed(received, rows):
    total = jnp.sum(received.astype(F32), axis=0)
    parts = (total.shape[0] - EXTRA) // rows
    grad = total[: parts * rows].reshape(parts, rows, LANES).transpose(1, 0, 2).reshape(rows, parts * LANES)
    at = parts * rows
    return grad, total[at, 0] + total[at + 4, 0] + total[at + 8, 0]


def shards(n_clip, n_act, clips, actions, positive_ids, robot_ids, robot_bias):
    both = ("clip", "act")
    pairs = n_act // 2
    core = lax.axis_index("act") % 2
    first = core == 0
    along_act = [[[k * n_act + 2 * m + c for m in range(pairs)] for k in range(n_clip)] for c in range(2)]
    along_clip = [[[k * n_act + 2 * m + c for k in range(n_clip)] for m in range(pairs)] for c in range(2)]
    clips_first = along_act[0] + along_clip[1]
    actions_first = along_clip[0] + along_act[1]
    swap = [(i, i ^ 1) for i in range(n_act)]
    exchange = functools.partial(lax.all_to_all, axis_name=both, split_axis=0, concat_axis=0)

    clip_half = clips.astype(BF16)
    action_half = actions.astype(BF16)
    rows = action_half.shape[0]
    count = action_half.shape[1]
    width = rows * n_clip
    clip_twice = jnp.concatenate([clip_half, clip_half], axis=0)
    other = lax.ppermute(jnp.where(first, action_half, clip_twice), "act", swap)
    clip_pair = jnp.concatenate([clip_half, other[: rows // 2]], axis=0)
    chunk = jnp.stack([jnp.where(first, clip_pair, other), action_half])
    gathered = exchange(jnp.broadcast_to(chunk[None], (n_clip, 2, rows, count)), axis_index_groups=clips_first)
    got = lax.ppermute(gathered[:, 0].reshape(width, count), "act", swap)

    onehot = (robot_ids[:, None] == jnp.arange(robot_bias.shape[0], dtype=jnp.int32)[None, :]).astype(F32)
    bias = jnp.dot(onehot, robot_bias, precision=lax.Precision.HIGHEST)
    columns = lax.axis_index("act") * count + jnp.arange(count, dtype=jnp.int32)
    zero = jnp.zeros_like(bias)
    row_bias = jnp.where(first, zero, bias)[:, None]
    column_bias = jnp.where(first, bias, zero)[None, :]
    row_key = jnp.where(first, positive_ids, columns)[:, None]
    column_key = jnp.where(first, columns, positive_ids)[None, :]

    parts = count // LANES
    flops = 2 * width * count * count
    weights, near, loss = vmem_call(
        functools.partial(logits_kernel, 2.0 / math.sqrt(width), 256),
        (
            jax.ShapeDtypeStruct((count, count), BF16),
            jax.ShapeDtypeStruct((n_clip, parts * rows + EXTRA, LANES), BF16),
            jax.ShapeDtypeStruct((1, 1), F32),
        ),
        [SMEM] + [VMEM] * 6,
        2 * flops,
        8 * width * count,
    )(core.astype(jnp.int32).reshape(1), gathered, got, row_bias, column_bias, row_key, column_key)
    near_got = exchange(near, axis_index_groups=actions_first)
    far = vmem_call(
        functools.partial(second_kernel, 256),
        jax.ShapeDtypeStruct((n_clip, parts * rows, LANES), BF16),
        [VMEM, VMEM],
        flops,
        4 * width * count,
    )(got, weights)
    near_sum, near_loss = summed(near_got, rows)
    shape = (n_clip, EXTRA, LANES)
    far = jnp.concatenate([far, loss_rows(jnp.broadcast_to(near_loss, shape), shape)], axis=1)
    far_got = exchange(far, axis_index_groups=clips_first)
    far_sum, far_loss = summed(far_got, rows)

    action_grad = jnp.where(first, near_sum, far_sum)
    clip_sum = jnp.where(first, far_sum, near_sum)
    half = rows // 2
    keep = jnp.where(first, clip_sum[:half], clip_sum[half:])
    give = jnp.where(first, clip_sum[half:], clip_sum[:half])
    give = jnp.concatenate([give, jnp.broadcast_to(far_loss, (8, count))], axis=0)
    taken = lax.ppermute(give, "act", swap)
    clip_grad = keep + taken[:half]
    loss = far_loss + taken[half, 0]
    total_clips = count * n_clip
    total_actions = count * n_act
    return (
        clip_grad / math.sqrt(total_actions),
        action_grad / math.sqrt(total_clips),
        loss / (total_clips * total_actions),
    )


def solution(mesh):
    return jax.shard_map(
        functools.partial(shards, mesh.shape["clip"], mesh.shape["act"]),
        mesh=mesh,
        in_specs=(P("act", "clip"), P("clip", "act"), P("clip"), P("act"), P()),
        out_specs=(P("act", "clip"), P("clip", "act"), P()),
        check_vma=False,
    )
```

time: 383 us -> 127 us (0.33)
  the two profiles are of different devices: /device:TPU:4 before, /device:TPU:1 now
where the time goes in v1:
time: 127 us; the launch traced here: 126 us
  blocking collectives  54.7 us (43%)
  starting transfers between devices  28.1 us (22%)
  waiting for transfers between devices  21 us (17%)
  between operations  6.55 us (5%)
  local copies, waits for them, and re-layouts  6.3 us (5%)
  other arithmetic  5.13 us (4%)
  Pallas kernels  4.23 us (3%)
    all_to_all x1, blocking collectives, shards(): exchange(jnp.broadcast_to(chunk[None], (n_clip, 2, rows, count)), axis_in...  30 us
    all_to_all x1, blocking collectives, shards(): far_got = exchange(far, axis_index_groups=clips_first)  24.7 us
    all_to_all x1, waiting for transfers between devices, shards(): near_got = exchange(near, axis_index_groups=actions_first)  19.7 us
    ppermute x1, starting transfers between devices, shards(): got = lax.ppermute(gathered[:, 0].reshape(width, count), 'act', swap)  10.9 us
    ppermute x1, starting transfers between devices, shards(): other = lax.ppermute(jnp.where(first, action_half, clip_twice), 'act', swap)  8.79 us
    all_to_all x1, starting transfers between devices, shards(): near_got = exchange(near, axis_index_groups=actions_first)  4.52 us
    ppermute x1, starting transfers between devices, shards(): taken = lax.ppermute(give, 'act', swap)  3.9 us
    pallas_call x1, Pallas kernels, shards(): vmem_call(functools.partial(logits_kernel, 2.0 / math.sqrt(width), 256),...  3.49 us
  transfers between devices with their start and end apart: 4, of which 3 were waited for; matrix products, arithmetic and copies ran while one was open for 2% of the time, Pallas kernels for 1%

profile of v1, /device:TPU:1, one launch (start us, length us, event | category | flops | bytes accessed | tf_op | source)
XLA Modules:
  0.0 126.3 jit_solution(16964256685296890633)
XLA Ops:
  0.7 0.8 convert_element_type.40
  1.5 0.9 fusion.4
  2.4 8.8 %collective-permute-start = (bf16[64,512]{1,0:T(8,128)(2,1)S(1)}, bf16[64,512]{1,0:T(8,128)(2,1)S(1)}, u32[]{:S(2)}, u32[]{:S(2)}) collective-permute-start(bf16[64,512]{1,0:T(8,128)(2,1)S(1)} %fusion.4), channel_id=1, source_target_pairs={{0,1},{1,0},{2,3},{3,2},{4,5},{5,4},{6,7},{7,6},{8,9},{9,8},{10,11... | collective-permute-start | bytes 196616 | tf_op jit(solution)/shard_map/ppermute | solution.py:112
  11.2 0.9 convert_bitcast_fusion
  12.4 30.0 %all_to_all.15.own_ref = bf16[16,2,64,512]{3,2,1,0:T(8,128)(2,1)S(1)} all-to-all(bf16[16,2,64,512]{3,2,1,0:T(8,128)(2,1)S(1)} %broadcast_in_dim.35), channel_id=1, replica_groups={{0,2,4,6,8,10,12,14,16,18,20,22,24,26,28,30},{32,34,36,38,40,42,44,46,4..., dimensions={0} | all-to-all | bytes 4194304 | tf_op jit(solution)/shard_map/all_to_all | solution.py:115
  42.5 1.0 slice.61
  43.5 10.9 %collective-permute-start.1 = (bf16[1024,512]{1,0:T(8,128)(2,1)}, bf16[1024,512]{1,0:T(8,128)(2,1)S(1)}, u32[]{:S(2)}, u32[]{:S(2)}) collective-permute-start(bf16[1024,512]{1,0:T(8,128)(2,1)} %bitcast.2), channel_id=1, source_target_pairs={{0,1},{1,0},{2,3},{3,2},{4,5},{5,4},{6,7},{7,6},{8,9},{9,8},{10,11... | collective-permute-start | bytes 3145736 | tf_op jit(solution)/shard_map/ppermute | solution.py:116
  54.4 0.3 fusion
  54.9 0.9 copy.11.row_key_ref
  55.8 1.1 collective-permute-done.1.got_ref
  56.9 0.9 copy-done.3
  57.8 3.5 %shard_map.76 = (bf16[512,512]{1,0:T(8,128)(2,1)S(1)}, bf16[16,272,128]{2,1,0:T(8,128)(2,1)}, f32[1,1]{1,0:T(1,128)}) custom-call(s32[1]{0:T(128)} %bitcast.3.core_ref, bf16[16,2,64,512]{3,2,1,0:T(8,128)(2,1)S(1)} %all_to_all.15.own_ref, bf16[1024,512]{1,0:T(8,128)(2,1)S(1)} %collective-permute-done.1.got_ref, f32[512,1]{1,0:T(8,128)S(1)} %copy.10.row_bias_ref, ...), custom_call_target="tpu_custom_call" | custom-call | flops 1073741824 | bytes 4194304 | tf_op jit(solution)/shard_map/pallas_call | solution.py:129
  61.3 0.8 copy-done.1
  62.1 4.5 %all-to-all-start.1 = ((bf16[16,272,128]{2,1,0:T(8,128)(2,1)}), bf16[16,272,128]{2,1,0:T(8,128)(2,1)}, u32[]{:S(2)}, u32[]{:S(2)}) async-start(bf16[16,272,128]{2,1,0:T(8,128)(2,1)} %get-tuple-element.6), calls=%async_computation.1 | async-start | bytes 2228224 | tf_op jit(solution)/shard_map/all_to_all | solution.py:140
  66.7 0.7 shard_map.77
  67.4 19.7 %all-to-all-done.1 = bf16[16,272,128]{2,1,0:T(8,128)(2,1)} async-done(((bf16[16,272,128]{2,1,0:T(8,128)(2,1)}), bf16[16,272,128]{2,1,0:T(8,128)(2,1)}, u32[]{:S(2)}, u32[]{:S(2)}) %all-to-all-start.1) | async-done | bytes 1114144 | tf_op jit(solution)/shard_map/all_to_all | solution.py:140
  87.1 1.4 %convert_reduce_fusion.1 = f32[272,128]{1,0:T(8,128)S(1)} fusion(bf16[16,272,128]{2,1,0:T(8,128)(2,1)} %all-to-all-done.1), kind=kLoop, calls=%fused_computation.1 | loop fusion | flops 1079296 | bytes 1253376 | tf_op jit(solution)/shard_map/reduce_sum | solution.py:87
  88.5 0.5 fusion.10
  91.2 24.7 %all_to_all.16 = bf16[16,272,128]{2,1,0:T(8,128)(2,1)S(1)} all-to-all(bf16[16,272,128]{2,1,0:T(8,128)(2,1)S(1)} %pad_maximum_fusion), channel_id=1, replica_groups={{0,2,4,6,8,10,12,14,16,18,20,22,24,26,28,30},{32,34,36,38,40,42,44,46,4..., dimensions={0} | all-to-all | bytes 2228224 | tf_op jit(solution)/shard_map/all_to_all | solution.py:151
  116.1 0.5 fusion.9
  118.6 3.9 %collective-permute-start.2 = (f32[40,512]{1,0:T(8,128)S(1)}, f32[40,512]{1,0:T(8,128)S(1)}, u32[]{:S(2)}, u32[]{:S(2)}) collective-permute-start(f32[40,512]{1,0:T(8,128)S(1)} %concatenate.15), channel_id=1, source_target_pairs={{0,1},{1,0},{2,3},{3,2},{4,5},{5,4},{6,7},{7,6},{8,9},{9,8},{10,11... | collective-permute-start | bytes 245768 | tf_op jit(solution)/shard_map/ppermute | solution.py:160
  122.5 0.7 copy.21
  123.4 0.5 slice.73
  124.6 0.6 fusion.5
  (28 shorter events, 1.1 us)
Async XLA Ops:
  0.6 53.8 %copy-start = (f32[16]{0:T(128)S(1)}, f32[16]{0:T(128)}, u32[]{:S(2)}) copy-start(f32[16]{0:T(128)} %param.9) | copy-start | bytes 196
  2.4 9.7 %collective-permute-start = (bf16[64,512]{1,0:T(8,128)(2,1)S(1)}, bf16[64,512]{1,0:T(8,128)(2,1)S(1)}, u32[]{:S(2)}, u32[]{:S(2)}) collective-permute-start(bf16[64,512]{1,0:T(8,128)(2,1)S(1)} %fusion.4), channel_id=1, source_target_pairs={{0,1},{1,0},{2,3},{3,2},{4,5},{5,4},{6,7},{7,6},{8,9},{9,8},{10,11... | collective-permute-start | bytes 196616 | tf_op jit(solution)/shard_map/ppermute | solution.py:112
  42.5 11.9 %copy-start.5 = (s32[512]{0:T(512)S(1)}, s32[512]{0:T(512)}, u32[]{:S(2)}) copy-start(s32[512]{0:T(512)} %param.8) | copy-start | bytes 6148
  42.5 12.4 %copy-start.4 = (s32[512]{0:T(512)S(1)}, s32[512]{0:T(512)}, u32[]{:S(2)}) copy-start(s32[512]{0:T(512)} %param.7) | copy-start | bytes 6148
  43.5 13.4 %collective-permute-start.1 = (bf16[1024,512]{1,0:T(8,128)(2,1)}, bf16[1024,512]{1,0:T(8,128)(2,1)S(1)}, u32[]{:S(2)}, u32[]{:S(2)}) collective-permute-start(bf16[1024,512]{1,0:T(8,128)(2,1)} %bitcast.2), channel_id=1, source_target_pairs={{0,1},{1,0},{2,3},{3,2},{4,5},{5,4},{6,7},{7,6},{8,9},{9,8},{10,11... | collective-permute-start | bytes 3145736 | tf_op jit(solution)/shard_map/ppermute | solution.py:116
  56.9 0.9 copy-start.3
  61.3 0.8 copy-start.1
  62.1 4.5 %copy-start.2 = (bf16[512,512]{1,0:T(8,128)(2,1)S(1)}, bf16[512,512]{1,0:T(8,128)(2,1)}, u32[]{:S(2)}) copy-start(bf16[512,512]{1,0:T(8,128)(2,1)} %copy-done.1) | copy-start | bytes 1572868
  62.1 25.0 %all-to-all-start.1 = ((bf16[16,272,128]{2,1,0:T(8,128)(2,1)}), bf16[16,272,128]{2,1,0:T(8,128)(2,1)}, u32[]{:S(2)}, u32[]{:S(2)}) async-start(bf16[16,272,128]{2,1,0:T(8,128)(2,1)} %get-tuple-element.6), calls=%async_computation.1 | async-start | bytes 2228224 | tf_op jit(solution)/shard_map/all_to_all | solution.py:140
  118.6 4.8 %collective-permute-start.2 = (f32[40,512]{1,0:T(8,128)S(1)}, f32[40,512]{1,0:T(8,128)S(1)}, u32[]{:S(2)}, u32[]{:S(2)}) collective-permute-start(f32[40,512]{1,0:T(8,128)S(1)} %concatenate.15), channel_id=1, source_target_pairs={{0,1},{1,0},{2,3},{3,2},{4,5},{5,4},{6,7},{7,6},{8,9},{9,8},{10,11... | collective-permute-start | bytes 245768 | tf_op jit(solution)/shard_map/ppermute | solution.py:160

commit v2 on v1

v2 whole, which is shorter than its diff:
```python
import functools
import math

import jax
import jax.numpy as jnp
from jax import lax
from jax.experimental import pallas as pl
from jax.experimental.pallas import tpu as pltpu
from jax.sharding import PartitionSpec as P

BF16 = jnp.bfloat16
F32 = jnp.float32
LANES = 128
EXTRA = 16
VMEM = pl.BlockSpec(memory_space=pltpu.VMEM)
SMEM = pl.BlockSpec(memory_space=pltpu.SMEM)
ANY = pl.BlockSpec(memory_space=pl.ANY)


def loss_rows(value, shape):
    high = value.astype(BF16).astype(F32)
    middle = (value - high).astype(BF16).astype(F32)
    low = (value - high - middle).astype(BF16).astype(F32)
    row = lax.broadcasted_iota(jnp.int32, shape, len(shape) - 2)
    rows = jnp.where(row < 4, high, jnp.where(row < 8, middle, jnp.where(row < 12, low, 0.0)))
    return rows.astype(BF16)


def store_blocks(out_ref, values, first_column):
    blocks = out_ref.shape[0]
    rows = values.shape[0] // blocks
    for part in range(values.shape[1] // LANES):
        at = (first_column // LANES + part) * rows
        columns = values[:, part * LANES : (part + 1) * LANES]
        out_ref[:, at : at + rows, :] = columns.reshape(blocks, rows, LANES).astype(BF16)


def cast_kernel(core_ref, clips_ref, actions_ref, clip_ref, action_ref, send_ref):
    clip = clips_ref[...].astype(BF16)
    action = actions_ref[...].astype(BF16)
    clip_ref[...] = clip
    action_ref[...] = action

    @pl.when(core_ref[0] == 0)
    def _():
        send_ref[...] = action

    @pl.when(core_ref[0] != 0)
    def _():
        send_ref[: clip.shape[0], :] = clip
        send_ref[clip.shape[0] :, :] = clip


def chunk_kernel(core_ref, clip_ref, action_ref, other_ref, out_ref):
    half = clip_ref.shape[0]
    blocks = out_ref.shape[0]

    @pl.when(core_ref[0] == 0)
    def _():
        clip = clip_ref[...]
        other = other_ref[:half, :]
        action = action_ref[...]
        for block in range(blocks):
            out_ref[block, 0, :half, :] = clip
            out_ref[block, 0, half:, :] = other
            out_ref[block, 1] = action

    @pl.when(core_ref[0] != 0)
    def _():
        other = other_ref[...]
        action = action_ref[...]
        for block in range(blocks):
            out_ref[block, 0] = other
            out_ref[block, 1] = action


def side_kernel(core_ref, bias_ref, positive_ref, robot_ref, out_ref):
    count = positive_ref.shape[1]
    robot = robot_ref[...]
    bias = jnp.zeros((1, count), F32)
    for index in range(bias_ref.shape[0]):
        bias = jnp.where(robot == index, bias_ref[index], bias)
    zero = jnp.zeros((1, count), F32)
    positive = positive_ref[...].astype(F32)
    columns = (lax.broadcasted_iota(jnp.int32, (1, count), 1) + core_ref[1] * count).astype(F32)
    first = core_ref[0] == 0
    rows = [
        jnp.where(first, zero, bias),
        jnp.where(first, positive, columns),
        jnp.where(first, bias, zero),
        jnp.where(first, columns, positive),
        zero, zero, zero, zero,
    ]
    for index, row in enumerate(rows):
        out_ref[index : index + 1, :] = row


def logits_kernel(scale, step, core_ref, own_ref, got_ref, side_ref, weights_ref, grad_ref, weights, sent):
    core = core_ref[0]
    blocks, _, rows, count = own_ref.shape
    width = blocks * rows
    own = own_ref[:, core].reshape(width, count)
    own_t = own.T
    side_t = side_ref[...].T
    row_bias = side_t[:, 0:1]
    row_key = side_t[:, 1:2]
    total = jnp.zeros((1, 1), F32)
    copies = []
    for index, start in enumerate(range(0, got_ref.shape[1], step)):
        got = got_ref[:, start : start + step]
        logits = jnp.dot(own_t, got, preferred_element_type=F32) * scale
        logits = logits + (row_bias + side_ref[2:3, start : start + step])
        positive = row_key == side_ref[3:4, start : start + step]
        margin = jnp.where(positive, -logits, logits)
        small = jnp.exp(-jnp.abs(margin))
        loss = jnp.maximum(margin, 0.0) + jnp.log1p(small)
        sigmoid = jnp.where(margin >= 0.0, 1.0, small) / (1.0 + small)
        block = jnp.where(positive, -sigmoid, sigmoid).astype(BF16)
        weights[:, start : start + step] = block
        copies.append(
            pltpu.make_async_copy(
                weights.at[:, start : start + step], weights_ref.at[:, start : start + step], sent.at[index]
            )
        )
        copies[-1].start()
        total = total + jnp.sum(loss, keepdims=True)
        store_blocks(grad_ref, jnp.dot(own, block, preferred_element_type=F32), start)
    shape = (grad_ref.shape[0], EXTRA, LANES)
    grad_ref[:, grad_ref.shape[1] - EXTRA :, :] = loss_rows(jnp.broadcast_to(total.reshape(1, 1, 1), shape), shape)
    for copy in copies:
        copy.wait()


def second_kernel(step, got_ref, weights_ref, grad_ref):
    for start in range(0, weights_ref.shape[0], step):
        weights = weights_ref[start : start + step, :]
        grad = lax.dot_general(got_ref[...], weights, (((1,), (1,)), ((), ())), preferred_element_type=F32)
        store_blocks(grad_ref, grad, start)


def summed(received_ref, grad_rows):
    total = received_ref[0].astype(F32)
    for block in range(1, received_ref.shape[0]):
        total = total + received_ref[block].astype(F32)
    parts = [total[at : at + grad_rows] for at in range(0, total.shape[0] - EXTRA, grad_rows)]
    at = total.shape[0] - EXTRA
    loss = total[at : at + 1] + total[at + 4 : at + 5] + total[at + 8 : at + 9]
    return parts, loss


def near_kernel(received_ref, sum_ref, rows_ref):
    parts, loss = summed(received_ref, sum_ref.shape[0])
    for index, part in enumerate(parts):
        sum_ref[:, index * LANES : (index + 1) * LANES] = part
    rows = loss_rows(jnp.broadcast_to(loss, rows_ref.shape[1:]), rows_ref.shape[1:])
    for block in range(rows_ref.shape[0]):
        rows_ref[block] = rows


def far_kernel(clip_scale, action_scale, core_ref, received_ref, near_ref, action_ref, keep_ref, give_ref):
    half = keep_ref.shape[0]
    parts, loss = summed(received_ref, near_ref.shape[0])
    give_ref[half:, :] = jnp.concatenate([jnp.broadcast_to(loss, (8, LANES))] * len(parts), axis=1)

    @pl.when(core_ref[0] == 0)
    def _():
        action_ref[...] = near_ref[...] * action_scale
        for index, part in enumerate(parts):
            columns = slice(index * LANES, (index + 1) * LANES)
            keep_ref[:, columns] = part[:half] * clip_scale
            give_ref[:half, columns] = part[half:] * clip_scale

    @pl.when(core_ref[0] != 0)
    def _():
        keep_ref[...] = near_ref[half:, :] * clip_scale
        give_ref[:half, :] = near_ref[:half, :] * clip_scale
        for index, part in enumerate(parts):
            action_ref[:, index * LANES : (index + 1) * LANES] = part * action_scale


def last_kernel(loss_scale, keep_ref, give_ref, taken_ref, clip_ref, loss_ref):
    half = keep_ref.shape[0]
    clip_ref[...] = keep_ref[...] + taken_ref[:half, :]
    loss_ref[...] = (give_ref[half : half + 1, :1] + taken_ref[half : half + 1, :1]) * loss_scale


def call(kernel, out_shape, in_specs, out_specs=None, scratch=(), flops=0, moved=0):
    return pl.pallas_call(
        kernel,
        out_shape=out_shape,
        in_specs=in_specs,
        out_specs=jax.tree.map(lambda _: VMEM, out_shape) if out_specs is None else out_specs,
        scratch_shapes=scratch,
        compiler_params=pltpu.CompilerParams(vmem_limit_bytes=24 * 1024 * 1024),
        cost_estimate=pl.CostEstimate(flops=flops, bytes_accessed=moved, transcendentals=0),
    )


def shards(n_clip, n_act, clips, actions, positive_ids, robot_ids, robot_bias):
    both = ("clip", "act")
    pairs = n_act // 2
    along_act = [[[k * n_act + 2 * m + c for m in range(pairs)] for k in range(n_clip)] for c in range(2)]
    along_clip = [[[k * n_act + 2 * m + c for k in range(n_clip)] for m in range(pairs)] for c in range(2)]
    clips_first = along_act[0] + along_clip[1]
    actions_first = along_clip[0] + along_act[1]
    swap = [(i, i ^ 1) for i in range(n_act)]
    exchange = functools.partial(lax.all_to_all, axis_name=both, split_axis=0, concat_axis=0)

    half, count = clips.shape
    rows = actions.shape[0]
    width = rows * n_clip
    act = lax.axis_index("act")
    core = jnp.stack([act % 2, act]).astype(jnp.int32)
    shard = jax.ShapeDtypeStruct((rows, count), BF16)
    clip_half, action_half, send = call(
        cast_kernel, (jax.ShapeDtypeStruct((half, count), BF16), shard, shard), [SMEM, VMEM, VMEM]
    )(core, clips, actions)
    other = lax.ppermute(send, "act", swap)
    chunks = call(chunk_kernel, jax.ShapeDtypeStruct((n_clip, 2, rows, count), BF16), [SMEM] + [VMEM] * 3)(
        core, clip_half, action_half, other
    )
    gathered = exchange(chunks, axis_index_groups=clips_first)
    got = lax.ppermute(gathered[:, 0].reshape(width, count), "act", swap)
    side = call(side_kernel, jax.ShapeDtypeStruct((8, count), F32), [SMEM, SMEM, VMEM, VMEM])(
        core, robot_bias, positive_ids[None, :], robot_ids[None, :]
    )

    parts = count // LANES
    flops = 2 * width * count * count
    step = 256
    weights, near = call(
        functools.partial(logits_kernel, 2.0 / math.sqrt(width), step),
        (
            jax.ShapeDtypeStruct((count, count), BF16),
            jax.ShapeDtypeStruct((n_clip, parts * rows + EXTRA, LANES), BF16),
        ),
        [SMEM, VMEM, VMEM, VMEM],
        (ANY, VMEM),
        [pltpu.VMEM((count, count), BF16), pltpu.SemaphoreType.DMA((count // step,))],
        2 * flops,
        8 * width * count,
    )(core, gathered, got, side)
    near_got = exchange(near, axis_index_groups=actions_first)
    far = call(
        functools.partial(second_kernel, step),
        jax.ShapeDtypeStruct((n_clip, parts * rows, LANES), BF16),
        [VMEM, VMEM],
        flops=flops,
        moved=4 * width * count,
    )(got, weights)
    near_sum, far_rows = call(
        near_kernel,
        (jax.ShapeDtypeStruct((rows, count), F32), jax.ShapeDtypeStruct((n_clip, EXTRA, LANES), BF16)),
        [VMEM],
    )(near_got)
    far_got = exchange(jnp.concatenate([far, far_rows], axis=1), axis_index_groups=clips_first)

    total_clips = count * n_clip
    total_actions = count * n_act
    action_grad, keep, give = call(
        functools.partial(far_kernel, 1.0 / math.sqrt(total_actions), 1.0 / math.sqrt(total_clips)),
        (
            jax.ShapeDtypeStruct((rows, count), F32),
            jax.ShapeDtypeStruct((half, count), F32),
            jax.ShapeDtypeStruct((half + 8, count), F32),
        ),
        [SMEM, VMEM, VMEM],
    )(core, far_got, near_sum)
    taken = lax.ppermute(give, "act", swap)
    clip_grad, loss = call(
        functools.partial(last_kernel, 1.0 / (total_clips * total_actions)),
        (jax.ShapeDtypeStruct((half, count), F32), jax.ShapeDtypeStruct((1, 1), F32)),
        [VMEM] * 3,
    )(keep, give, taken)
    return clip_grad, action_grad, loss.reshape(())


def solution(mesh):
    return jax.shard_map(
        functools.partial(shards, mesh.shape["clip"], mesh.shape["act"]),
        mesh=mesh,
        in_specs=(P("act", "clip"), P("clip", "act"), P("clip"), P("act"), P()),
        out_specs=(P("act", "clip"), P("clip", "act"), P()),
        check_vma=False,
    )
```

time: 127 us -> 119 us (0.937)
  between operations: 6.55 us -> 0.78 us
  Pallas kernels: 4.23 us -> 9.26 us
  other arithmetic: 5.13 us -> 0.15 us
  local copies, waits for them, and re-layouts: 6.3 us -> 3.69 us
    pallas_call x2 -> x8, Pallas kernels: 4.23 us -> 9.26 us  [the longest x1 4.46 us: shards(): call(functools.partial(logits_kernel, 2.0 / math.sqrt(width), step), (jax...]
    unnamed x12 -> x14, local copies, waits for them, and re-layouts: 1.76 us -> 3.6 us
    slice x4 -> x0, local copies, waits for them, and re-layouts: 1.56 us -> none  [the longest x2 1.05 us: summed(): return (grad, total[at, 0] + total[at + 4, 0] + total[at + 8, 0])]
    reduce_sum x2 -> x0, other arithmetic: 1.56 us -> none  [summed(): total = jnp.sum(received.astype(F32), axis=0)]
    all_to_all x1, waiting for transfers between devices: 19.7 us -> 18.3 us  [shards(): near_got = exchange(near, axis_index_groups=actions_first)]
  transfers between devices with their start and end apart: 4 -> 4, of which waited for: 3 -> 4; matrix products, arithmetic and copies ran while one was open for 2% -> 0% of each run, Pallas kernels for 1% -> 1%
where the time goes in v2:
time: 119 us; the launch traced here: 118 us
  blocking collectives  55.4 us (47%)
  starting transfers between devices  27.3 us (23%)
  waiting for transfers between devices  21.7 us (18%)
  Pallas kernels  9.26 us (8%)
  local copies, waits for them, and re-layouts  3.69 us (3%)
    all_to_all x1, blocking collectives, shards(): gathered = exchange(chunks, axis_index_groups=clips_first)  30 us
    all_to_all x1, blocking collectives, shards(): exchange(jnp.concatenate([far, far_rows], axis=1), axis_index_groups=clip...  25.4 us
    all_to_all x1, waiting for transfers between devices, shards(): near_got = exchange(near, axis_index_groups=actions_first)  18.3 us
    ppermute x1, starting transfers between devices, shards(): got = lax.ppermute(gathered[:, 0].reshape(width, count), 'act', swap)  11 us
    ppermute x1, starting transfers between devices, shards(): other = lax.ppermute(send, 'act', swap)  8.79 us
    pallas_call x1, Pallas kernels, shards(): call(functools.partial(logits_kernel, 2.0 / math.sqrt(width), step), (jax...  4.46 us
    ppermute x1, starting transfers between devices, shards(): taken = lax.ppermute(give, 'act', swap)  3.89 us
    all_to_all x1, starting transfers between devices, shards(): near_got = exchange(near, axis_index_groups=actions_first)  3.7 us
  transfers between devices with their start and end apart: 4, of which 4 were waited for; matrix products, arithmetic and copies ran while one was open for 0% of the time, Pallas kernels for 1%

profile of v2, /device:TPU:1, one launch (start us, length us, event | category | flops | bytes accessed | tf_op | source)
XLA Modules:
  0.0 118.4 jit_solution(2668425507475761054)
XLA Ops:
  0.6 0.1 pad_add_fusion.core_ref
  0.7 0.9 copy-done.2
  1.6 0.8 copy-done.3
  2.5 0.6 shard_map.76
  3.0 8.8 %collective-permute-start = (bf16[64,512]{1,0:T(8,128)(2,1)S(1)}, bf16[64,512]{1,0:T(8,128)(2,1)S(1)}, u32[]{:S(2)}, u32[]{:S(2)}) collective-permute-start(bf16[64,512]{1,0:T(8,128)(2,1)S(1)} %get-tuple-element.17), channel_id=1, source_target_pairs={{0,1},{1,0},{2,3},{3,2},{4,5},{5,4},{6,7},{7,6},{8,9},{9,8},{10,11... | collective-permute-start | bytes 196616 | tf_op jit(solution)/shard_map/ppermute | solution.py:218
  11.8 0.9 collective-permute-done.other_ref
  12.7 0.7 shard_map.77
  13.5 30.0 %all_to_all.15.own_ref = bf16[16,2,64,512]{3,2,1,0:T(8,128)(2,1)S(1)} all-to-all(bf16[16,2,64,512]{3,2,1,0:T(8,128)(2,1)S(1)} %shard_map.77), channel_id=1, replica_groups={{0,2,4,6,8,10,12,14,16,18,20,22,24,26,28,30},{32,34,36,38,40,42,44,46,4..., dimensions={0} | all-to-all | bytes 4194304 | tf_op jit(solution)/shard_map/all_to_all | solution.py:222
  43.5 0.1 slice.4
  43.6 11.0 %collective-permute-start.1 = (bf16[1024,512]{1,0:T(8,128)(2,1)S(1)}, bf16[1024,512]{1,0:T(8,128)(2,1)S(1)}, u32[]{:S(2)}, u32[]{:S(2)}) collective-permute-start(bf16[1024,512]{1,0:T(8,128)(2,1)S(1)} %bitcast.8), channel_id=1, source_target_pairs={{0,1},{1,0},{2,3},{3,2},{4,5},{5,4},{6,7},{7,6},{8,9},{9,8},{10,11... | collective-permute-start | bytes 3145736 | tf_op jit(solution)/shard_map/ppermute | solution.py:223
  54.6 0.6 shard_map.78.side_ref
  55.1 1.7 %collective-permute-done.1.got_ref = bf16[1024,512]{1,0:T(8,128)(2,1)S(1)} collective-permute-done((bf16[1024,512]{1,0:T(8,128)(2,1)S(1)}, bf16[1024,512]{1,0:T(8,128)(2,1)S(1)}, u32[]{:S(2)}, u32[]{:S(2)}) %collective-permute-start.1) | collective-permute-done | bytes 1048608 | tf_op jit(solution)/shard_map/ppermute | solution.py:223
  56.8 4.5 %shard_map.79 = (bf16[512,512]{1,0:T(8,128)(2,1)S(1)}, bf16[16,272,128]{2,1,0:T(8,128)(2,1)}) custom-call(s32[2]{0:T(128)S(1)} %pad_add_fusion.core_ref, bf16[16,2,64,512]{3,2,1,0:T(8,128)(2,1)S(1)} %all_to_all.15.own_ref, bf16[1024,512]{1,0:T(8,128)(2,1)S(1)} %collective-permute-done.1.got_ref, f32[8,512]{1,0:T(8,128)S(1)} %shard_map.78.side_ref), custom_call_target="tpu_custom_call" | custom-call | flops 1073741824 | bytes 4194304 | tf_op jit(solution)/shard_map/pallas_call | solution.py:231
  61.3 0.8 copy-done
  62.1 3.7 %all-to-all-start.1 = ((bf16[16,272,128]{2,1,0:T(8,128)(2,1)}), bf16[16,272,128]{2,1,0:T(8,128)(2,1)S(1)}, u32[]{:S(2)}, u32[]{:S(2)}) async-start(bf16[16,272,128]{2,1,0:T(8,128)(2,1)} %get-tuple-element.19), calls=%async_computation.1 | async-start | bytes 2228224 | tf_op jit(solution)/shard_map/all_to_all | solution.py:243
  65.8 1.0 copy-done.1
  66.8 0.7 shard_map.80
  67.6 18.3 %all-to-all-done.1.received_ref = bf16[16,272,128]{2,1,0:T(8,128)(2,1)S(1)} async-done(((bf16[16,272,128]{2,1,0:T(8,128)(2,1)}), bf16[16,272,128]{2,1,0:T(8,128)(2,1)S(1)}, u32[]{:S(2)}, u32[]{:S(2)}) %all-to-all-start.1) | async-done | bytes 1114144 | tf_op jit(solution)/shard_map/all_to_all | solution.py:243
  85.9 0.2 shard_map.81
  86.1 25.4 %all_to_all.16.received_ref = bf16[16,272,128]{2,1,0:T(8,128)(2,1)S(1)} all-to-all(bf16[16,272,128]{2,1,0:T(8,128)(2,1)S(1)} %pad_maximum_fusion), channel_id=1, replica_groups={{0,2,4,6,8,10,12,14,16,18,20,22,24,26,28,30},{32,34,36,38,40,42,44,46,4..., dimensions={0} | all-to-all | bytes 2228224 | tf_op jit(solution)/shard_map/all_to_all | solution.py:256
  111.6 1.4 %shard_map.82 = (f32[64,512]{1,0:T(8,128)}, f32[32,512]{1,0:T(8,128)S(1)}, f32[40,512]{1,0:T(8,128)S(1)}) custom-call(s32[2]{0:T(128)S(1)} %pad_add_fusion.core_ref, bf16[16,272,128]{2,1,0:T(8,128)(2,1)S(1)} %all_to_all.16.received_ref, f32[64,512]{1,0:T(8,128)S(1)} %get-tuple-element.21.near_ref), custom_call_target="tpu_custom_call" | custom-call | tf_op jit(solution)/shard_map/pallas_call | solution.py:260
  113.0 3.9 %collective-permute-start.2 = (f32[40,512]{1,0:T(8,128)S(1)}, f32[40,512]{1,0:T(8,128)S(1)}, u32[]{:S(2)}, u32[]{:S(2)}) collective-permute-start(f32[40,512]{1,0:T(8,128)S(1)} %get-tuple-element.23.give_ref), channel_id=1, source_target_pairs={{0,1},{1,0},{2,3},{3,2},{4,5},{5,4},{6,7},{7,6},{8,9},{9,8},{10,11... | collective-permute-start | bytes 245768 | tf_op jit(solution)/shard_map/ppermute | solution.py:269
  116.9 0.9 collective-permute-done.2.taken_ref
  117.8 0.6 shard_map.83
  (11 shorter events, 0.1 us)
Async XLA Ops:
  0.7 0.9 copy-start.2
  1.6 0.8 copy-start.3
  3.0 9.7 %collective-permute-start = (bf16[64,512]{1,0:T(8,128)(2,1)S(1)}, bf16[64,512]{1,0:T(8,128)(2,1)S(1)}, u32[]{:S(2)}, u32[]{:S(2)}) collective-permute-start(bf16[64,512]{1,0:T(8,128)(2,1)S(1)} %get-tuple-element.17), channel_id=1, source_target_pairs={{0,1},{1,0},{2,3},{3,2},{4,5},{5,4},{6,7},{7,6},{8,9},{9,8},{10,11... | collective-permute-start | bytes 196616 | tf_op jit(solution)/shard_map/ppermute | solution.py:218
  43.5 11.1 %copy-start.4 = (s32[512]{0:T(512)S(1)}, s32[512]{0:T(512)}, u32[]{:S(2)}) copy-start(s32[512]{0:T(512)} %param.7) | copy-start | bytes 6148
  43.5 11.1 %copy-start.5 = (s32[512]{0:T(512)S(1)}, s32[512]{0:T(512)}, u32[]{:S(2)}) copy-start(s32[512]{0:T(512)} %param.8) | copy-start | bytes 6148
  43.5 11.1 %copy-start.6 = (f32[16]{0:T(128)S(1)}, f32[16]{0:T(128)}, u32[]{:S(2)}) copy-start(f32[16]{0:T(128)} %bias_ref.1) | copy-start | bytes 196
  43.6 13.2 %collective-permute-start.1 = (bf16[1024,512]{1,0:T(8,128)(2,1)S(1)}, bf16[1024,512]{1,0:T(8,128)(2,1)S(1)}, u32[]{:S(2)}, u32[]{:S(2)}) collective-permute-start(bf16[1024,512]{1,0:T(8,128)(2,1)S(1)} %bitcast.8), channel_id=1, source_target_pairs={{0,1},{1,0},{2,3},{3,2},{4,5},{5,4},{6,7},{7,6},{8,9},{9,8},{10,11... | collective-permute-start | bytes 3145736 | tf_op jit(solution)/shard_map/ppermute | solution.py:223
  61.3 0.8 copy-start
  62.1 23.8 %all-to-all-start.1 = ((bf16[16,272,128]{2,1,0:T(8,128)(2,1)}), bf16[16,272,128]{2,1,0:T(8,128)(2,1)S(1)}, u32[]{:S(2)}, u32[]{:S(2)}) async-start(bf16[16,272,128]{2,1,0:T(8,128)(2,1)} %get-tuple-element.19), calls=%async_computation.1 | async-start | bytes 2228224 | tf_op jit(solution)/shard_map/all_to_all | solution.py:243
  65.8 1.0 copy-start.1
  113.0 4.8 %collective-permute-start.2 = (f32[40,512]{1,0:T(8,128)S(1)}, f32[40,512]{1,0:T(8,128)S(1)}, u32[]{:S(2)}, u32[]{:S(2)}) collective-permute-start(f32[40,512]{1,0:T(8,128)S(1)} %get-tuple-element.23.give_ref), channel_id=1, source_target_pairs={{0,1},{1,0},{2,3},{3,2},{4,5},{5,4},{6,7},{7,6},{8,9},{9,8},{10,11... | collective-permute-start | bytes 245768 | tf_op jit(solution)/shard_map/ppermute | solution.py:269

commit v3 on v2

v3 whole, which is shorter than its diff:
```python
import functools
import math

import jax
import jax.numpy as jnp
from jax import lax
from jax.experimental import pallas as pl
from jax.experimental.pallas import tpu as pltpu
from jax.sharding import PartitionSpec as P

BF16 = jnp.bfloat16
F32 = jnp.float32
LANES = 128
EXTRA = 16
VMEM = pl.BlockSpec(memory_space=pltpu.VMEM)
SMEM = pl.BlockSpec(memory_space=pltpu.SMEM)
ANY = pl.BlockSpec(memory_space=pl.ANY)


def loss_rows(value, shape):
    high = value.astype(BF16).astype(F32)
    middle = (value - high).astype(BF16).astype(F32)
    low = (value - high - middle).astype(BF16).astype(F32)
    row = lax.broadcasted_iota(jnp.int32, shape, len(shape) - 2)
    rows = jnp.where(row < 4, high, jnp.where(row < 8, middle, jnp.where(row < 12, low, 0.0)))
    return rows.astype(BF16)


def store_blocks(out_ref, values, first_column):
    blocks = out_ref.shape[0]
    rows = values.shape[0] // blocks
    for part in range(values.shape[1] // LANES):
        at = (first_column // LANES + part) * rows
        columns = values[:, part * LANES : (part + 1) * LANES]
        out_ref[:, at : at + rows, :] = columns.reshape(blocks, rows, LANES).astype(BF16)


def cast_kernel(core_ref, clips_ref, actions_ref, clip_ref, action_ref, send_ref, clips, actions, arrived):
    half = clips.shape[0]
    copies = [
        pltpu.make_async_copy(clips_ref, clips, arrived.at[0]),
        pltpu.make_async_copy(actions_ref, actions, arrived.at[1]),
    ]
    for copy in copies:
        copy.start()
    for copy in copies:
        copy.wait()
    clip = clips[...].astype(BF16)
    action = actions[...].astype(BF16)
    clip_ref[...] = clip
    action_ref[...] = action

    @pl.when(core_ref[0] == 0)
    def _():
        send_ref[...] = action

    @pl.when(core_ref[0] != 0)
    def _():
        send_ref[:half, :] = clip
        send_ref[half:, :] = clip


def chunk_kernel(core_ref, clip_ref, action_ref, other_ref, side_ref, out_ref):
    del side_ref
    half = clip_ref.shape[0]
    blocks = out_ref.shape[0]

    @pl.when(core_ref[0] == 0)
    def _():
        clip = clip_ref[...]
        other = other_ref[:half, :]
        action = action_ref[...]
        for block in range(blocks):
            out_ref[block, 0, :half, :] = clip
            out_ref[block, 0, half:, :] = other
            out_ref[block, 1] = action

    @pl.when(core_ref[0] != 0)
    def _():
        other = other_ref[...]
        action = action_ref[...]
        for block in range(blocks):
            out_ref[block, 0] = other
            out_ref[block, 1] = action


def side_kernel(core_ref, bias_ref, positive_ref, robot_ref, out_ref):
    count = positive_ref.shape[1]
    robot = robot_ref[...]
    bias = jnp.zeros((1, count), F32)
    for index in range(bias_ref.shape[0]):
        bias = jnp.where(robot == index, bias_ref[index], bias)
    zero = jnp.zeros((1, count), F32)
    positive = positive_ref[...].astype(F32)
    columns = (lax.broadcasted_iota(jnp.int32, (1, count), 1) + core_ref[1] * count).astype(F32)
    first = core_ref[0] == 0
    rows = [
        jnp.where(first, zero, bias),
        jnp.where(first, positive, columns),
        jnp.where(first, bias, zero),
        jnp.where(first, columns, positive),
        zero, zero, zero, zero,
    ]
    for index, row in enumerate(rows):
        out_ref[index : index + 1, :] = row


def transpose_kernel(core_ref, own_ref, side_ref, own_t_ref, side_t_ref):
    blocks, _, rows, count = own_ref.shape
    own_t_ref[...] = own_ref[:, core_ref[0]].reshape(blocks * rows, count).T
    side_t_ref[...] = side_ref[...].T


def logits_kernel(scale, step, core_ref, own_ref, own_t_ref, got_ref, side_ref, side_t_ref, weights_ref, grad_ref, loss_ref):
    blocks, _, rows, count = own_ref.shape
    width = blocks * rows
    own = own_ref[:, core_ref[0]].reshape(width, count)
    own_t = own_t_ref[...]
    row_bias = side_t_ref[:, 0:1]
    row_key = side_t_ref[:, 1:2]
    total = jnp.zeros((1, 1), F32)
    for start in range(0, count, step):
        got = got_ref[:, start : start + step]
        logits = jnp.dot(own_t, got, preferred_element_type=F32) * scale
        logits = logits + (row_bias + side_ref[2:3, start : start + step])
        positive = row_key == side_ref[3:4, start : start + step]
        margin = jnp.where(positive, -logits, logits)
        small = jnp.exp(-jnp.abs(margin))
        above = 1.0 + small
        inverse = 1.0 / above
        log = jnp.log(above) + (small - (above - 1.0)) * inverse
        total = total + jnp.sum(jnp.maximum(margin, 0.0) + log, keepdims=True)
        sigmoid = jnp.where(margin >= 0.0, inverse, small * inverse)
        weights = jnp.where(positive, -sigmoid, sigmoid).astype(BF16)
        weights_ref[:, start : start + step] = weights
        store_blocks(grad_ref, jnp.dot(own, weights, preferred_element_type=F32), start)
    shape = (grad_ref.shape[0], EXTRA, LANES)
    grad_ref[:, grad_ref.shape[1] - EXTRA :, :] = loss_rows(jnp.broadcast_to(total.reshape(1, 1, 1), shape), shape)
    loss_ref[...] = jnp.broadcast_to(total, loss_ref.shape)


def second_kernel(step, got_ref, weights_ref, grad_ref):
    for start in range(0, weights_ref.shape[0], step):
        weights = weights_ref[start : start + step, :]
        grad = lax.dot_general(got_ref[...], weights, (((1,), (1,)), ((), ())), preferred_element_type=F32)
        store_blocks(grad_ref, grad, start)


def received_loss(rows):
    return rows[0:1] + rows[4:5] + rows[8:9]


def merge_kernel(core_ref, own_ref, got_ref, loss_ref, keep_ref, send_ref, rows_ref):
    blocks, size, _ = own_ref.shape
    loss = loss_ref[0:1, :] + received_loss(got_ref[0, size:, :].astype(F32))
    rows = loss_rows(jnp.broadcast_to(loss, rows_ref.shape[1:]), rows_ref.shape[1:])
    for block in range(blocks):
        rows_ref[block] = rows

    @pl.when(core_ref[0] == 0)
    def _():
        for block in range(blocks):
            keep_ref[block] = (own_ref[block].astype(F32) + got_ref[block, :size, :].astype(F32)).astype(BF16)

    @pl.when((core_ref[0] != 0) & (core_ref[2] == 0))
    def _():
        for block in range(blocks):
            keep_ref[block] = got_ref[block, :size, :]
            send_ref[block] = own_ref[block]

    @pl.when((core_ref[0] != 0) & (core_ref[2] != 0))
    def _():
        for block in range(blocks):
            keep_ref[block] = own_ref[block]
            send_ref[block] = got_ref[block, :size, :]


def add_kernel(core_ref, keep_ref, got_ref, loss_ref, out_ref):
    blocks, size, _ = keep_ref.shape
    total = loss_ref[0].astype(F32)
    for block in range(1, blocks):
        total = total + loss_ref[block].astype(F32)
    rows = loss_rows(jnp.broadcast_to(received_loss(total), total.shape), total.shape)
    for block in range(blocks):
        out_ref[block, size:, :] = rows

    @pl.when(core_ref[0] == 0)
    def _():
        for block in range(blocks):
            out_ref[block, :size, :] = keep_ref[block]

    @pl.when(core_ref[0] != 0)
    def _():
        for block in range(blocks):
            out_ref[block, :size, :] = (keep_ref[block].astype(F32) + got_ref[block].astype(F32)).astype(BF16)


def sum_kernel(clip_scale, action_scale, core_ref, got_ref, keep_ref, give_ref):
    blocks = got_ref.shape[0]
    rows, count = keep_ref.shape
    half = rows // 2

    def over(first, last):
        total = got_ref[first].astype(F32)
        for block in range(first + 1, last):
            total = total + got_ref[block].astype(F32)
        return total

    lower = over(0, blocks // 2)
    upper = over(blocks // 2, blocks)
    both = lower + upper
    loss = received_loss(both[both.shape[0] - EXTRA :])
    give_ref[rows:, :] = jnp.concatenate([jnp.broadcast_to(loss, (8, LANES))] * (count // LANES), axis=1)
    for part in range(count // LANES):
        columns = slice(part * LANES, (part + 1) * LANES)
        at = slice(part * rows, (part + 1) * rows)

        @pl.when(core_ref[0] == 0)
        def _():
            keep_ref[:half, columns] = both[at][:half] * clip_scale
            give_ref[:half, columns] = both[at][half:] * clip_scale

        @pl.when(core_ref[0] != 0)
        def _():
            keep_ref[:, columns] = upper[at] * action_scale
            give_ref[:rows, columns] = lower[at] * action_scale


def last_kernel(loss_scale, core_ref, keep_ref, give_ref, taken_ref, clip_ref, action_ref, loss_ref):
    rows = keep_ref.shape[0]
    half = clip_ref.shape[0]

    @pl.when(core_ref[0] == 0)
    def _():
        clip_ref[...] = keep_ref[:half, :]
        action_ref[...] = taken_ref[:rows, :]
        loss_ref[...] = give_ref[rows : rows + 1, :1] * loss_scale

    @pl.when(core_ref[0] != 0)
    def _():
        clip_ref[...] = taken_ref[:half, :]
        action_ref[...] = keep_ref[...]
        loss_ref[...] = taken_ref[rows : rows + 1, :1] * loss_scale


def call(kernel, out_shape, in_specs, scratch=(), flops=0, moved=0):
    return pl.pallas_call(
        kernel,
        out_shape=out_shape,
        in_specs=in_specs,
        out_specs=jax.tree.map(lambda _: VMEM, out_shape),
        scratch_shapes=scratch,
        compiler_params=pltpu.CompilerParams(vmem_limit_bytes=24 * 1024 * 1024),
        cost_estimate=pl.CostEstimate(flops=flops, bytes_accessed=moved, transcendentals=0),
    )


def shards(n_clip, n_act, clips, actions, positive_ids, robot_ids, robot_bias):
    both = ("clip", "act")
    pairs = n_act // 2
    near = n_clip // 2
    along_act = [[[k * n_act + 2 * m + c for m in range(pairs)] for k in range(n_clip)] for c in range(2)]
    along_clip = [[[k * n_act + 2 * m + c for k in range(n_clip)] for m in range(pairs)] for c in range(2)]
    clips_first = along_act[0] + along_clip[1]
    actions_first = along_clip[0] + along_act[1]
    swap = [(i, i ^ 1) for i in range(n_act)]
    neighbours = [
        (k * n_act + 2 * m + 1, (k + near) % n_clip * n_act + 2 * m + 1) for k in range(n_clip) for m in range(pairs)
    ]
    exchange = functools.partial(lax.all_to_all, axis_name=both, split_axis=0, concat_axis=0)

    half, count = clips.shape
    rows = actions.shape[0]
    width = rows * n_clip
    parts = count // LANES
    act = lax.axis_index("act")
    core = jnp.stack([act % 2, act, lax.axis_index("clip") // near]).astype(jnp.int32)
    shape = jax.ShapeDtypeStruct

    clip_half, action_half, send = call(
        cast_kernel,
        (shape((half, count), BF16), shape((rows, count), BF16), shape((rows, count), BF16)),
        [SMEM, ANY, ANY],
        [pltpu.VMEM((half, count), F32), pltpu.VMEM((rows, count), F32), pltpu.SemaphoreType.DMA((2,))],
    )(core, clips, actions)
    other = lax.ppermute(send, "act", swap)
    side = call(side_kernel, shape((8, count), F32), [SMEM, SMEM, VMEM, VMEM])(
        core, robot_bias, positive_ids[None, :], robot_ids[None, :]
    )
    chunks = call(chunk_kernel, shape((n_clip, 2, rows, count), BF16), [SMEM] + [VMEM] * 4)(
        core, clip_half, action_half, other, side
    )
    gathered = exchange(chunks, axis_index_groups=clips_first)
    got = lax.ppermute(gathered[:, 0].reshape(width, count), "act", swap)
    own_t, side_t = call(
        transpose_kernel, (shape((count, width), BF16), shape((count, 8), F32)), [SMEM, VMEM, VMEM]
    )(core, gathered, side)

    flops = 2 * width * count * count
    step = 256
    weights, first, loss = call(
        functools.partial(logits_kernel, 2.0 / math.sqrt(width), step),
        (
            shape((count, count), BF16),
            shape((n_clip, parts * rows + EXTRA, LANES), BF16),
            shape((8, LANES), F32),
        ),
        [SMEM] + [VMEM] * 5,
        flops=2 * flops,
        moved=8 * width * count,
    )(core, gathered, own_t, got, side, side_t)
    first_got = lax.ppermute(first, "act", swap)
    blocks = shape((n_clip, parts * rows, LANES), BF16)
    second = call(functools.partial(second_kernel, step), blocks, [VMEM, VMEM], flops=flops, moved=4 * width * count)(
        got, weights
    )
    keep, send, loss_sent = call(
        merge_kernel, (blocks, blocks, shape((n_clip, EXTRA, LANES), BF16)), [SMEM] + [VMEM] * 3
    )(core, second, first_got, loss)
    near_got = lax.ppermute(send, both, neighbours)
    loss_got = exchange(loss_sent, axis_index_groups=actions_first)
    ready = call(add_kernel, shape((n_clip, parts * rows + EXTRA, LANES), BF16), [SMEM] + [VMEM] * 3)(
        core, keep, near_got, loss_got
    )
    scattered = exchange(ready, axis_index_groups=clips_first)

    total_clips = count * n_clip
    total_actions = count * n_act
    keep, give = call(
        functools.partial(sum_kernel, 1.0 / math.sqrt(total_actions), 1.0 / math.sqrt(total_clips)),
        (shape((rows, count), F32), shape((rows + 8, count), F32)),
        [SMEM, VMEM],
    )(core, scattered)
    taken = lax.ppermute(give, "act", swap)
    clip_grad, action_grad, loss = call(
        functools.partial(last_kernel, 1.0 / (total_clips * total_actions)),
        (shape((half, count), F32), shape((rows, count), F32), shape((1, 1), F32)),
        [SMEM] + [VMEM] * 3,
    )(core, keep, give, taken)
    return clip_grad, action_grad, loss.reshape(())


def solution(mesh):
    return jax.shard_map(
        functools.partial(shards, mesh.shape["clip"], mesh.shape["act"]),
        mesh=mesh,
        in_specs=(P("act", "clip"), P("clip", "act"), P("clip"), P("act"), P()),
        out_specs=(P("act", "clip"), P("clip", "act"), P()),
        check_vma=False,
    )
```

time: 119 us -> 115 us (0.966)
  waiting for transfers between devices: 21.7 us -> 4.19 us
  blocking collectives: 55.4 us -> 69 us
    all_to_all x1 -> x0, waiting for transfers between devices: 18.3 us -> none  [shards(): near_got = exchange(near, axis_index_groups=actions_first)]
    all_to_all x1 -> x2, blocking collectives: 25.4 us -> 38.9 us  [the longest x1 25.1 us: shards(): scattered = exchange(ready, axis_index_groups=clips_first)]
    ppermute x0 -> x2, starting transfers between devices: none -> 4.5 us  [the longest x1 2.28 us: shards(): first_got = lax.ppermute(first, 'act', swap)]
    all_to_all x1 -> x0, starting transfers between devices: 3.7 us -> none  [shards(): near_got = exchange(near, axis_index_groups=actions_first)]
    ppermute x0 -> x2, waiting for transfers between devices: none -> 1.91 us  [the longest x1 1.61 us: shards(): first_got = lax.ppermute(first, 'act', swap)]
    ppermute x1, starting transfers between devices: 3.89 us -> 2.29 us  [shards(): taken = lax.ppermute(give, 'act', swap)]
    pallas_call x7 -> x9, Pallas kernels: 8.62 us -> 9.02 us  [the longest x1 2.88 us: shards(): call(functools.partial(logits_kernel, 2.0 / math.sqrt(width), step), (sha...]
    unnamed x14 -> x10, local copies, waits for them, and re-layouts: 3.6 us -> 3.76 us
  transfers between devices with their start and end apart: 4 -> 5, of which waited for: 4 -> 4; matrix products, arithmetic and copies ran while one was open for 0% -> 0% of each run, Pallas kernels for 1% -> 2%
where the time goes in v3:
time: 115 us; the launch traced here: 114 us
  blocking collectives  69 us (60%)
  starting transfers between devices  26.2 us (23%)
  Pallas kernels  10.3 us (9%)
  waiting for transfers between devices  4.19 us (4%)
  local copies, waits for them, and re-layouts  3.83 us (3%)
    all_to_all x1, blocking collectives, shards(): gathered = exchange(chunks, axis_index_groups=clips_first)  30 us
    all_to_all x1, blocking collectives, shards(): scattered = exchange(ready, axis_index_groups=clips_first)  25.1 us
    all_to_all x1, blocking collectives, shards(): loss_got = exchange(loss_sent, axis_index_groups=actions_first)  13.8 us
    ppermute x1, starting transfers between devices, shards(): got = lax.ppermute(gathered[:, 0].reshape(width, count), 'act', swap)  10.6 us
    ppermute x1, starting transfers between devices, shards(): other = lax.ppermute(send, 'act', swap)  8.79 us
    unnamed x10, local copies, waits for them, and re-layouts  3.76 us
    pallas_call x1, Pallas kernels, shards(): call(functools.partial(logits_kernel, 2.0 / math.sqrt(width), step), (sha...  2.88 us
  transfers between devices with their start and end apart: 5, of which 4 were waited for; matrix products, arithmetic and copies ran while one was open for 0% of the time, Pallas kernels for 2%

profile of v3, /device:TPU:1, one launch (start us, length us, event | category | flops | bytes accessed | tf_op | source)
XLA Modules:
  0.0 114.3 jit_solution(6443338953207400717)
XLA Ops:
  0.7 0.9 copy-done
  1.6 0.8 copy-done.1
  2.5 0.8 shard_map.76
  3.3 8.8 %collective-permute-start = (bf16[64,512]{1,0:T(8,128)(2,1)S(1)}, bf16[64,512]{1,0:T(8,128)(2,1)S(1)}, u32[]{:S(2)}, u32[]{:S(2)}) collective-permute-start(bf16[64,512]{1,0:T(8,128)(2,1)S(1)} %get-tuple-element.21), channel_id=1, source_target_pairs={{0,1},{1,0},{2,3},{3,2},{4,5},{5,4},{6,7},{7,6},{8,9},{9,8},{10,11... | collective-permute-start | bytes 196616 | tf_op jit(solution)/shard_map/ppermute | solution.py:286
  12.1 0.7 copy-done.2
  12.8 0.7 copy-done.3
  14.7 0.7 shard_map.78
  15.5 30.0 %all_to_all.15.own_ref = bf16[16,2,64,512]{3,2,1,0:T(8,128)(2,1)S(1)} all-to-all(bf16[16,2,64,512]{3,2,1,0:T(8,128)(2,1)S(1)} %shard_map.78), channel_id=1, replica_groups={{0,2,4,6,8,10,12,14,16,18,20,22,24,26,28,30},{32,34,36,38,40,42,44,46,4..., dimensions={0} | all-to-all | bytes 4194304 | tf_op jit(solution)/shard_map/all_to_all | solution.py:293
  45.5 10.6 %collective-permute-start.1 = (bf16[1024,512]{1,0:T(8,128)(2,1)S(1)}, bf16[1024,512]{1,0:T(8,128)(2,1)S(1)}, u32[]{:S(2)}, u32[]{:S(2)}) collective-permute-start(bf16[1024,512]{1,0:T(8,128)(2,1)S(1)} %bitcast.9), channel_id=1, source_target_pairs={{0,1},{1,0},{2,3},{3,2},{4,5},{5,4},{6,7},{7,6},{8,9},{9,8},{10,11... | collective-permute-start | bytes 3145736 | tf_op jit(solution)/shard_map/ppermute | solution.py:294
  56.2 1.0 shard_map.79
  57.1 1.3 %collective-permute-done.1.got_ref = bf16[1024,512]{1,0:T(8,128)(2,1)S(1)} collective-permute-done((bf16[1024,512]{1,0:T(8,128)(2,1)S(1)}, bf16[1024,512]{1,0:T(8,128)(2,1)S(1)}, u32[]{:S(2)}, u32[]{:S(2)}) %collective-permute-start.1) | collective-permute-done | bytes 1048608 | tf_op jit(solution)/shard_map/ppermute | solution.py:294
  58.4 2.9 %shard_map.80 = (bf16[512,512]{1,0:T(8,128)(2,1)S(1)}, bf16[16,272,128]{2,1,0:T(8,128)(2,1)S(1)}, f32[8,128]{1,0:T(8,128)S(1)}) custom-call(s32[3]{0:T(128)S(1)} %pad_add_fusion.core_ref, bf16[16,2,64,512]{3,2,1,0:T(8,128)(2,1)S(1)} %all_to_all.15.own_ref, bf16[512,1024]{1,0:T(8,128)(2,1)S(1)} %get-tuple-element.22.own_t_ref, ...), custom_call_target="tpu_custom_call" | custom-call | flops 1073741824 | bytes 4194304 | tf_op jit(solution)/shard_map/pallas_call | solution.py:301
  61.3 2.3 %collective-permute-start.2 = (bf16[16,272,128]{2,1,0:T(8,128)(2,1)S(1)}, bf16[16,272,128]{2,1,0:T(8,128)(2,1)S(1)}, u32[]{:S(2)}, u32[]{:S(2)}) collective-permute-start(bf16[16,272,128]{2,1,0:T(8,128)(2,1)S(1)} %get-tuple-element.25), channel_id=1, source_target_pairs={{0,1},{1,0},{2,3},{3,2},{4,5},{5,4},{6,7},{7,6},{8,9},{9,8},{10,11... | collective-permute-start | bytes 3342344 | tf_op jit(solution)/shard_map/ppermute | solution.py:312
  63.6 0.7 shard_map.81.own_ref
  64.4 1.6 %collective-permute-done.2.got_ref = bf16[16,272,128]{2,1,0:T(8,128)(2,1)S(1)} collective-permute-done((bf16[16,272,128]{2,1,0:T(8,128)(2,1)S(1)}, bf16[16,272,128]{2,1,0:T(8,128)(2,1)S(1)}, u32[]{:S(2)}, u32[]{:S(2)}) %collective-permute-start.2) | collective-permute-done | bytes 1114144 | tf_op jit(solution)/shard_map/ppermute | solution.py:312
  66.0 0.7 shard_map.82
  66.7 2.2 %collective-permute-start.3 = (bf16[16,256,128]{2,1,0:T(8,128)(2,1)S(1)}, bf16[16,256,128]{2,1,0:T(8,128)(2,1)S(1)}, u32[]{:S(2)}, u32[]{:S(2)}) collective-permute-start(bf16[16,256,128]{2,1,0:T(8,128)(2,1)S(1)} %get-tuple-element.28), channel_id=1, source_target_pairs={{1,257},{3,259},{5,261},{7,263},{9,265},{11,267},{13,269},{15,271}... | collective-permute-start | bytes 3145736 | tf_op jit(solution)/shard_map/ppermute | solution.py:320
  68.9 13.8 %all_to_all.16.loss_ref = bf16[16,16,128]{2,1,0:T(8,128)(2,1)S(1)} all-to-all(bf16[16,16,128]{2,1,0:T(8,128)(2,1)S(1)} %get-tuple-element.29), channel_id=1, replica_groups={{0,32,64,96,128,160,192,224,256,288,320,352,384,416,448,480},{2,34,66,9..., dimensions={0} | all-to-all | bytes 131072 | tf_op jit(solution)/shard_map/all_to_all | solution.py:321
  83.1 0.8 shard_map.83
  83.9 25.1 %all_to_all.17.got_ref = bf16[16,272,128]{2,1,0:T(8,128)(2,1)S(1)} all-to-all(bf16[16,272,128]{2,1,0:T(8,128)(2,1)S(1)} %shard_map.83), channel_id=1, replica_groups={{0,2,4,6,8,10,12,14,16,18,20,22,24,26,28,30},{32,34,36,38,40,42,44,46,4..., dimensions={0} | all-to-all | bytes 2228224 | tf_op jit(solution)/shard_map/all_to_all | solution.py:325
  109.0 0.8 shard_map.84
  109.8 2.3 %collective-permute-start.4 = (f32[72,512]{1,0:T(8,128)S(1)}, f32[72,512]{1,0:T(8,128)S(1)}, u32[]{:S(2)}, u32[]{:S(2)}) collective-permute-start(f32[72,512]{1,0:T(8,128)S(1)} %get-tuple-element.31.give_ref), channel_id=1, source_target_pairs={{0,1},{1,0},{2,3},{3,2},{4,5},{5,4},{6,7},{7,6},{8,9},{9,8},{10,11... | collective-permute-start | bytes 442376 | tf_op jit(solution)/shard_map/ppermute | solution.py:334
  112.1 1.0 collective-permute-done.4.taken_ref
  113.1 1.2 %shard_map.85 = (f32[32,512]{1,0:T(8,128)}, f32[64,512]{1,0:T(8,128)}, f32[1,1]{1,0:T(1,128)}) custom-call(s32[3]{0:T(128)S(1)} %pad_add_fusion.core_ref, f32[64,512]{1,0:T(8,128)S(1)} %get-tuple-element.30.keep_ref, f32[72,512]{1,0:T(8,128)S(1)} %get-tuple-element.31.give_ref, f32[72,512]{1,0:T(8,128)S(1)} %collective-permute-done.4.taken_ref), custom_call_target="tpu_custom_call" | custom-call | tf_op jit(solution)/shard_map/pallas_call | solution.py:335
  (11 shorter events, 1.7 us)
Async XLA Ops:
  0.7 0.9 copy-start
  1.6 0.8 copy-start.1
  3.3 11.4 %collective-permute-start = (bf16[64,512]{1,0:T(8,128)(2,1)S(1)}, bf16[64,512]{1,0:T(8,128)(2,1)S(1)}, u32[]{:S(2)}, u32[]{:S(2)}) collective-permute-start(bf16[64,512]{1,0:T(8,128)(2,1)S(1)} %get-tuple-element.21), channel_id=1, source_target_pairs={{0,1},{1,0},{2,3},{3,2},{4,5},{5,4},{6,7},{7,6},{8,9},{9,8},{10,11... | collective-permute-start | bytes 196616 | tf_op jit(solution)/shard_map/ppermute | solution.py:286
  12.1 0.7 copy-start.2
  12.8 0.7 copy-start.3
  13.5 0.7 copy-start.4
  45.5 12.9 %collective-permute-start.1 = (bf16[1024,512]{1,0:T(8,128)(2,1)S(1)}, bf16[1024,512]{1,0:T(8,128)(2,1)S(1)}, u32[]{:S(2)}, u32[]{:S(2)}) collective-permute-start(bf16[1024,512]{1,0:T(8,128)(2,1)S(1)} %bitcast.9), channel_id=1, source_target_pairs={{0,1},{1,0},{2,3},{3,2},{4,5},{5,4},{6,7},{7,6},{8,9},{9,8},{10,11... | collective-permute-start | bytes 3145736 | tf_op jit(solution)/shard_map/ppermute | solution.py:294
  61.3 4.6 %collective-permute-start.2 = (bf16[16,272,128]{2,1,0:T(8,128)(2,1)S(1)}, bf16[16,272,128]{2,1,0:T(8,128)(2,1)S(1)}, u32[]{:S(2)}, u32[]{:S(2)}) collective-permute-start(bf16[16,272,128]{2,1,0:T(8,128)(2,1)S(1)} %get-tuple-element.25), channel_id=1, source_target_pairs={{0,1},{1,0},{2,3},{3,2},{4,5},{5,4},{6,7},{7,6},{8,9},{9,8},{10,11... | collective-permute-start | bytes 3342344 | tf_op jit(solution)/shard_map/ppermute | solution.py:312
  66.7 16.4 %collective-permute-start.3 = (bf16[16,256,128]{2,1,0:T(8,128)(2,1)S(1)}, bf16[16,256,128]{2,1,0:T(8,128)(2,1)S(1)}, u32[]{:S(2)}, u32[]{:S(2)}) collective-permute-start(bf16[16,256,128]{2,1,0:T(8,128)(2,1)S(1)} %get-tuple-element.28), channel_id=1, source_target_pairs={{1,257},{3,259},{5,261},{7,263},{9,265},{11,267},{13,269},{15,271}... | collective-permute-start | bytes 3145736 | tf_op jit(solution)/shard_map/ppermute | solution.py:320
  109.8 3.3 %collective-permute-start.4 = (f32[72,512]{1,0:T(8,128)S(1)}, f32[72,512]{1,0:T(8,128)S(1)}, u32[]{:S(2)}, u32[]{:S(2)}) collective-permute-start(f32[72,512]{1,0:T(8,128)S(1)} %get-tuple-element.31.give_ref), channel_id=1, source_target_pairs={{0,1},{1,0},{2,3},{3,2},{4,5},{5,4},{6,7},{7,6},{8,9},{9,8},{10,11... | collective-permute-start | bytes 442376 | tf_op jit(solution)/shard_map/ppermute | solution.py:334

commit v4 on v3

--- a/solution.py
+++ b/solution.py
@@ -14,7 +14,6 @@
 EXTRA = 16
 VMEM = pl.BlockSpec(memory_space=pltpu.VMEM)
 SMEM = pl.BlockSpec(memory_space=pltpu.SMEM)
-ANY = pl.BlockSpec(memory_space=pl.ANY)
 
 
 def loss_rows(value, shape):
@@ -35,61 +34,12 @@
         out_ref[:, at : at + rows, :] = columns.reshape(blocks, rows, LANES).astype(BF16)
 
 
-def cast_kernel(core_ref, clips_ref, actions_ref, clip_ref, action_ref, send_ref, clips, actions, arrived):
-    half = clips.shape[0]
-    copies = [
-        pltpu.make_async_copy(clips_ref, clips, arrived.at[0]),
-        pltpu.make_async_copy(actions_ref, actions, arrived.at[1]),
-    ]
-    for copy in copies:
-        copy.start()
-    for copy in copies:
-        copy.wait()
-    clip = clips[...].astype(BF16)
-    action = actions[...].astype(BF16)
-    clip_ref[...] = clip
-    action_ref[...] = action
-
-    @pl.when(core_ref[0] == 0)
-    def _():
-        send_ref[...] = action
-
-    @pl.when(core_ref[0] != 0)
-    def _():
-        send_ref[:half, :] = clip
-        send_ref[half:, :] = clip
-
-
-def chunk_kernel(core_ref, clip_ref, action_ref, other_ref, side_ref, out_ref):
-    del side_ref
-    half = clip_ref.shape[0]
-    blocks = out_ref.shape[0]
-
-    @pl.when(core_ref[0] == 0)
-    def _():
-        clip = clip_ref[...]
-        other = other_ref[:half, :]
-        action = action_ref[...]
-        for block in range(blocks):
-            out_ref[block, 0, :half, :] = clip
-            out_ref[block, 0, half:, :] = other
-            out_ref[block, 1] = action
-
-    @pl.when(core_ref[0] != 0)
-    def _():
-        other = other_ref[...]
-        action = action_ref[...]
-        for block in range(blocks):
-            out_ref[block, 0] = other
-            out_ref[block, 1] = action
-
-
-def side_kernel(core_ref, bias_ref, positive_ref, robot_ref, out_ref):
+def side_kernel(core_ref, bias_ref, positive_ref, robot_ref, out_ref, out_t_ref):
     count = positive_ref.shape[1]
     robot = robot_ref[...]
     bias = jnp.zeros((1, count), F32)
-    for index in range(bias_ref.shape[0]):
-        bias = jnp.where(robot == index, bias_ref[index], bias)
+    for index in range(bias_ref.shape[1]):
+        bias = jnp.where(robot == index, bias_ref[:, index : index + 1], bias)
     zero = jnp.zeros((1, count), F32)
     positive = positive_ref[...].astype(F32)
     columns = (lax.broadcasted_iota(jnp.int32, (1, count), 1) + core_ref[1] * count).astype(F32)
@@ -101,14 +51,14 @@
         jnp.where(first, columns, positive),
         zero, zero, zero, zero,
     ]
-    for index, row in enumerate(rows):
-        out_ref[index : index + 1, :] = row
-
-
-def transpose_kernel(core_ref, own_ref, side_ref, own_t_ref, side_t_ref):
+    side = jnp.concatenate(rows, axis=0)
+    out_ref[...] = side
+    out_t_ref[...] = side.T
+
+
+def transpose_kernel(core_ref, own_ref, own_t_ref):
     blocks, _, rows, count = own_ref.shape
     own_t_ref[...] = own_ref[:, core_ref[0]].reshape(blocks * rows, count).T
-    side_t_ref[...] = side_ref[...].T
 
 
 def logits_kernel(scale, step, core_ref, own_ref, own_t_ref, got_ref, side_ref, side_t_ref, weights_ref, grad_ref, loss_ref):
@@ -139,60 +89,62 @@
     loss_ref[...] = jnp.broadcast_to(total, loss_ref.shape)
 
 
-def second_kernel(step, got_ref, weights_ref, grad_ref):
+def second_kernel(step, core_ref, got_ref, weights_ref, first_ref, grad_ref, send_ref):
+    size = grad_ref.shape[1]
     for start in range(0, weights_ref.shape[0], step):
         weights = weights_ref[start : start + step, :]
         grad = lax.dot_general(got_ref[...], weights, (((1,), (1,)), ((), ())), preferred_element_type=F32)
         store_blocks(grad_ref, grad, start)
 
+    @pl.when(core_ref[0] == 0)
+    def _():
+        for block in range(grad_ref.shape[0]):
+            send_ref[block] = first_ref[block, :size, :]
+
+    @pl.when(core_ref[0] != 0)
+    def _():
+        for block in range(grad_ref.shape[0]):
+            send_ref[block] = grad_ref[block]
+
 
 def received_loss(rows):
     return rows[0:1] + rows[4:5] + rows[8:9]
 
 
-def merge_kernel(core_ref, own_ref, got_ref, loss_ref, keep_ref, send_ref, rows_ref):
+def loss_kernel(loss_ref, got_ref, rows_ref):
+    loss = loss_ref[0:1, :] + received_loss(got_ref[0, got_ref.shape[1] - EXTRA :, :].astype(F32))
+    rows = loss_rows(jnp.broadcast_to(loss, rows_ref.shape[1:]), rows_ref.shape[1:])
+    for block in range(rows_ref.shape[0]):
+        rows_ref[block] = rows
+
+
+def add_kernel(core_ref, own_ref, other_ref, near_ref, loss_ref, out_ref):
     blocks, size, _ = own_ref.shape
-    loss = loss_ref[0:1, :] + received_loss(got_ref[0, size:, :].astype(F32))
-    rows = loss_rows(jnp.broadcast_to(loss, rows_ref.shape[1:]), rows_ref.shape[1:])
-    for block in range(blocks):
-        rows_ref[block] = rows
-
-    @pl.when(core_ref[0] == 0)
-    def _():
-        for block in range(blocks):
-            keep_ref[block] = (own_ref[block].astype(F32) + got_ref[block, :size, :].astype(F32)).astype(BF16)
-
-    @pl.when((core_ref[0] != 0) & (core_ref[2] == 0))
-    def _():
-        for block in range(blocks):
-            keep_ref[block] = got_ref[block, :size, :]
-            send_ref[block] = own_ref[block]
-
-    @pl.when((core_ref[0] != 0) & (core_ref[2] != 0))
-    def _():
-        for block in range(blocks):
-            keep_ref[block] = own_ref[block]
-            send_ref[block] = got_ref[block, :size, :]
-
-
-def add_kernel(core_ref, keep_ref, got_ref, loss_ref, out_ref):
-    blocks, size, _ = keep_ref.shape
     total = loss_ref[0].astype(F32)
     for block in range(1, blocks):
         total = total + loss_ref[block].astype(F32)
     rows = loss_rows(jnp.broadcast_to(received_loss(total), total.shape), total.shape)
     for block in range(blocks):
         out_ref[block, size:, :] = rows
-
-    @pl.when(core_ref[0] == 0)
+    core, side = core_ref[0], core_ref[2]
+
+    @pl.when(core == 0)
     def _():
         for block in range(blocks):
-            out_ref[block, :size, :] = keep_ref[block]
-
-    @pl.when(core_ref[0] != 0)
+            added = own_ref[block].astype(F32) + other_ref[block, :size, :].astype(F32)
+            out_ref[block, :size, :] = added.astype(BF16)
+
+    @pl.when((core != 0) & (side == 0))
     def _():
         for block in range(blocks):
-            out_ref[block, :size, :] = (keep_ref[block].astype(F32) + got_ref[block].astype(F32)).astype(BF16)
+            added = other_ref[block, :size, :].astype(F32) + near_ref[block].astype(F32)
+            out_ref[block, :size, :] = added.astype(BF16)
+
+    @pl.when((core != 0) & (side != 0))
+    def _():
+        for block in range(blocks):
+            added = own_ref[block].astype(F32) + near_ref[block].astype(F32)
+            out_ref[block, :size, :] = added.astype(BF16)
 
 
 def sum_kernel(clip_scale, action_scale, core_ref, got_ref, keep_ref, give_ref):
@@ -264,9 +216,11 @@
     clips_first = along_act[0] + along_clip[1]
     actions_first = along_clip[0] + along_act[1]
     swap = [(i, i ^ 1) for i in range(n_act)]
-    neighbours = [
-        (k * n_act + 2 * m + 1, (k + near) % n_clip * n_act + 2 * m + 1) for k in range(n_clip) for m in range(pairs)
-    ]
+    neighbours = []
+    for k in range(near):
+        for m in range(pairs):
+            low, high = k * n_act + 2 * m, (k + near) * n_act + 2 * m
+            neighbours += [(high, low + 1), (low + 1, high + 1)]
     exchange = functools.partial(lax.all_to_all, axis_name=both, split_axis=0, concat_axis=0)
 
     half, count = clips.shape
@@ -277,24 +231,23 @@
     core = jnp.stack([act % 2, act, lax.axis_index("clip") // near]).astype(jnp.int32)
     shape = jax.ShapeDtypeStruct
 
-    clip_half, action_half, send = call(
-        cast_kernel,
-        (shape((half, count), BF16), shape((rows, count), BF16), shape((rows, count), BF16)),
-        [SMEM, ANY, ANY],
-        [pltpu.VMEM((half, count), F32), pltpu.VMEM((rows, count), F32), pltpu.SemaphoreType.DMA((2,))],
-    )(core, clips, actions)
+    first_core = act % 2 == 0
+    clip_twice = jnp.broadcast_to(clips[None], (2, half, count)).reshape(rows, count)
+    send = jnp.where(first_core, actions, clip_twice).astype(BF16)
+    mine = jnp.where(first_core, clip_twice, actions).astype(BF16)
     other = lax.ppermute(send, "act", swap)
-    side = call(side_kernel, shape((8, count), F32), [SMEM, SMEM, VMEM, VMEM])(
-        core, robot_bias, positive_ids[None, :], robot_ids[None, :]
-    )
-    chunks = call(chunk_kernel, shape((n_clip, 2, rows, count), BF16), [SMEM] + [VMEM] * 4)(
-        core, clip_half, action_half, other, side
+    clip_pair = jnp.concatenate([mine[:half], other[:half]], axis=0)
+    chunk = jnp.stack([jnp.where(first_core, clip_pair, other), mine])
+    chunks = jnp.broadcast_to(chunk[None], (n_clip, 2, rows, count))
+    chunks, positive_ids, robot_ids, robot_bias = lax.optimization_barrier(
+        (chunks, positive_ids, robot_ids, robot_bias)
     )
     gathered = exchange(chunks, axis_index_groups=clips_first)
+    side, side_t = call(side_kernel, (shape((8, count), F32), shape((count, 8), F32)), [SMEM] + [VMEM] * 3)(
+        core, robot_bias[None, :], positive_ids[None, :], robot_ids[None, :]
+    )
     got = lax.ppermute(gathered[:, 0].reshape(width, count), "act", swap)
-    own_t, side_t = call(
-        transpose_kernel, (shape((count, width), BF16), shape((count, 8), F32)), [SMEM, VMEM, VMEM]
-    )(core, gathered, side)
+    own_t = call(transpose_kernel, shape((count, width), BF16), [SMEM, VMEM])(core, gathered)
 
     flops = 2 * width * count * count
     step = 256
@@ -311,16 +264,18 @@
     )(core, gathered, own_t, got, side, side_t)
     first_got = lax.ppermute(first, "act", swap)
     blocks = shape((n_clip, parts * rows, LANES), BF16)
-    second = call(functools.partial(second_kernel, step), blocks, [VMEM, VMEM], flops=flops, moved=4 * width * count)(
-        got, weights
-    )
-    keep, send, loss_sent = call(
-        merge_kernel, (blocks, blocks, shape((n_clip, EXTRA, LANES), BF16)), [SMEM] + [VMEM] * 3
-    )(core, second, first_got, loss)
+    second, send = call(
+        functools.partial(second_kernel, step),
+        (blocks, blocks),
+        [SMEM] + [VMEM] * 3,
+        flops=flops,
+        moved=8 * width * count,
+    )(core, got, weights, first)
     near_got = lax.ppermute(send, both, neighbours)
+    loss_sent = call(loss_kernel, shape((n_clip, EXTRA, LANES), BF16), [VMEM, VMEM])(loss, first_got)
     loss_got = exchange(loss_sent, axis_index_groups=actions_first)
-    ready = call(add_kernel, shape((n_clip, parts * rows + EXTRA, LANES), BF16), [SMEM] + [VMEM] * 3)(
-        core, keep, near_got, loss_got
+    ready = call(add_kernel, shape((n_clip, parts * rows + EXTRA, LANES), BF16), [SMEM] + [VMEM] * 4)(
+        core, second, first_got, near_got, loss_got
     )
     scattered = exchange(ready, axis_index_groups=clips_first)
 

time: 115 us -> 115 us (level)
  blocking collectives: 69 us -> 55.3 us
  waiting for transfers between devices: 4.19 us -> 12.8 us
  starting transfers between devices: 26.2 us -> 32.4 us
  local copies, waits for them, and re-layouts: 3.83 us -> 2.33 us
    all_to_all x1 -> x0, blocking collectives: 13.8 us -> none  [shards(): loss_got = exchange(loss_sent, axis_index_groups=actions_first)]
    ppermute x1, waiting for transfers between devices: 0.29 us -> 10.3 us  [shards(): near_got = lax.ppermute(send, both, neighbours)]
    all_to_all x0 -> x1, starting transfers between devices: none -> 3.93 us  [shards(): loss_got = exchange(loss_sent, axis_index_groups=actions_first)]
    unnamed x10, local copies, waits for them, and re-layouts: 3.76 us -> 1.01 us
    ppermute x1, starting transfers between devices: 2.29 us -> 4.07 us  [shards(): taken = lax.ppermute(give, 'act', swap)]
    ppermute x1, waiting for transfers between devices: 1.61 us -> 0.01 us  [shards(): first_got = lax.ppermute(first, 'act', swap)]
    pallas_call x6 -> x4, Pallas kernels: 4.55 us -> 4.66 us  [the longest x1 2.34 us: shards(): call(functools.partial(second_kernel, step), (blocks, blocks), [SMEM] + [...]
  transfers between devices with their start and end apart: 5 -> 6, of which waited for: 4 -> 4; matrix products, arithmetic and copies ran while one was open for 0% -> 0% of each run, Pallas kernels for 2% -> 4%
where the time goes in v4:
time: 115 us
  blocking collectives  55.3 us (48%)
  starting transfers between devices  32.4 us (28%)
  waiting for transfers between devices  12.8 us (11%)
  Pallas kernels  10.4 us (9%)
  local copies, waits for them, and re-layouts  2.33 us (2%)
    all_to_all x1, blocking collectives, shards(): gathered = exchange(chunks, axis_index_groups=clips_first)  30 us
    all_to_all x1, blocking collectives, shards(): scattered = exchange(ready, axis_index_groups=clips_first)  25.2 us
    ppermute x1, starting transfers between devices, shards(): got = lax.ppermute(gathered[:, 0].reshape(width, count), 'act', swap)  10.9 us
    ppermute x1, waiting for transfers between devices, shards(): near_got = lax.ppermute(send, both, neighbours)  10.3 us
    ppermute x1, starting transfers between devices, shards(): other = lax.ppermute(send, 'act', swap)  8.79 us
    ppermute x1, starting transfers between devices, shards(): taken = lax.ppermute(give, 'act', swap)  4.07 us
    all_to_all x1, starting transfers between devices, shards(): loss_got = exchange(loss_sent, axis_index_groups=actions_first)  3.93 us
    pallas_call x1, Pallas kernels, shards(): call(functools.partial(logits_kernel, 2.0 / math.sqrt(width), step), (sha...  2.87 us
  transfers between devices with their start and end apart: 6, of which 4 were waited for; matrix products, arithmetic and copies ran while one was open for 0% of the time, Pallas kernels for 4%

profile of v4, /device:TPU:1, one launch (start us, length us, event | category | flops | bytes accessed | tf_op | source)
XLA Modules:
  0.0 115.0 jit_solution(7089820078800976493)
XLA Ops:
  0.6 0.9 fusion.1
  1.6 8.8 %collective-permute-start = (bf16[64,512]{1,0:T(8,128)(2,1)S(1)}, bf16[64,512]{1,0:T(8,128)(2,1)S(1)}, u32[]{:S(2)}, u32[]{:S(2)}) collective-permute-start(bf16[64,512]{1,0:T(8,128)(2,1)S(1)} %get-tuple-element.35), channel_id=1, source_target_pairs={{0,1},{1,0},{2,3},{3,2},{4,5},{5,4},{6,7},{7,6},{8,9},{9,8},{10,11... | collective-permute-start | bytes 196616 | tf_op jit(solution)/shard_map/ppermute | solution.py:238
  10.4 0.9 collective-permute-done
  11.3 0.2 broadcast_in_dim.22
  11.5 30.0 %all_to_all.15.own_ref = bf16[16,2,64,512]{3,2,1,0:T(8,128)(2,1)S(1)} all-to-all(bf16[16,2,64,512]{3,2,1,0:T(8,128)(2,1)S(1)} %broadcast_in_dim.22), channel_id=1, replica_groups={{0,2,4,6,8,10,12,14,16,18,20,22,24,26,28,30},{32,34,36,38,40,42,44,46,4..., dimensions={0} | all-to-all | bytes 4194304 | tf_op jit(solution)/shard_map/all_to_all | solution.py:245
  41.5 1.1 slice.14
  42.6 10.9 %collective-permute-start.1 = (bf16[1024,512]{1,0:T(8,128)(2,1)}, bf16[1024,512]{1,0:T(8,128)(2,1)S(1)}, u32[]{:S(2)}, u32[]{:S(2)}) collective-permute-start(bf16[1024,512]{1,0:T(8,128)(2,1)} %bitcast.6), channel_id=1, source_target_pairs={{0,1},{1,0},{2,3},{3,2},{4,5},{5,4},{6,7},{7,6},{8,9},{9,8},{10,11... | collective-permute-start | bytes 3145736 | tf_op jit(solution)/shard_map/ppermute | solution.py:249
  53.7 0.8 shard_map.77
  54.5 0.9 shard_map.76.own_t_ref
  55.4 0.7 collective-permute-done.1.got_ref
  56.1 2.9 %shard_map.78 = (bf16[512,512]{1,0:T(8,128)(2,1)S(1)}, bf16[16,272,128]{2,1,0:T(8,128)(2,1)S(1)}, f32[8,128]{1,0:T(8,128)S(1)}) custom-call(s32[3]{0:T(128)S(1)} %pad_add_fusion.core_ref, bf16[16,2,64,512]{3,2,1,0:T(8,128)(2,1)S(1)} %all_to_all.15.own_ref, bf16[512,1024]{1,0:T(8,128)(2,1)S(1)} %shard_map.76.own_t_ref, ...), custom_call_target="tpu_custom_call" | custom-call | flops 1073741824 | bytes 4194304 | tf_op jit(solution)/shard_map/pallas_call | solution.py:254
  58.9 2.3 %collective-permute-start.2 = (bf16[16,272,128]{2,1,0:T(8,128)(2,1)S(1)}, bf16[16,272,128]{2,1,0:T(8,128)(2,1)S(1)}, u32[]{:S(2)}, u32[]{:S(2)}) collective-permute-start(bf16[16,272,128]{2,1,0:T(8,128)(2,1)S(1)} %get-tuple-element.26.first_ref), channel_id=1, source_target_pairs={{0,1},{1,0},{2,3},{3,2},{4,5},{5,4},{6,7},{7,6},{8,9},{9,8},{10,11... | collective-permute-start | bytes 3342344 | tf_op jit(solution)/shard_map/ppermute | solution.py:265
  61.2 2.3 %shard_map.79 = (bf16[16,256,128]{2,1,0:T(8,128)(2,1)S(1)}, bf16[16,256,128]{2,1,0:T(8,128)(2,1)}) custom-call(s32[3]{0:T(128)S(1)} %pad_add_fusion.core_ref, bf16[1024,512]{1,0:T(8,128)(2,1)S(1)} %collective-permute-done.1.got_ref, bf16[512,512]{1,0:T(8,128)(2,1)S(1)} %get-tuple-element.25.weights_ref, bf16[16,272,128]{2,1,0:T(8,128)(2,1)S(1)} %get-tuple-element.26.first_ref), custom_call_target="tpu_custom_call" | custom-call | flops 536870912 | bytes 4194304 | tf_op jit(solution)/shard_map/pallas_call | solution.py:267
  63.6 1.0 copy-done
  64.6 2.3 %collective-permute-start.3 = (bf16[16,256,128]{2,1,0:T(8,128)(2,1)}, bf16[16,256,128]{2,1,0:T(8,128)(2,1)S(1)}, u32[]{:S(2)}, u32[]{:S(2)}) collective-permute-start(bf16[16,256,128]{2,1,0:T(8,128)(2,1)} %get-tuple-element.28), channel_id=1, source_target_pairs={{256,1},{1,257},{258,3},{3,259},{260,5},{5,261},{262,7},{7,263},{2... | collective-permute-start | bytes 3145736 | tf_op jit(solution)/shard_map/ppermute | solution.py:274
  66.9 0.6 shard_map.80
  67.6 3.9 %all-to-all-start.1 = ((bf16[16,16,128]{2,1,0:T(8,128)(2,1)}), bf16[16,16,128]{2,1,0:T(8,128)(2,1)S(1)}, u32[]{:S(2)}, u32[]{:S(2)}) async-start(bf16[16,16,128]{2,1,0:T(8,128)(2,1)} %shard_map.80), calls=%async_computation.1 | async-start | bytes 131072 | tf_op jit(solution)/shard_map/all_to_all | solution.py:276
  71.5 10.3 %collective-permute-done.3.near_ref = bf16[16,256,128]{2,1,0:T(8,128)(2,1)S(1)} collective-permute-done((bf16[16,256,128]{2,1,0:T(8,128)(2,1)}, bf16[16,256,128]{2,1,0:T(8,128)(2,1)S(1)}, u32[]{:S(2)}, u32[]{:S(2)}) %collective-permute-start.3) | collective-permute-done | bytes 1048608 | tf_op jit(solution)/shard_map/ppermute | solution.py:274
  81.8 0.8 shard_map.81
  82.6 25.2 %all_to_all.16.got_ref = bf16[16,272,128]{2,1,0:T(8,128)(2,1)S(1)} all-to-all(bf16[16,272,128]{2,1,0:T(8,128)(2,1)S(1)} %shard_map.81), channel_id=1, replica_groups={{0,2,4,6,8,10,12,14,16,18,20,22,24,26,28,30},{32,34,36,38,40,42,44,46,4..., dimensions={0} | all-to-all | bytes 2228224 | tf_op jit(solution)/shard_map/all_to_all | solution.py:280
  107.9 0.8 shard_map.82
  108.7 4.1 %collective-permute-start.4 = (f32[72,512]{1,0:T(8,128)S(1)}, f32[72,512]{1,0:T(8,128)S(1)}, u32[]{:S(2)}, u32[]{:S(2)}) collective-permute-start(f32[72,512]{1,0:T(8,128)S(1)} %get-tuple-element.31.give_ref), channel_id=1, source_target_pairs={{0,1},{1,0},{2,3},{3,2},{4,5},{5,4},{6,7},{7,6},{8,9},{9,8},{10,11... | collective-permute-start | bytes 442376 | tf_op jit(solution)/shard_map/ppermute | solution.py:289
  112.7 1.0 collective-permute-done.4.taken_ref
  113.7 1.2 %shard_map.83 = (f32[32,512]{1,0:T(8,128)}, f32[64,512]{1,0:T(8,128)}, f32[1,1]{1,0:T(1,128)}) custom-call(s32[3]{0:T(128)S(1)} %pad_add_fusion.core_ref, f32[64,512]{1,0:T(8,128)S(1)} %get-tuple-element.30.keep_ref, f32[72,512]{1,0:T(8,128)S(1)} %get-tuple-element.31.give_ref, f32[72,512]{1,0:T(8,128)S(1)} %collective-permute-done.4.taken_ref), custom_call_target="tpu_custom_call" | custom-call | tf_op jit(solution)/shard_map/pallas_call | solution.py:290
  (16 shorter events, 0.1 us)
Async XLA Ops:
  1.6 9.7 %collective-permute-start = (bf16[64,512]{1,0:T(8,128)(2,1)S(1)}, bf16[64,512]{1,0:T(8,128)(2,1)S(1)}, u32[]{:S(2)}, u32[]{:S(2)}) collective-permute-start(bf16[64,512]{1,0:T(8,128)(2,1)S(1)} %get-tuple-element.35), channel_id=1, source_target_pairs={{0,1},{1,0},{2,3},{3,2},{4,5},{5,4},{6,7},{7,6},{8,9},{9,8},{10,11... | collective-permute-start | bytes 196616 | tf_op jit(solution)/shard_map/ppermute | solution.py:238
  41.5 12.1 %copy-start.2 = (s32[512]{0:T(512)S(1)}, s32[512]{0:T(512)}, u32[]{:S(2)}) copy-start(s32[512]{0:T(512)} %param.7) | copy-start | bytes 6148
  41.5 12.1 %copy-start.3 = (s32[512]{0:T(512)S(1)}, s32[512]{0:T(512)}, u32[]{:S(2)}) copy-start(s32[512]{0:T(512)} %param.8) | copy-start | bytes 6148
  41.5 12.1 %copy-start.4 = (f32[16]{0:T(128)S(1)}, f32[16]{0:T(128)}, u32[]{:S(2)}) copy-start(f32[16]{0:T(128)} %param.9) | copy-start | bytes 196
  42.6 13.4 %collective-permute-start.1 = (bf16[1024,512]{1,0:T(8,128)(2,1)}, bf16[1024,512]{1,0:T(8,128)(2,1)S(1)}, u32[]{:S(2)}, u32[]{:S(2)}) collective-permute-start(bf16[1024,512]{1,0:T(8,128)(2,1)} %bitcast.6), channel_id=1, source_target_pairs={{0,1},{1,0},{2,3},{3,2},{4,5},{5,4},{6,7},{7,6},{8,9},{9,8},{10,11... | collective-permute-start | bytes 3145736 | tf_op jit(solution)/shard_map/ppermute | solution.py:249
  58.9 8.0 %collective-permute-start.2 = (bf16[16,272,128]{2,1,0:T(8,128)(2,1)S(1)}, bf16[16,272,128]{2,1,0:T(8,128)(2,1)S(1)}, u32[]{:S(2)}, u32[]{:S(2)}) collective-permute-start(bf16[16,272,128]{2,1,0:T(8,128)(2,1)S(1)} %get-tuple-element.26.first_ref), channel_id=1, source_target_pairs={{0,1},{1,0},{2,3},{3,2},{4,5},{5,4},{6,7},{7,6},{8,9},{9,8},{10,11... | collective-permute-start | bytes 3342344 | tf_op jit(solution)/shard_map/ppermute | solution.py:265
  63.6 1.0 copy-start
  64.6 17.2 %copy-start.1 = (bf16[16,256,128]{2,1,0:T(8,128)(2,1)S(1)}, bf16[16,256,128]{2,1,0:T(8,128)(2,1)}, u32[]{:S(2)}) copy-start(bf16[16,256,128]{2,1,0:T(8,128)(2,1)} %copy-done) | copy-start | bytes 3145732
  64.6 17.2 %collective-permute-start.3 = (bf16[16,256,128]{2,1,0:T(8,128)(2,1)}, bf16[16,256,128]{2,1,0:T(8,128)(2,1)S(1)}, u32[]{:S(2)}, u32[]{:S(2)}) collective-permute-start(bf16[16,256,128]{2,1,0:T(8,128)(2,1)} %get-tuple-element.28), channel_id=1, source_target_pairs={{256,1},{1,257},{258,3},{3,259},{260,5},{5,261},{262,7},{7,263},{2... | collective-permute-start | bytes 3145736 | tf_op jit(solution)/shard_map/ppermute | solution.py:274
  67.6 14.2 %all-to-all-start.1 = ((bf16[16,16,128]{2,1,0:T(8,128)(2,1)}), bf16[16,16,128]{2,1,0:T(8,128)(2,1)S(1)}, u32[]{:S(2)}, u32[]{:S(2)}) async-start(bf16[16,16,128]{2,1,0:T(8,128)(2,1)} %shard_map.80), calls=%async_computation.1 | async-start | bytes 131072 | tf_op jit(solution)/shard_map/all_to_all | solution.py:276
  108.7 5.1 %collective-permute-start.4 = (f32[72,512]{1,0:T(8,128)S(1)}, f32[72,512]{1,0:T(8,128)S(1)}, u32[]{:S(2)}, u32[]{:S(2)}) collective-permute-start(f32[72,512]{1,0:T(8,128)S(1)} %get-tuple-element.31.give_ref), channel_id=1, source_target_pairs={{0,1},{1,0},{2,3},{3,2},{4,5},{5,4},{6,7},{7,6},{8,9},{9,8},{10,11... | collective-permute-start | bytes 442376 | tf_op jit(solution)/shard_map/ppermute | solution.py:289

commit v5 on v4

--- a/solution.py
+++ b/solution.py
@@ -34,14 +34,34 @@
         out_ref[:, at : at + rows, :] = columns.reshape(blocks, rows, LANES).astype(BF16)
 
 
-def side_kernel(core_ref, bias_ref, positive_ref, robot_ref, out_ref, out_t_ref):
-    count = positive_ref.shape[1]
-    robot = robot_ref[...]
+def chunk_kernel(core_ref, mine_ref, other_ref, out_ref):
+    half = mine_ref.shape[0] // 2
+    mine = mine_ref[...]
+    other = other_ref[...]
+    pair = jnp.concatenate([mine[:half], other[:half]], axis=0)
+
+    @pl.when(core_ref[0] == 0)
+    def _():
+        for block in range(out_ref.shape[0]):
+            out_ref[block, 0] = pair
+            out_ref[block, 1] = pair
+
+    @pl.when(core_ref[0] != 0)
+    def _():
+        for block in range(out_ref.shape[0]):
+            out_ref[block, 0] = other
+            out_ref[block, 1] = mine
+
+
+def side_kernel(robots, core_ref, own_ref, table_ref, own_t_ref, out_ref, out_t_ref):
+    blocks, _, size, _ = own_ref.shape
+    count = table_ref.shape[1]
+    robot = table_ref[1:2, :]
     bias = jnp.zeros((1, count), F32)
-    for index in range(bias_ref.shape[1]):
-        bias = jnp.where(robot == index, bias_ref[:, index : index + 1], bias)
+    for index in range(robots):
+        bias = jnp.where(robot == index, table_ref[2:3, index : index + 1], bias)
     zero = jnp.zeros((1, count), F32)
-    positive = positive_ref[...].astype(F32)
+    positive = table_ref[0:1, :]
     columns = (lax.broadcasted_iota(jnp.int32, (1, count), 1) + core_ref[1] * count).astype(F32)
     first = core_ref[0] == 0
     rows = [
@@ -54,11 +74,7 @@
     side = jnp.concatenate(rows, axis=0)
     out_ref[...] = side
     out_t_ref[...] = side.T
-
-
-def transpose_kernel(core_ref, own_ref, own_t_ref):
-    blocks, _, rows, count = own_ref.shape
-    own_t_ref[...] = own_ref[:, core_ref[0]].reshape(blocks * rows, count).T
+    own_t_ref[...] = own_ref[:, core_ref[0]].reshape(blocks * size, count).T
 
 
 def logits_kernel(scale, step, core_ref, own_ref, own_t_ref, got_ref, side_ref, side_t_ref, weights_ref, grad_ref, loss_ref):
@@ -84,13 +100,12 @@
         weights = jnp.where(positive, -sigmoid, sigmoid).astype(BF16)
         weights_ref[:, start : start + step] = weights
         store_blocks(grad_ref, jnp.dot(own, weights, preferred_element_type=F32), start)
-    shape = (grad_ref.shape[0], EXTRA, LANES)
-    grad_ref[:, grad_ref.shape[1] - EXTRA :, :] = loss_rows(jnp.broadcast_to(total.reshape(1, 1, 1), shape), shape)
     loss_ref[...] = jnp.broadcast_to(total, loss_ref.shape)
 
 
-def second_kernel(step, core_ref, got_ref, weights_ref, first_ref, grad_ref, send_ref):
+def second_kernel(step, core_ref, got_ref, weights_ref, first_ref, loss_ref, grad_ref, send_ref, rows_ref):
     size = grad_ref.shape[1]
+    rows_ref[...] = loss_rows(jnp.broadcast_to(loss_ref[0:1, :], rows_ref.shape), rows_ref.shape)
     for start in range(0, weights_ref.shape[0], step):
         weights = weights_ref[start : start + step, :]
         grad = lax.dot_general(got_ref[...], weights, (((1,), (1,)), ((), ())), preferred_element_type=F32)
@@ -99,7 +114,7 @@
     @pl.when(core_ref[0] == 0)
     def _():
         for block in range(grad_ref.shape[0]):
-            send_ref[block] = first_ref[block, :size, :]
+            send_ref[block] = first_ref[block]
 
     @pl.when(core_ref[0] != 0)
     def _():
@@ -109,13 +124,6 @@
 
 def received_loss(rows):
     return rows[0:1] + rows[4:5] + rows[8:9]
-
-
-def loss_kernel(loss_ref, got_ref, rows_ref):
-    loss = loss_ref[0:1, :] + received_loss(got_ref[0, got_ref.shape[1] - EXTRA :, :].astype(F32))
-    rows = loss_rows(jnp.broadcast_to(loss, rows_ref.shape[1:]), rows_ref.shape[1:])
-    for block in range(rows_ref.shape[0]):
-        rows_ref[block] = rows
 
 
 def add_kernel(core_ref, own_ref, other_ref, near_ref, loss_ref, out_ref):
@@ -131,13 +139,13 @@
     @pl.when(core == 0)
     def _():
         for block in range(blocks):
-            added = own_ref[block].astype(F32) + other_ref[block, :size, :].astype(F32)
+            added = own_ref[block].astype(F32) + other_ref[block].astype(F32)
             out_ref[block, :size, :] = added.astype(BF16)
 
     @pl.when((core != 0) & (side == 0))
     def _():
         for block in range(blocks):
-            added = other_ref[block, :size, :].astype(F32) + near_ref[block].astype(F32)
+            added = other_ref[block].astype(F32) + near_ref[block].astype(F32)
             out_ref[block, :size, :] = added.astype(BF16)
 
     @pl.when((core != 0) & (side != 0))
@@ -181,18 +189,17 @@
 def last_kernel(loss_scale, core_ref, keep_ref, give_ref, taken_ref, clip_ref, action_ref, loss_ref):
     rows = keep_ref.shape[0]
     half = clip_ref.shape[0]
+    loss_ref[...] = (give_ref[rows : rows + 1, :1] + taken_ref[rows : rows + 1, :1]) * loss_scale
 
     @pl.when(core_ref[0] == 0)
     def _():
         clip_ref[...] = keep_ref[:half, :]
         action_ref[...] = taken_ref[:rows, :]
-        loss_ref[...] = give_ref[rows : rows + 1, :1] * loss_scale
 
     @pl.when(core_ref[0] != 0)
     def _():
         clip_ref[...] = taken_ref[:half, :]
         action_ref[...] = keep_ref[...]
-        loss_ref[...] = taken_ref[rows : rows + 1, :1] * loss_scale
 
 
 def call(kernel, out_shape, in_specs, scratch=(), flops=0, moved=0):
@@ -202,7 +209,7 @@
         in_specs=in_specs,
         out_specs=jax.tree.map(lambda _: VMEM, out_shape),
         scratch_shapes=scratch,
-        compiler_params=pltpu.CompilerParams(vmem_limit_bytes=24 * 1024 * 1024),
+        compiler_params=pltpu.CompilerParams(vmem_limit_bytes=12 * 1024 * 1024),
         cost_estimate=pl.CostEstimate(flops=flops, bytes_accessed=moved, transcendentals=0),
     )
 
@@ -236,43 +243,38 @@
     send = jnp.where(first_core, actions, clip_twice).astype(BF16)
     mine = jnp.where(first_core, clip_twice, actions).astype(BF16)
     other = lax.ppermute(send, "act", swap)
-    clip_pair = jnp.concatenate([mine[:half], other[:half]], axis=0)
-    chunk = jnp.stack([jnp.where(first_core, clip_pair, other), mine])
-    chunks = jnp.broadcast_to(chunk[None], (n_clip, 2, rows, count))
-    chunks, positive_ids, robot_ids, robot_bias = lax.optimization_barrier(
-        (chunks, positive_ids, robot_ids, robot_bias)
-    )
+    chunks = call(chunk_kernel, shape((n_clip, 2, rows, count), BF16), [SMEM, VMEM, VMEM])(core, mine, other)
+    robots = robot_bias.shape[0]
+    table = jnp.stack([positive_ids.astype(F32), robot_ids.astype(F32), jnp.pad(robot_bias, (0, count - robots))])
+    chunks, table = lax.optimization_barrier((chunks, table))
     gathered = exchange(chunks, axis_index_groups=clips_first)
-    side, side_t = call(side_kernel, (shape((8, count), F32), shape((count, 8), F32)), [SMEM] + [VMEM] * 3)(
-        core, robot_bias[None, :], positive_ids[None, :], robot_ids[None, :]
-    )
     got = lax.ppermute(gathered[:, 0].reshape(width, count), "act", swap)
-    own_t = call(transpose_kernel, shape((count, width), BF16), [SMEM, VMEM])(core, gathered)
+    own_t, side, side_t = call(
+        functools.partial(side_kernel, robots),
+        (shape((count, width), BF16), shape((8, count), F32), shape((count, 8), F32)),
+        [SMEM, VMEM, VMEM],
+    )(core, gathered, table)
 
     flops = 2 * width * count * count
     step = 256
+    blocks = shape((n_clip, parts * rows, LANES), BF16)
+    loss_blocks = shape((n_clip, EXTRA, LANES), BF16)
     weights, first, loss = call(
         functools.partial(logits_kernel, 2.0 / math.sqrt(width), step),
-        (
-            shape((count, count), BF16),
-            shape((n_clip, parts * rows + EXTRA, LANES), BF16),
-            shape((8, LANES), F32),
-        ),
+        (shape((count, count), BF16), blocks, shape((8, LANES), F32)),
         [SMEM] + [VMEM] * 5,
         flops=2 * flops,
         moved=8 * width * count,
     )(core, gathered, own_t, got, side, side_t)
     first_got = lax.ppermute(first, "act", swap)
-    blocks = shape((n_clip, parts * rows, LANES), BF16)
-    second, send = call(
+    second, send, loss_sent = call(
         functools.partial(second_kernel, step),
-        (blocks, blocks),
-        [SMEM] + [VMEM] * 3,
+        (blocks, blocks, loss_blocks),
+        [SMEM] + [VMEM] * 4,
         flops=flops,
         moved=8 * width * count,
-    )(core, got, weights, first)
+    )(core, got, weights, first, loss)
     near_got = lax.ppermute(send, both, neighbours)
-    loss_sent = call(loss_kernel, shape((n_clip, EXTRA, LANES), BF16), [VMEM, VMEM])(loss, first_got)
     loss_got = exchange(loss_sent, axis_index_groups=actions_first)
     ready = call(add_kernel, shape((n_clip, parts * rows + EXTRA, LANES), BF16), [SMEM] + [VMEM] * 4)(
         core, second, first_got, near_got, loss_got

time: 115 us -> 112 us (0.974)
  blocking collectives: 55.3 us -> 68.7 us
  waiting for transfers between devices: 12.8 us -> 2.18 us
  starting transfers between devices: 32.4 us -> 28.2 us
  local copies, waits for them, and re-layouts: 2.33 us -> 0.75 us
  Pallas kernels: 10.4 us -> 8.83 us
  other arithmetic: 1.04 us -> 2.39 us
    all_to_all x0 -> x1, blocking collectives: none -> 13.3 us  [shards(): loss_got = exchange(loss_sent, axis_index_groups=actions_first)]
    ppermute x1, waiting for transfers between devices: 10.3 us -> 0.01 us  [shards(): near_got = lax.ppermute(send, both, neighbours)]
    all_to_all x1 -> x0, starting transfers between devices: 3.93 us -> none  [shards(): loss_got = exchange(loss_sent, axis_index_groups=actions_first)]
    pallas_call x4 -> x3, Pallas kernels: 4.66 us -> 3.11 us  [the longest x1 1.35 us: shards(): call(functools.partial(second_kernel, step), (blocks, blocks, loss_blocks...]
    convert_element_type x0 -> x2, other arithmetic: none -> 1.37 us  [the longest x1 0.69 us: shards(): positive_ids.astype(F32)]
  transfers between devices with their start and end apart: 6 -> 5, of which waited for: 4 -> 2; matrix products, arithmetic and copies ran while one was open for 0% -> 2% of each run, Pallas kernels for 4% -> 1%
where the time goes in v5:
time: 112 us
  blocking collectives  68.7 us (61%)
  starting transfers between devices  28.2 us (25%)
  Pallas kernels  8.83 us (8%)
  other arithmetic  2.39 us (2%)
  waiting for transfers between devices  2.18 us (2%)
    all_to_all x1, blocking collectives, shards(): gathered = exchange(chunks, axis_index_groups=clips_first)  30 us
    all_to_all x1, blocking collectives, shards(): scattered = exchange(ready, axis_index_groups=clips_first)  25.4 us
    all_to_all x1, blocking collectives, shards(): loss_got = exchange(loss_sent, axis_index_groups=actions_first)  13.3 us
    ppermute x1, starting transfers between devices, shards(): got = lax.ppermute(gathered[:, 0].reshape(width, count), 'act', swap)  10.6 us
    ppermute x1, starting transfers between devices, shards(): other = lax.ppermute(send, 'act', swap)  8.79 us
    ppermute x1, starting transfers between devices, shards(): taken = lax.ppermute(give, 'act', swap)  4.61 us
    pallas_call x1, Pallas kernels, shards(): call(functools.partial(logits_kernel, 2.0 / math.sqrt(width), step), (sha...  2.88 us
  transfers between devices with their start and end apart: 5, of which 2 were waited for; matrix products, arithmetic and copies ran while one was open for 2% of the time, Pallas kernels for 1%

profile of v5, /device:TPU:1, one launch (start us, length us, event | category | flops | bytes accessed | tf_op | source)
XLA Modules:
  0.0 111.8 jit_solution(11005615776721286696)
XLA Ops:
  0.6 0.9 fusion.1
  1.6 8.8 %collective-permute-start = (bf16[64,512]{1,0:T(8,128)(2,1)S(1)}, bf16[64,512]{1,0:T(8,128)(2,1)S(1)}, u32[]{:S(2)}, u32[]{:S(2)}) collective-permute-start(bf16[64,512]{1,0:T(8,128)(2,1)S(1)} %get-tuple-element.35), channel_id=1, source_target_pairs={{0,1},{1,0},{2,3},{3,2},{4,5},{5,4},{6,7},{7,6},{8,9},{9,8},{10,11... | collective-permute-start | bytes 196616 | tf_op jit(solution)/shard_map/ppermute | solution.py:245
  10.4 0.7 convert_element_type.16
  11.1 0.7 convert_element_type.17
  11.8 0.7 pad.4
  12.4 0.1 pad_add_fusion.core_ref
  12.5 0.7 shard_map.76
  13.2 30.0 %all_to_all.15.own_ref = bf16[16,2,64,512]{3,2,1,0:T(8,128)(2,1)S(1)} all-to-all(bf16[16,2,64,512]{3,2,1,0:T(8,128)(2,1)S(1)} %shard_map.76), channel_id=1, replica_groups={{0,2,4,6,8,10,12,14,16,18,20,22,24,26,28,30},{32,34,36,38,40,42,44,46,4..., dimensions={0} | all-to-all | bytes 4194304 | tf_op jit(solution)/shard_map/all_to_all | solution.py:250
  43.2 0.1 slice.4
  43.3 10.6 %collective-permute-start.1 = (bf16[1024,512]{1,0:T(8,128)(2,1)S(1)}, bf16[1024,512]{1,0:T(8,128)(2,1)S(1)}, u32[]{:S(2)}, u32[]{:S(2)}) collective-permute-start(bf16[1024,512]{1,0:T(8,128)(2,1)S(1)} %bitcast.15), channel_id=1, source_target_pairs={{0,1},{1,0},{2,3},{3,2},{4,5},{5,4},{6,7},{7,6},{8,9},{9,8},{10,11... | collective-permute-start | bytes 3145736 | tf_op jit(solution)/shard_map/ppermute | solution.py:251
  53.9 1.1 shard_map.77
  55.0 1.2 %collective-permute-done.1.got_ref = bf16[1024,512]{1,0:T(8,128)(2,1)S(1)} collective-permute-done((bf16[1024,512]{1,0:T(8,128)(2,1)S(1)}, bf16[1024,512]{1,0:T(8,128)(2,1)S(1)}, u32[]{:S(2)}, u32[]{:S(2)}) %collective-permute-start.1) | collective-permute-done | bytes 1048608 | tf_op jit(solution)/shard_map/ppermute | solution.py:251
  56.2 2.9 %shard_map.78 = (bf16[512,512]{1,0:T(8,128)(2,1)S(1)}, bf16[16,256,128]{2,1,0:T(8,128)(2,1)S(1)}, f32[8,128]{1,0:T(8,128)S(1)}) custom-call(s32[3]{0:T(128)S(1)} %pad_add_fusion.core_ref, bf16[16,2,64,512]{3,2,1,0:T(8,128)(2,1)S(1)} %all_to_all.15.own_ref, bf16[512,1024]{1,0:T(8,128)(2,1)S(1)} %get-tuple-element.21.own_t_ref, ...), custom_call_target="tpu_custom_call" | custom-call | flops 1073741824 | bytes 4194304 | tf_op jit(solution)/shard_map/pallas_call | solution.py:262
  59.1 1.3 %shard_map.79 = (bf16[16,256,128]{2,1,0:T(8,128)(2,1)S(1)}, bf16[16,256,128]{2,1,0:T(8,128)(2,1)S(1)}, bf16[16,16,128]{2,1,0:T(8,128)(2,1)S(1)}) custom-call(s32[3]{0:T(128)S(1)} %pad_add_fusion.core_ref, bf16[1024,512]{1,0:T(8,128)(2,1)S(1)} %collective-permute-done.1.got_ref, bf16[512,512]{1,0:T(8,128)(2,1)S(1)} %get-tuple-element.24.weights_ref, ...), custom_call_target="tpu_custom_call" | custom-call | flops 536870912 | bytes 4194304 | tf_op jit(solution)/shard_map/pallas_call | solution.py:270
  60.5 2.2 %collective-permute-start.3 = (bf16[16,256,128]{2,1,0:T(8,128)(2,1)S(1)}, bf16[16,256,128]{2,1,0:T(8,128)(2,1)S(1)}, u32[]{:S(2)}, u32[]{:S(2)}) collective-permute-start(bf16[16,256,128]{2,1,0:T(8,128)(2,1)S(1)} %get-tuple-element.28), channel_id=1, source_target_pairs={{256,1},{1,257},{258,3},{3,259},{260,5},{5,261},{262,7},{7,263},{2... | collective-permute-start | bytes 3145736 | tf_op jit(solution)/shard_map/ppermute | solution.py:277
  62.7 1.9 %collective-permute-start.2 = (bf16[16,256,128]{2,1,0:T(8,128)(2,1)S(1)}, bf16[16,256,128]{2,1,0:T(8,128)(2,1)S(1)}, u32[]{:S(2)}, u32[]{:S(2)}) collective-permute-start(bf16[16,256,128]{2,1,0:T(8,128)(2,1)S(1)} %get-tuple-element.25.first_ref), channel_id=1, source_target_pairs={{0,1},{1,0},{2,3},{3,2},{4,5},{5,4},{6,7},{7,6},{8,9},{9,8},{10,11... | collective-permute-start | bytes 3145736 | tf_op jit(solution)/shard_map/ppermute | solution.py:269
  64.6 13.3 %all_to_all.16.loss_ref = bf16[16,16,128]{2,1,0:T(8,128)(2,1)S(1)} all-to-all(bf16[16,16,128]{2,1,0:T(8,128)(2,1)S(1)} %get-tuple-element.29), channel_id=1, replica_groups={{0,32,64,96,128,160,192,224,256,288,320,352,384,416,448,480},{2,34,66,9..., dimensions={0} | all-to-all | bytes 131072 | tf_op jit(solution)/shard_map/all_to_all | solution.py:278
  77.9 0.0 collective-permute-done.3.near_ref
  77.9 0.8 shard_map.80
  78.7 25.4 %all_to_all.17.got_ref = bf16[16,272,128]{2,1,0:T(8,128)(2,1)S(1)} all-to-all(bf16[16,272,128]{2,1,0:T(8,128)(2,1)S(1)} %shard_map.80), channel_id=1, replica_groups={{0,2,4,6,8,10,12,14,16,18,20,22,24,26,28,30},{32,34,36,38,40,42,44,46,4..., dimensions={0} | all-to-all | bytes 2228224 | tf_op jit(solution)/shard_map/all_to_all | solution.py:282
  104.2 0.8 shard_map.81
  104.9 4.6 %collective-permute-start.4 = (f32[72,512]{1,0:T(8,128)S(1)}, f32[72,512]{1,0:T(8,128)S(1)}, u32[]{:S(2)}, u32[]{:S(2)}) collective-permute-start(f32[72,512]{1,0:T(8,128)S(1)} %get-tuple-element.31.give_ref), channel_id=1, source_target_pairs={{0,1},{1,0},{2,3},{3,2},{4,5},{5,4},{6,7},{7,6},{8,9},{9,8},{10,11... | collective-permute-start | bytes 442376 | tf_op jit(solution)/shard_map/ppermute | solution.py:291
  109.6 1.0 collective-permute-done.4.taken_ref
  110.5 1.2 %shard_map.82 = (f32[32,512]{1,0:T(8,128)}, f32[64,512]{1,0:T(8,128)}, f32[1,1]{1,0:T(1,128)}) custom-call(s32[3]{0:T(128)S(1)} %pad_add_fusion.core_ref, f32[64,512]{1,0:T(8,128)S(1)} %get-tuple-element.30.keep_ref, f32[72,512]{1,0:T(8,128)S(1)} %get-tuple-element.31.give_ref, f32[72,512]{1,0:T(8,128)S(1)} %collective-permute-done.4.taken_ref), custom_call_target="tpu_custom_call" | custom-call | tf_op jit(solution)/shard_map/pallas_call | solution.py:292
  (3 shorter events, 0.0 us)
Async XLA Ops:
  1.6 10.9 %collective-permute-start = (bf16[64,512]{1,0:T(8,128)(2,1)S(1)}, bf16[64,512]{1,0:T(8,128)(2,1)S(1)}, u32[]{:S(2)}, u32[]{:S(2)}) collective-permute-start(bf16[64,512]{1,0:T(8,128)(2,1)S(1)} %get-tuple-element.35), channel_id=1, source_target_pairs={{0,1},{1,0},{2,3},{3,2},{4,5},{5,4},{6,7},{7,6},{8,9},{9,8},{10,11... | collective-permute-start | bytes 196616 | tf_op jit(solution)/shard_map/ppermute | solution.py:245
  43.3 12.9 %collective-permute-start.1 = (bf16[1024,512]{1,0:T(8,128)(2,1)S(1)}, bf16[1024,512]{1,0:T(8,128)(2,1)S(1)}, u32[]{:S(2)}, u32[]{:S(2)}) collective-permute-start(bf16[1024,512]{1,0:T(8,128)(2,1)S(1)} %bitcast.15), channel_id=1, source_target_pairs={{0,1},{1,0},{2,3},{3,2},{4,5},{5,4},{6,7},{7,6},{8,9},{9,8},{10,11... | collective-permute-start | bytes 3145736 | tf_op jit(solution)/shard_map/ppermute | solution.py:251
  60.5 17.4 %collective-permute-start.3 = (bf16[16,256,128]{2,1,0:T(8,128)(2,1)S(1)}, bf16[16,256,128]{2,1,0:T(8,128)(2,1)S(1)}, u32[]{:S(2)}, u32[]{:S(2)}) collective-permute-start(bf16[16,256,128]{2,1,0:T(8,128)(2,1)S(1)} %get-tuple-element.28), channel_id=1, source_target_pairs={{256,1},{1,257},{258,3},{3,259},{260,5},{5,261},{262,7},{7,263},{2... | collective-permute-start | bytes 3145736 | tf_op jit(solution)/shard_map/ppermute | solution.py:277
  62.7 15.2 %collective-permute-start.2 = (bf16[16,256,128]{2,1,0:T(8,128)(2,1)S(1)}, bf16[16,256,128]{2,1,0:T(8,128)(2,1)S(1)}, u32[]{:S(2)}, u32[]{:S(2)}) collective-permute-start(bf16[16,256,128]{2,1,0:T(8,128)(2,1)S(1)} %get-tuple-element.25.first_ref), channel_id=1, source_target_pairs={{0,1},{1,0},{2,3},{3,2},{4,5},{5,4},{6,7},{7,6},{8,9},{9,8},{10,11... | collective-permute-start | bytes 3145736 | tf_op jit(solution)/shard_map/ppermute | solution.py:269
  104.9 5.6 %collective-permute-start.4 = (f32[72,512]{1,0:T(8,128)S(1)}, f32[72,512]{1,0:T(8,128)S(1)}, u32[]{:S(2)}, u32[]{:S(2)}) collective-permute-start(f32[72,512]{1,0:T(8,128)S(1)} %get-tuple-element.31.give_ref), channel_id=1, source_target_pairs={{0,1},{1,0},{2,3},{3,2},{4,5},{5,4},{6,7},{7,6},{8,9},{9,8},{10,11... | collective-permute-start | bytes 442376 | tf_op jit(solution)/shard_map/ppermute | solution.py:291

commit v6 on v5

--- a/solution.py
+++ b/solution.py
@@ -35,35 +35,35 @@
 
 
 def chunk_kernel(core_ref, mine_ref, other_ref, out_ref):
+    blocks = out_ref.shape[0]
     half = mine_ref.shape[0] // 2
     mine = mine_ref[...]
     other = other_ref[...]
-    pair = jnp.concatenate([mine[:half], other[:half]], axis=0)
 
     @pl.when(core_ref[0] == 0)
     def _():
-        for block in range(out_ref.shape[0]):
-            out_ref[block, 0] = pair
-            out_ref[block, 1] = pair
+        pair = jnp.concatenate([mine[:half], other[:half]], axis=0)
+        for block in range(blocks):
+            out_ref[block] = pair
 
     @pl.when(core_ref[0] != 0)
     def _():
-        for block in range(out_ref.shape[0]):
-            out_ref[block, 0] = other
-            out_ref[block, 1] = mine
-
-
-def side_kernel(robots, core_ref, own_ref, table_ref, own_t_ref, out_ref, out_t_ref):
-    blocks, _, size, _ = own_ref.shape
-    count = table_ref.shape[1]
-    robot = table_ref[1:2, :]
+        for block in range(blocks // 2):
+            out_ref[block] = other
+        for block in range(blocks // 2, blocks):
+            out_ref[block] = mine
+
+
+def side_kernel(core_ref, bias_ref, ids_ref, got_ref, out_ref, out_t_ref):
+    count = ids_ref.shape[1]
+    first = core_ref[0] == 0
+    robot = jnp.where(first & (core_ref[2] == 0), ids_ref[1:2, :], got_ref[1:2, :])
     bias = jnp.zeros((1, count), F32)
-    for index in range(robots):
-        bias = jnp.where(robot == index, table_ref[2:3, index : index + 1], bias)
+    for index in range(bias_ref.shape[1]):
+        bias = jnp.where(robot == index, bias_ref[:, index : index + 1], bias)
     zero = jnp.zeros((1, count), F32)
-    positive = table_ref[0:1, :]
+    positive = jnp.where(first, ids_ref[0:1, :], got_ref[0:1, :]).astype(F32)
     columns = (lax.broadcasted_iota(jnp.int32, (1, count), 1) + core_ref[1] * count).astype(F32)
-    first = core_ref[0] == 0
     rows = [
         jnp.where(first, zero, bias),
         jnp.where(first, positive, columns),
@@ -74,13 +74,15 @@
     side = jnp.concatenate(rows, axis=0)
     out_ref[...] = side
     out_t_ref[...] = side.T
-    own_t_ref[...] = own_ref[:, core_ref[0]].reshape(blocks * size, count).T
-
-
-def logits_kernel(scale, step, core_ref, own_ref, own_t_ref, got_ref, side_ref, side_t_ref, weights_ref, grad_ref, loss_ref):
-    blocks, _, rows, count = own_ref.shape
-    width = blocks * rows
-    own = own_ref[:, core_ref[0]].reshape(width, count)
+
+
+def transpose_kernel(own_ref, own_t_ref):
+    own_t_ref[...] = own_ref[...].T
+
+
+def logits_kernel(scale, step, own_ref, own_t_ref, got_ref, side_ref, side_t_ref, weights_ref, grad_ref, loss_ref):
+    count = own_ref.shape[1]
+    own = own_ref[...]
     own_t = own_t_ref[...]
     row_bias = side_t_ref[:, 0:1]
     row_key = side_t_ref[:, 1:2]
@@ -103,30 +105,19 @@
     loss_ref[...] = jnp.broadcast_to(total, loss_ref.shape)
 
 
-def second_kernel(step, core_ref, got_ref, weights_ref, first_ref, loss_ref, grad_ref, send_ref, rows_ref):
-    size = grad_ref.shape[1]
+def second_kernel(step, got_ref, weights_ref, loss_ref, grad_ref, rows_ref):
     rows_ref[...] = loss_rows(jnp.broadcast_to(loss_ref[0:1, :], rows_ref.shape), rows_ref.shape)
     for start in range(0, weights_ref.shape[0], step):
         weights = weights_ref[start : start + step, :]
         grad = lax.dot_general(got_ref[...], weights, (((1,), (1,)), ((), ())), preferred_element_type=F32)
         store_blocks(grad_ref, grad, start)
 
-    @pl.when(core_ref[0] == 0)
-    def _():
-        for block in range(grad_ref.shape[0]):
-            send_ref[block] = first_ref[block]
-
-    @pl.when(core_ref[0] != 0)
-    def _():
-        for block in range(grad_ref.shape[0]):
-            send_ref[block] = grad_ref[block]
-
 
 def received_loss(rows):
     return rows[0:1] + rows[4:5] + rows[8:9]
 
 
-def add_kernel(core_ref, own_ref, other_ref, near_ref, loss_ref, out_ref):
+def add_kernel(own_ref, got_ref, loss_ref, out_ref):
     blocks, size, _ = own_ref.shape
     total = loss_ref[0].astype(F32)
     for block in range(1, blocks):
@@ -134,25 +125,7 @@
     rows = loss_rows(jnp.broadcast_to(received_loss(total), total.shape), total.shape)
     for block in range(blocks):
         out_ref[block, size:, :] = rows
-    core, side = core_ref[0], core_ref[2]
-
-    @pl.when(core == 0)
-    def _():
-        for block in range(blocks):
-            added = own_ref[block].astype(F32) + other_ref[block].astype(F32)
-            out_ref[block, :size, :] = added.astype(BF16)
-
-    @pl.when((core != 0) & (side == 0))
-    def _():
-        for block in range(blocks):
-            added = other_ref[block].astype(F32) + near_ref[block].astype(F32)
-            out_ref[block, :size, :] = added.astype(BF16)
-
-    @pl.when((core != 0) & (side != 0))
-    def _():
-        for block in range(blocks):
-            added = own_ref[block].astype(F32) + near_ref[block].astype(F32)
-            out_ref[block, :size, :] = added.astype(BF16)
+        out_ref[block, :size, :] = (own_ref[block].astype(F32) + got_ref[block].astype(F32)).astype(BF16)
 
 
 def sum_kernel(clip_scale, action_scale, core_ref, got_ref, keep_ref, give_ref):
@@ -223,11 +196,13 @@
     clips_first = along_act[0] + along_clip[1]
     actions_first = along_clip[0] + along_act[1]
     swap = [(i, i ^ 1) for i in range(n_act)]
-    neighbours = []
+    gather_pass, scatter_pass, ids_pass = [], [], []
     for k in range(near):
         for m in range(pairs):
             low, high = k * n_act + 2 * m, (k + near) * n_act + 2 * m
-            neighbours += [(high, low + 1), (low + 1, high + 1)]
+            gather_pass += [(low + 1, low), (high + 1, high), (low, high + 1), (high, low + 1)]
+            scatter_pass += [(low, low + 1), (high, high + 1), (low + 1, high), (high + 1, low)]
+            ids_pass += [(high, low + 1), (low + 1, high + 1), (high + 1, high)]
     exchange = functools.partial(lax.all_to_all, axis_name=both, split_axis=0, concat_axis=0)
 
     half, count = clips.shape
@@ -235,7 +210,8 @@
     width = rows * n_clip
     parts = count // LANES
     act = lax.axis_index("act")
-    core = jnp.stack([act % 2, act, lax.axis_index("clip") // near]).astype(jnp.int32)
+    side_of = lax.axis_index("clip") // near
+    core = jnp.stack([act % 2, act - act % 2 + side_of, side_of]).astype(jnp.int32)
     shape = jax.ShapeDtypeStruct
 
     first_core = act % 2 == 0
@@ -243,17 +219,15 @@
     send = jnp.where(first_core, actions, clip_twice).astype(BF16)
     mine = jnp.where(first_core, clip_twice, actions).astype(BF16)
     other = lax.ppermute(send, "act", swap)
-    chunks = call(chunk_kernel, shape((n_clip, 2, rows, count), BF16), [SMEM, VMEM, VMEM])(core, mine, other)
-    robots = robot_bias.shape[0]
-    table = jnp.stack([positive_ids.astype(F32), robot_ids.astype(F32), jnp.pad(robot_bias, (0, count - robots))])
-    chunks, table = lax.optimization_barrier((chunks, table))
-    gathered = exchange(chunks, axis_index_groups=clips_first)
-    got = lax.ppermute(gathered[:, 0].reshape(width, count), "act", swap)
-    own_t, side, side_t = call(
-        functools.partial(side_kernel, robots),
-        (shape((count, width), BF16), shape((8, count), F32), shape((count, 8), F32)),
-        [SMEM, VMEM, VMEM],
-    )(core, gathered, table)
+    chunks = call(chunk_kernel, shape((n_clip, rows, count), BF16), [SMEM, VMEM, VMEM])(core, mine, other)
+    ids = jnp.stack([positive_ids, robot_ids])
+    own = exchange(chunks, axis_index_groups=clips_first).reshape(width, count)
+    got = lax.ppermute(own, both, gather_pass)
+    own_t = call(transpose_kernel, shape((count, width), BF16), [VMEM])(own)
+    ids_got = lax.ppermute(ids, both, ids_pass)
+    side, side_t = call(side_kernel, (shape((8, count), F32), shape((count, 8), F32)), [SMEM] + [VMEM] * 3)(
+        core, robot_bias[None, :], ids, ids_got
+    )
 
     flops = 2 * width * count * count
     step = 256
@@ -262,22 +236,21 @@
     weights, first, loss = call(
         functools.partial(logits_kernel, 2.0 / math.sqrt(width), step),
         (shape((count, count), BF16), blocks, shape((8, LANES), F32)),
-        [SMEM] + [VMEM] * 5,
+        [VMEM] * 5,
         flops=2 * flops,
         moved=8 * width * count,
-    )(core, gathered, own_t, got, side, side_t)
-    first_got = lax.ppermute(first, "act", swap)
-    second, send, loss_sent = call(
+    )(own, own_t, got, side, side_t)
+    first_got = lax.ppermute(first, both, scatter_pass)
+    second, loss_sent = call(
         functools.partial(second_kernel, step),
-        (blocks, blocks, loss_blocks),
-        [SMEM] + [VMEM] * 4,
+        (blocks, loss_blocks),
+        [VMEM] * 3,
         flops=flops,
         moved=8 * width * count,
-    )(core, got, weights, first, loss)
-    near_got = lax.ppermute(send, both, neighbours)
+    )(got, weights, loss)
     loss_got = exchange(loss_sent, axis_index_groups=actions_first)
-    ready = call(add_kernel, shape((n_clip, parts * rows + EXTRA, LANES), BF16), [SMEM] + [VMEM] * 4)(
-        core, second, first_got, near_got, loss_got
+    ready = call(add_kernel, shape((n_clip, parts * rows + EXTRA, LANES), BF16), [VMEM] * 3)(
+        second, first_got, loss_got
     )
     scattered = exchange(ready, axis_index_groups=clips_first)
 

time: 112 us -> 107 us (0.955)
  blocking collectives: 68.7 us -> 57.1 us
  waiting for transfers between devices: 2.18 us -> 12.2 us
  Pallas kernels: 8.83 us -> 7.14 us
  other arithmetic: 2.39 us -> 1.01 us
    all_to_all x1, blocking collectives: 30 us -> 18.9 us  [shards(): own = exchange(chunks, axis_index_groups=clips_first).reshape(width, count)]
    ppermute x3, waiting for transfers between devices: 1.2 us -> 10.5 us  [the longest x1 10.4 us: shards(): ids_got = lax.ppermute(ids, both, ids_pass)]
    convert_element_type x2 -> x0, other arithmetic: 1.37 us -> none  [the longest x1 0.69 us: shards(): positive_ids.astype(F32)]
    pallas_call x4 -> x5, Pallas kernels: 3.92 us -> 2.73 us  [the longest x1 0.78 us: shards(): call(side_kernel, (shape((8, count), F32), shape((count, 8), F32)), [SMEM...]
    all_to_all x1, blocking collectives: 25.4 us -> 24.3 us  [shards(): scattered = exchange(ready, axis_index_groups=clips_first)]
  transfers between devices with their start and end apart: 5 -> 5, of which waited for: 2 -> 3; matrix products, arithmetic and copies ran while one was open for 2% -> 0% of each run, Pallas kernels for 1% -> 2%
where the time goes in v6:
time: 107 us
  blocking collectives  57.1 us (53%)
  starting transfers between devices  28.8 us (27%)
  waiting for transfers between devices  12.2 us (11%)
  Pallas kernels  7.14 us (7%)
    all_to_all x1, blocking collectives, shards(): scattered = exchange(ready, axis_index_groups=clips_first)  24.3 us
    all_to_all x1, blocking collectives, shards(): own = exchange(chunks, axis_index_groups=clips_first).reshape(width, count)  18.9 us
    all_to_all x1, blocking collectives, shards(): loss_got = exchange(loss_sent, axis_index_groups=actions_first)  13.9 us
    ppermute x1, starting transfers between devices, shards(): got = lax.ppermute(own, both, gather_pass)  10.9 us
    ppermute x1, waiting for transfers between devices, shards(): ids_got = lax.ppermute(ids, both, ids_pass)  10.4 us
    ppermute x1, starting transfers between devices, shards(): other = lax.ppermute(send, 'act', swap)  8.79 us
    ppermute x1, starting transfers between devices, shards(): taken = lax.ppermute(give, 'act', swap)  4.95 us
    pallas_call x1, Pallas kernels, shards(): call(functools.partial(logits_kernel, 2.0 / math.sqrt(width), step), (sha...  2.39 us
  transfers between devices with their start and end apart: 5, of which 3 were waited for; matrix products, arithmetic and copies ran while one was open for 0% of the time, Pallas kernels for 2%

profile of v6, /device:TPU:1, one launch (start us, length us, event | category | flops | bytes accessed | tf_op | source)
XLA Modules:
  0.0 107.1 jit_solution(15363669276273618557)
XLA Ops:
  0.6 0.9 fusion.1
  1.6 8.8 %collective-permute-start = (bf16[64,512]{1,0:T(8,128)(2,1)S(1)}, bf16[64,512]{1,0:T(8,128)(2,1)S(1)}, u32[]{:S(2)}, u32[]{:S(2)}) collective-permute-start(bf16[64,512]{1,0:T(8,128)(2,1)S(1)} %get-tuple-element.27), channel_id=1, source_target_pairs={{0,1},{1,0},{2,3},{3,2},{4,5},{5,4},{6,7},{7,6},{8,9},{9,8},{10,11... | collective-permute-start | bytes 196616 | tf_op jit(solution)/shard_map/ppermute | solution.py:221
  10.4 0.1 pad_add_fusion.1.core_ref
  10.5 0.8 collective-permute-done.other_ref
  11.2 0.6 shard_map.76
  11.9 0.0 copy-start.1
  11.9 0.0 copy-start.2
  11.9 0.0 copy-start
  11.9 18.9 %all_to_all.15 = bf16[16,64,512]{2,1,0:T(8,128)(2,1)S(1)} all-to-all(bf16[16,64,512]{2,1,0:T(8,128)(2,1)S(1)} %shard_map.76), channel_id=1, replica_groups={{0,2,4,6,8,10,12,14,16,18,20,22,24,26,28,30},{32,34,36,38,40,42,44,46,4..., dimensions={0} | all-to-all | bytes 2097152 | tf_op jit(solution)/shard_map/all_to_all | solution.py:224
  30.8 10.9 %collective-permute-start.1 = (bf16[1024,512]{1,0:T(8,128)(2,1)S(1)}, bf16[1024,512]{1,0:T(8,128)(2,1)S(1)}, u32[]{:S(2)}, u32[]{:S(2)}) collective-permute-start(bf16[1024,512]{1,0:T(8,128)(2,1)S(1)} %bitcast.15), channel_id=1, source_target_pairs={{1,0},{257,256},{0,257},{256,1},{3,2},{259,258},{2,259},{258,3},{5... | collective-permute-start | bytes 3145736 | tf_op jit(solution)/shard_map/ppermute | solution.py:225
  41.8 2.2 %collective-permute-start.2 = (s32[2,512]{1,0:T(2,128)S(1)}, s32[2,512]{1,0:T(2,128)S(1)}, u32[]{:S(2)}, u32[]{:S(2)}) collective-permute-start(s32[2,512]{1,0:T(2,128)S(1)} %pad_add_fusion.ids_ref), channel_id=1, source_target_pairs={{256,1},{1,257},{257,256},{258,3},{3,259},{259,258},{260,5},{5,261... | collective-permute-start | bytes 12296 | tf_op jit(solution)/shard_map/ppermute | solution.py:227
  44.0 10.4 %collective-permute-done.2.got_ref = s32[2,512]{1,0:T(2,128)S(1)} collective-permute-done((s32[2,512]{1,0:T(2,128)S(1)}, s32[2,512]{1,0:T(2,128)S(1)}, u32[]{:S(2)}, u32[]{:S(2)}) %collective-permute-start.2) | collective-permute-done | bytes 4128 | tf_op jit(solution)/shard_map/ppermute | solution.py:227
  54.5 0.8 shard_map.78
  55.3 0.3 shard_map.77.own_t_ref
  55.6 2.4 %shard_map.79 = (bf16[512,512]{1,0:T(8,128)(2,1)S(1)}, bf16[16,256,128]{2,1,0:T(8,128)(2,1)S(1)}, f32[8,128]{1,0:T(8,128)S(1)}) custom-call(bf16[1024,512]{1,0:T(8,128)(2,1)S(1)} %bitcast.17, bf16[512,1024]{1,0:T(8,128)(2,1)S(1)} %shard_map.77.own_t_ref, bf16[1024,512]{1,0:T(8,128)(2,1)S(1)} %collective-permute-done.1.got_ref, ...), custom_call_target="tpu_custom_call" | custom-call | flops 1073741824 | bytes 4194304 | tf_op jit(solution)/shard_map/pallas_call | solution.py:236
  58.0 1.9 %collective-permute-start.3 = (bf16[16,256,128]{2,1,0:T(8,128)(2,1)S(1)}, bf16[16,256,128]{2,1,0:T(8,128)(2,1)S(1)}, u32[]{:S(2)}, u32[]{:S(2)}) collective-permute-start(bf16[16,256,128]{2,1,0:T(8,128)(2,1)S(1)} %get-tuple-element.20), channel_id=1, source_target_pairs={{0,1},{256,257},{1,256},{257,0},{2,3},{258,259},{3,258},{259,2},{4... | collective-permute-start | bytes 3145736 | tf_op jit(solution)/shard_map/ppermute | solution.py:243
  60.0 0.7 shard_map.80
  60.7 13.9 %all_to_all.16.loss_ref = bf16[16,16,128]{2,1,0:T(8,128)(2,1)S(1)} all-to-all(bf16[16,16,128]{2,1,0:T(8,128)(2,1)S(1)} %get-tuple-element.21), channel_id=1, replica_groups={{0,32,64,96,128,160,192,224,256,288,320,352,384,416,448,480},{2,34,66,9..., dimensions={0} | all-to-all | bytes 131072 | tf_op jit(solution)/shard_map/all_to_all | solution.py:251
  74.6 0.3 shard_map.81
  74.8 24.3 %all_to_all.17.got_ref = bf16[16,272,128]{2,1,0:T(8,128)(2,1)S(1)} all-to-all(bf16[16,272,128]{2,1,0:T(8,128)(2,1)S(1)} %shard_map.81), channel_id=1, replica_groups={{0,2,4,6,8,10,12,14,16,18,20,22,24,26,28,30},{32,34,36,38,40,42,44,46,4..., dimensions={0} | all-to-all | bytes 2228224 | tf_op jit(solution)/shard_map/all_to_all | solution.py:255
  99.1 0.8 shard_map.82
  99.9 4.9 %collective-permute-start.4 = (f32[72,512]{1,0:T(8,128)S(1)}, f32[72,512]{1,0:T(8,128)S(1)}, u32[]{:S(2)}, u32[]{:S(2)}) collective-permute-start(f32[72,512]{1,0:T(8,128)S(1)} %get-tuple-element.23.give_ref), channel_id=1, source_target_pairs={{0,1},{1,0},{2,3},{3,2},{4,5},{5,4},{6,7},{7,6},{8,9},{9,8},{10,11... | collective-permute-start | bytes 442376 | tf_op jit(solution)/shard_map/ppermute | solution.py:264
  104.9 1.0 collective-permute-done.4.taken_ref
  105.9 1.2 %shard_map.83 = (f32[32,512]{1,0:T(8,128)}, f32[64,512]{1,0:T(8,128)}, f32[1,1]{1,0:T(1,128)}) custom-call(s32[3]{0:T(128)S(1)} %pad_add_fusion.1.core_ref, f32[64,512]{1,0:T(8,128)S(1)} %get-tuple-element.22.keep_ref, f32[72,512]{1,0:T(8,128)S(1)} %get-tuple-element.23.give_ref, f32[72,512]{1,0:T(8,128)S(1)} %collective-permute-done.4.taken_ref), custom_call_target="tpu_custom_call" | custom-call | tf_op jit(solution)/shard_map/pallas_call | solution.py:265
  (6 shorter events, 0.0 us)
Async XLA Ops:
  1.6 9.7 %collective-permute-start = (bf16[64,512]{1,0:T(8,128)(2,1)S(1)}, bf16[64,512]{1,0:T(8,128)(2,1)S(1)}, u32[]{:S(2)}, u32[]{:S(2)}) collective-permute-start(bf16[64,512]{1,0:T(8,128)(2,1)S(1)} %get-tuple-element.27), channel_id=1, source_target_pairs={{0,1},{1,0},{2,3},{3,2},{4,5},{5,4},{6,7},{7,6},{8,9},{9,8},{10,11... | collective-permute-start | bytes 196616 | tf_op jit(solution)/shard_map/ppermute | solution.py:221
  11.9 29.9 %copy-start.1 = (s32[512]{0:T(512)S(1)}, s32[512]{0:T(512)}, u32[]{:S(2)}) copy-start(s32[512]{0:T(512)} %param.8) | copy-start | bytes 6148
  11.9 29.9 %copy-start.2 = (s32[512]{0:T(512)S(1)}, s32[512]{0:T(512)}, u32[]{:S(2)}) copy-start(s32[512]{0:T(512)} %param.7) | copy-start | bytes 6148
  11.9 42.6 %copy-start = (f32[16]{0:T(128)S(1)}, f32[16]{0:T(128)}, u32[]{:S(2)}) copy-start(f32[16]{0:T(128)} %param.9) | copy-start | bytes 196
  30.8 24.8 %collective-permute-start.1 = (bf16[1024,512]{1,0:T(8,128)(2,1)S(1)}, bf16[1024,512]{1,0:T(8,128)(2,1)S(1)}, u32[]{:S(2)}, u32[]{:S(2)}) collective-permute-start(bf16[1024,512]{1,0:T(8,128)(2,1)S(1)} %bitcast.15), channel_id=1, source_target_pairs={{1,0},{257,256},{0,257},{256,1},{3,2},{259,258},{2,259},{258,3},{5... | collective-permute-start | bytes 3145736 | tf_op jit(solution)/shard_map/ppermute | solution.py:225
  41.8 12.7 %collective-permute-start.2 = (s32[2,512]{1,0:T(2,128)S(1)}, s32[2,512]{1,0:T(2,128)S(1)}, u32[]{:S(2)}, u32[]{:S(2)}) collective-permute-start(s32[2,512]{1,0:T(2,128)S(1)} %pad_add_fusion.ids_ref), channel_id=1, source_target_pairs={{256,1},{1,257},{257,256},{258,3},{3,259},{259,258},{260,5},{5,261... | collective-permute-start | bytes 12296 | tf_op jit(solution)/shard_map/ppermute | solution.py:227
  58.0 16.6 %collective-permute-start.3 = (bf16[16,256,128]{2,1,0:T(8,128)(2,1)S(1)}, bf16[16,256,128]{2,1,0:T(8,128)(2,1)S(1)}, u32[]{:S(2)}, u32[]{:S(2)}) collective-permute-start(bf16[16,256,128]{2,1,0:T(8,128)(2,1)S(1)} %get-tuple-element.20), channel_id=1, source_target_pairs={{0,1},{256,257},{1,256},{257,0},{2,3},{258,259},{3,258},{259,2},{4... | collective-permute-start | bytes 3145736 | tf_op jit(solution)/shard_map/ppermute | solution.py:243
  99.9 5.9 %collective-permute-start.4 = (f32[72,512]{1,0:T(8,128)S(1)}, f32[72,512]{1,0:T(8,128)S(1)}, u32[]{:S(2)}, u32[]{:S(2)}) collective-permute-start(f32[72,512]{1,0:T(8,128)S(1)} %get-tuple-element.23.give_ref), channel_id=1, source_target_pairs={{0,1},{1,0},{2,3},{3,2},{4,5},{5,4},{6,7},{7,6},{8,9},{9,8},{10,11... | collective-permute-start | bytes 442376 | tf_op jit(solution)/shard_map/ppermute | solution.py:264

commit v7 on v6

--- a/solution.py
+++ b/solution.py
@@ -34,6 +34,10 @@
         out_ref[:, at : at + rows, :] = columns.reshape(blocks, rows, LANES).astype(BF16)
 
 
+def block_of(index, blocks):
+    return (index // (blocks // 2) + index) % 2
+
+
 def chunk_kernel(core_ref, mine_ref, other_ref, out_ref):
     blocks = out_ref.shape[0]
     half = mine_ref.shape[0] // 2
@@ -48,50 +52,56 @@
 
     @pl.when(core_ref[0] != 0)
     def _():
-        for block in range(blocks // 2):
-            out_ref[block] = other
-        for block in range(blocks // 2, blocks):
-            out_ref[block] = mine
-
-
-def side_kernel(core_ref, bias_ref, ids_ref, got_ref, out_ref, out_t_ref):
-    count = ids_ref.shape[1]
+        for block in range(blocks):
+            out_ref[block] = mine if block_of(block, blocks) else other
+
+
+def split_kernel(own_ref, positive_ref, robot_ref, low_ref, high_ref):
+    width = own_ref.shape[0]
+    positive = positive_ref[...]
+    rows = [positive // LANES, positive % LANES, robot_ref[...]]
+    rows = jnp.concatenate(rows + [jnp.zeros_like(positive)] * (EXTRA - len(rows)), axis=0)
+    rows = rows.astype(F32).astype(BF16)
+    half = low_ref.shape[1]
+    low_ref[:width, :] = own_ref[:, :half]
+    low_ref[width:, :] = rows[:, :half]
+    high_ref[:width, :] = own_ref[:, half:]
+    high_ref[width:, :] = rows[:, half:]
+
+
+def transpose_kernel(own_ref, own_t_ref):
+    own_t_ref[...] = own_ref[...].T
+
+
+def sides(core_ref, bias_ref, positive_ref, robot_ref, got_rows):
+    count = robot_ref.shape[1]
     first = core_ref[0] == 0
-    robot = jnp.where(first & (core_ref[2] == 0), ids_ref[1:2, :], got_ref[1:2, :])
+    robot = jnp.where(core_ref[0] == core_ref[2], robot_ref[...].astype(F32), got_rows[2:3, :])
     bias = jnp.zeros((1, count), F32)
     for index in range(bias_ref.shape[1]):
         bias = jnp.where(robot == index, bias_ref[:, index : index + 1], bias)
     zero = jnp.zeros((1, count), F32)
-    positive = jnp.where(first, ids_ref[0:1, :], got_ref[0:1, :]).astype(F32)
-    columns = (lax.broadcasted_iota(jnp.int32, (1, count), 1) + core_ref[1] * count).astype(F32)
-    rows = [
-        jnp.where(first, zero, bias),
-        jnp.where(first, positive, columns),
-        jnp.where(first, bias, zero),
-        jnp.where(first, columns, positive),
-        zero, zero, zero, zero,
-    ]
-    side = jnp.concatenate(rows, axis=0)
-    out_ref[...] = side
-    out_t_ref[...] = side.T
-
-
-def transpose_kernel(own_ref, own_t_ref):
-    own_t_ref[...] = own_ref[...].T
-
-
-def logits_kernel(scale, step, own_ref, own_t_ref, got_ref, side_ref, side_t_ref, weights_ref, grad_ref, loss_ref):
-    count = own_ref.shape[1]
+    positive = jnp.where(first, positive_ref[...].astype(F32), got_rows[0:1, :] * LANES + got_rows[1:2, :])
+    action = (lax.broadcasted_iota(jnp.int32, (1, count), 1) + core_ref[1] * count).astype(F32)
+    rows = [jnp.where(first, zero, bias), jnp.where(first, positive, action)]
+    columns = [jnp.where(first, bias, zero), jnp.where(first, action, positive)]
+    rows = jnp.concatenate(rows + [zero] * 6, axis=0).T
+    return rows[:, 0:1], rows[:, 1:2], columns[0], columns[1]
+
+
+def logits_kernel(scale, core_ref, bias_ref, positive_ref, robot_ref, own_ref, own_t_ref, low_ref, high_ref,
+                  weights_ref, low_grad_ref, high_grad_ref, loss_ref):
+    width = own_ref.shape[0]
+    step = low_ref.shape[1]
+    got_rows = jnp.concatenate([low_ref[width:, :], high_ref[width:, :]], axis=1).astype(F32)
+    row_bias, row_key, column_bias, column_key = sides(core_ref, bias_ref, positive_ref, robot_ref, got_rows)
     own = own_ref[...]
     own_t = own_t_ref[...]
-    row_bias = side_t_ref[:, 0:1]
-    row_key = side_t_ref[:, 1:2]
     total = jnp.zeros((1, 1), F32)
-    for start in range(0, count, step):
-        got = got_ref[:, start : start + step]
-        logits = jnp.dot(own_t, got, preferred_element_type=F32) * scale
-        logits = logits + (row_bias + side_ref[2:3, start : start + step])
-        positive = row_key == side_ref[3:4, start : start + step]
+    for start, got_ref, grad_ref in ((0, low_ref, low_grad_ref), (step, high_ref, high_grad_ref)):
+        logits = jnp.dot(own_t, got_ref[:width, :], preferred_element_type=F32) * scale
+        logits = logits + (row_bias + column_bias[:, start : start + step])
+        positive = row_key == column_key[:, start : start + step]
         margin = jnp.where(positive, -logits, logits)
         small = jnp.exp(-jnp.abs(margin))
         above = 1.0 + small
@@ -101,15 +111,19 @@
         sigmoid = jnp.where(margin >= 0.0, inverse, small * inverse)
         weights = jnp.where(positive, -sigmoid, sigmoid).astype(BF16)
         weights_ref[:, start : start + step] = weights
-        store_blocks(grad_ref, jnp.dot(own, weights, preferred_element_type=F32), start)
+        store_blocks(grad_ref, jnp.dot(own, weights, preferred_element_type=F32), 0)
     loss_ref[...] = jnp.broadcast_to(total, loss_ref.shape)
 
 
-def second_kernel(step, got_ref, weights_ref, loss_ref, grad_ref, rows_ref):
+def second_kernel(low_ref, high_ref, weights_ref, loss_ref, grad_ref, rows_ref):
     rows_ref[...] = loss_rows(jnp.broadcast_to(loss_ref[0:1, :], rows_ref.shape), rows_ref.shape)
+    step = low_ref.shape[1]
+    width = low_ref.shape[0] - EXTRA
+    by_columns = (((1,), (1,)), ((), ()))
     for start in range(0, weights_ref.shape[0], step):
         weights = weights_ref[start : start + step, :]
-        grad = lax.dot_general(got_ref[...], weights, (((1,), (1,)), ((), ())), preferred_element_type=F32)
+        grad = lax.dot_general(low_ref[:width, :], weights[:, :step], by_columns, preferred_element_type=F32)
+        grad += lax.dot_general(high_ref[:width, :], weights[:, step:], by_columns, preferred_element_type=F32)
         store_blocks(grad_ref, grad, start)
 
 
@@ -117,15 +131,18 @@
     return rows[0:1] + rows[4:5] + rows[8:9]
 
 
-def add_kernel(own_ref, got_ref, loss_ref, out_ref):
+def add_kernel(own_ref, low_ref, high_ref, loss_ref, out_ref):
     blocks, size, _ = own_ref.shape
+    half = size // 2
     total = loss_ref[0].astype(F32)
     for block in range(1, blocks):
         total = total + loss_ref[block].astype(F32)
     rows = loss_rows(jnp.broadcast_to(received_loss(total), total.shape), total.shape)
     for block in range(blocks):
+        own = own_ref[block].astype(F32)
+        out_ref[block, :half, :] = (own[:half] + low_ref[block].astype(F32)).astype(BF16)
+        out_ref[block, half:size, :] = (own[half:] + high_ref[block].astype(F32)).astype(BF16)
         out_ref[block, size:, :] = rows
-        out_ref[block, :size, :] = (own_ref[block].astype(F32) + got_ref[block].astype(F32)).astype(BF16)
 
 
 def sum_kernel(clip_scale, action_scale, core_ref, got_ref, keep_ref, give_ref):
@@ -133,14 +150,15 @@
     rows, count = keep_ref.shape
     half = rows // 2
 
-    def over(first, last):
-        total = got_ref[first].astype(F32)
-        for block in range(first + 1, last):
+    def over(kind):
+        chosen = [block for block in range(blocks) if block_of(block, blocks) == kind]
+        total = got_ref[chosen[0]].astype(F32)
+        for block in chosen[1:]:
             total = total + got_ref[block].astype(F32)
         return total
 
-    lower = over(0, blocks // 2)
-    upper = over(blocks // 2, blocks)
+    lower = over(0)
+    upper = over(1)
     both = lower + upper
     loss = received_loss(both[both.shape[0] - EXTRA :])
     give_ref[rows:, :] = jnp.concatenate([jnp.broadcast_to(loss, (8, LANES))] * (count // LANES), axis=1)
@@ -196,13 +214,12 @@
     clips_first = along_act[0] + along_clip[1]
     actions_first = along_clip[0] + along_act[1]
     swap = [(i, i ^ 1) for i in range(n_act)]
-    gather_pass, scatter_pass, ids_pass = [], [], []
-    for k in range(near):
-        for m in range(pairs):
-            low, high = k * n_act + 2 * m, (k + near) * n_act + 2 * m
-            gather_pass += [(low + 1, low), (high + 1, high), (low, high + 1), (high, low + 1)]
-            scatter_pass += [(low, low + 1), (high, high + 1), (low + 1, high), (high + 1, low)]
-            ids_pass += [(high, low + 1), (low + 1, high + 1), (high + 1, high)]
+    gather_pass, scatter_pass = [], []
+    for neighbour in (lambda k: (k + near) % n_clip, lambda k: k ^ 1):
+        there = [(k * n_act + 2 * m, neighbour(k) * n_act + 2 * m + 1) for k in range(n_clip) for m in range(pairs)]
+        here = [(k * n_act + 2 * m, k * n_act + 2 * m + 1) for k in range(n_clip) for m in range(pairs)]
+        gather_pass.append(there + [(b, a) for a, b in here])
+        scatter_pass.append(here + [(b, a) for a, b in there])
     exchange = functools.partial(lax.all_to_all, axis_name=both, split_axis=0, concat_axis=0)
 
     half, count = clips.shape
@@ -210,8 +227,8 @@
     width = rows * n_clip
     parts = count // LANES
     act = lax.axis_index("act")
-    side_of = lax.axis_index("clip") // near
-    core = jnp.stack([act % 2, act - act % 2 + side_of, side_of]).astype(jnp.int32)
+    kind = block_of(lax.axis_index("clip"), n_clip)
+    core = jnp.stack([act % 2, act - act % 2 + kind, kind]).astype(jnp.int32)
     shape = jax.ShapeDtypeStruct
 
     first_core = act % 2 == 0
@@ -220,37 +237,33 @@
     mine = jnp.where(first_core, clip_twice, actions).astype(BF16)
     other = lax.ppermute(send, "act", swap)
     chunks = call(chunk_kernel, shape((n_clip, rows, count), BF16), [SMEM, VMEM, VMEM])(core, mine, other)
-    ids = jnp.stack([positive_ids, robot_ids])
+    positive_ids, robot_ids = positive_ids[None, :], robot_ids[None, :]
     own = exchange(chunks, axis_index_groups=clips_first).reshape(width, count)
-    got = lax.ppermute(own, both, gather_pass)
+    halves = shape((width + EXTRA, count // 2), BF16)
+    low, high = call(split_kernel, (halves, halves), [VMEM] * 3)(own, positive_ids, robot_ids)
+    low = lax.ppermute(low, both, gather_pass[0])
+    high = lax.ppermute(high, both, gather_pass[1])
     own_t = call(transpose_kernel, shape((count, width), BF16), [VMEM])(own)
-    ids_got = lax.ppermute(ids, both, ids_pass)
-    side, side_t = call(side_kernel, (shape((8, count), F32), shape((count, 8), F32)), [SMEM] + [VMEM] * 3)(
-        core, robot_bias[None, :], ids, ids_got
-    )
 
     flops = 2 * width * count * count
-    step = 256
     blocks = shape((n_clip, parts * rows, LANES), BF16)
+    half_blocks = shape((n_clip, parts * rows // 2, LANES), BF16)
     loss_blocks = shape((n_clip, EXTRA, LANES), BF16)
-    weights, first, loss = call(
-        functools.partial(logits_kernel, 2.0 / math.sqrt(width), step),
-        (shape((count, count), BF16), blocks, shape((8, LANES), F32)),
-        [VMEM] * 5,
+    weights, low_grad, high_grad, loss = call(
+        functools.partial(logits_kernel, 2.0 / math.sqrt(width)),
+        (shape((count, count), BF16), half_blocks, half_blocks, shape((8, LANES), F32)),
+        [SMEM] + [VMEM] * 7,
         flops=2 * flops,
         moved=8 * width * count,
-    )(own, own_t, got, side, side_t)
-    first_got = lax.ppermute(first, both, scatter_pass)
-    second, loss_sent = call(
-        functools.partial(second_kernel, step),
-        (blocks, loss_blocks),
-        [VMEM] * 3,
-        flops=flops,
-        moved=8 * width * count,
-    )(got, weights, loss)
+    )(core, robot_bias[None, :], positive_ids, robot_ids, own, own_t, low, high)
+    low_got = lax.ppermute(low_grad, both, scatter_pass[0])
+    high_got = lax.ppermute(high_grad, both, scatter_pass[1])
+    second, loss_sent = call(second_kernel, (blocks, loss_blocks), [VMEM] * 4, flops=flops, moved=8 * width * count)(
+        low, high, weights, loss
+    )
     loss_got = exchange(loss_sent, axis_index_groups=actions_first)
-    ready = call(add_kernel, shape((n_clip, parts * rows + EXTRA, LANES), BF16), [VMEM] * 3)(
-        second, first_got, loss_got
+    ready = call(add_kernel, shape((n_clip, parts * rows + EXTRA, LANES), BF16), [VMEM] * 4)(
+        second, low_got, high_got, loss_got
     )
     scattered = exchange(ready, axis_index_groups=clips_first)
 

time: 107 us -> 107 us (level)
  starting transfers between devices: 28.8 us -> 32.1 us
  waiting for transfers between devices: 12.2 us -> 10.1 us
  blocking collectives: 57.1 us -> 55.3 us
    ppermute x3 -> x4, starting transfers between devices: 15.1 us -> 18.4 us  [the longest x1 10.9 us: shards(): low = lax.ppermute(low, both, gather_pass[0])]
    ppermute x3 -> x4, waiting for transfers between devices: 10.5 us -> 8.32 us  [the longest x1 4.86 us: shards(): low = lax.ppermute(low, both, gather_pass[0])]
    all_to_all x1, blocking collectives: 13.9 us -> 12.3 us  [shards(): loss_got = exchange(loss_sent, axis_index_groups=actions_first)]
  transfers between devices with their start and end apart: 5 -> 6, of which waited for: 3 -> 4; matrix products, arithmetic and copies ran while one was open for 0% -> 0% of each run, Pallas kernels for 2% -> 1%
where the time goes in v7:
time: 107 us; the launch traced here: 106 us
  blocking collectives  55.3 us (52%)
  starting transfers between devices  32.1 us (30%)
  waiting for transfers between devices  10.1 us (9%)
  Pallas kernels  7.01 us (7%)
    all_to_all x1, blocking collectives, shards(): scattered = exchange(ready, axis_index_groups=clips_first)  24.2 us
    all_to_all x1, blocking collectives, shards(): own = exchange(chunks, axis_index_groups=clips_first).reshape(width, count)  18.8 us
    all_to_all x1, blocking collectives, shards(): loss_got = exchange(loss_sent, axis_index_groups=actions_first)  12.3 us
    ppermute x1, starting transfers between devices, shards(): low = lax.ppermute(low, both, gather_pass[0])  10.9 us
    ppermute x1, starting transfers between devices, shards(): other = lax.ppermute(send, 'act', swap)  8.79 us
    ppermute x1, starting transfers between devices, shards(): taken = lax.ppermute(give, 'act', swap)  4.94 us
    ppermute x1, waiting for transfers between devices, shards(): low = lax.ppermute(low, both, gather_pass[0])  4.86 us
    ppermute x1, starting transfers between devices, shards(): high_got = lax.ppermute(high_grad, both, scatter_pass[1])  3.59 us
  transfers between devices with their start and end apart: 6, of which 4 were waited for; matrix products, arithmetic and copies ran while one was open for 0% of the time, Pallas kernels for 1%

profile of v7, /device:TPU:1, one launch (start us, length us, event | category | flops | bytes accessed | tf_op | source)
XLA Modules:
  0.0 106.3 jit_solution(16544588956414567105)
XLA Ops:
  0.6 0.9 fusion.1
  1.6 8.8 %collective-permute-start = (bf16[64,512]{1,0:T(8,128)(2,1)S(1)}, bf16[64,512]{1,0:T(8,128)(2,1)S(1)}, u32[]{:S(2)}, u32[]{:S(2)}) collective-permute-start(bf16[64,512]{1,0:T(8,128)(2,1)S(1)} %get-tuple-element.29), channel_id=1, source_target_pairs={{0,1},{1,0},{2,3},{3,2},{4,5},{5,4},{6,7},{7,6},{8,9},{9,8},{10,11... | collective-permute-start | bytes 196616 | tf_op jit(solution)/shard_map/ppermute | solution.py:238
  10.4 0.1 pad_add_fusion.core_ref
  10.5 0.8 collective-permute-done.other_ref
  11.2 0.6 shard_map.76
  11.9 18.8 %all_to_all.15 = bf16[16,64,512]{2,1,0:T(8,128)(2,1)S(1)} all-to-all(bf16[16,64,512]{2,1,0:T(8,128)(2,1)S(1)} %shard_map.76), channel_id=1, replica_groups={{0,2,4,6,8,10,12,14,16,18,20,22,24,26,28,30},{32,34,36,38,40,42,44,46,4..., dimensions={0} | all-to-all | bytes 2097152 | tf_op jit(solution)/shard_map/all_to_all | solution.py:241
  30.7 0.1 shard_map.77
  30.8 0.0 copy-start.2
  30.8 10.9 %collective-permute-start.1 = (bf16[1040,256]{1,0:T(8,128)(2,1)S(1)}, bf16[1040,256]{1,0:T(8,128)(2,1)S(1)}, u32[]{:S(2)}, u32[]{:S(2)}) collective-permute-start(bf16[1040,256]{1,0:T(8,128)(2,1)S(1)} %get-tuple-element.16), channel_id=1, source_target_pairs={{0,257},{2,259},{4,261},{6,263},{8,265},{10,267},{12,269},{14,271}... | collective-permute-start | bytes 1597448 | tf_op jit(solution)/shard_map/ppermute | solution.py:244
  41.7 1.9 %collective-permute-start.2 = (bf16[1040,256]{1,0:T(8,128)(2,1)S(1)}, bf16[1040,256]{1,0:T(8,128)(2,1)S(1)}, u32[]{:S(2)}, u32[]{:S(2)}) collective-permute-start(bf16[1040,256]{1,0:T(8,128)(2,1)S(1)} %get-tuple-element.17), channel_id=1, source_target_pairs={{0,33},{2,35},{4,37},{6,39},{8,41},{10,43},{12,45},{14,47},{16,49}... | collective-permute-start | bytes 1597448 | tf_op jit(solution)/shard_map/ppermute | solution.py:245
  43.7 0.3 shard_map.78.own_t_ref
  44.0 4.9 %collective-permute-done.1.low_ref = bf16[1040,256]{1,0:T(8,128)(2,1)S(1)} collective-permute-done((bf16[1040,256]{1,0:T(8,128)(2,1)S(1)}, bf16[1040,256]{1,0:T(8,128)(2,1)S(1)}, u32[]{:S(2)}, u32[]{:S(2)}) %collective-permute-start.1) | collective-permute-done | bytes 532512 | tf_op jit(solution)/shard_map/ppermute | solution.py:244
  48.9 3.5 %collective-permute-done.2.high_ref = bf16[1040,256]{1,0:T(8,128)(2,1)S(1)} collective-permute-done((bf16[1040,256]{1,0:T(8,128)(2,1)S(1)}, bf16[1040,256]{1,0:T(8,128)(2,1)S(1)}, u32[]{:S(2)}, u32[]{:S(2)}) %collective-permute-start.2) | collective-permute-done | bytes 532512 | tf_op jit(solution)/shard_map/ppermute | solution.py:245
  52.3 3.0 %shard_map.79 = (bf16[512,512]{1,0:T(8,128)(2,1)S(1)}, bf16[16,128,128]{2,1,0:T(8,128)(2,1)S(1)}, bf16[16,128,128]{2,1,0:T(8,128)(2,1)S(1)}, f32[8,128]{1,0:T(8,128)S(1)}) custom-call(s32[3]{0:T(128)S(1)} %pad_add_fusion.core_ref, f32[1,16]{1,0:T(1,128)S(1)} %bitcast.22, s32[1,512]{1,0:T(1,128)S(1)} %bitcast.19, s32[1,512]{1,0:T(1,128)S(1)} %bitcast.21, ...), custom_call_target="tpu_custom_call" | custom-call | flops 1073741824 | bytes 4194304 | tf_op jit(solution)/shard_map/pallas_call | solution.py:252
  55.3 1.9 %collective-permute-start.3 = (bf16[16,128,128]{2,1,0:T(8,128)(2,1)S(1)}, bf16[16,128,128]{2,1,0:T(8,128)(2,1)S(1)}, u32[]{:S(2)}, u32[]{:S(2)}) collective-permute-start(bf16[16,128,128]{2,1,0:T(8,128)(2,1)S(1)} %get-tuple-element.21), channel_id=1, source_target_pairs={{0,1},{2,3},{4,5},{6,7},{8,9},{10,11},{12,13},{14,15},{16,17},{18,... | collective-permute-start | bytes 1572872 | tf_op jit(solution)/shard_map/ppermute | solution.py:259
  57.2 3.6 %collective-permute-start.4 = (bf16[16,128,128]{2,1,0:T(8,128)(2,1)S(1)}, bf16[16,128,128]{2,1,0:T(8,128)(2,1)S(1)}, u32[]{:S(2)}, u32[]{:S(2)}) collective-permute-start(bf16[16,128,128]{2,1,0:T(8,128)(2,1)S(1)} %get-tuple-element.22), channel_id=1, source_target_pairs={{0,1},{2,3},{4,5},{6,7},{8,9},{10,11},{12,13},{14,15},{16,17},{18,... | collective-permute-start | bytes 1572872 | tf_op jit(solution)/shard_map/ppermute | solution.py:260
  60.8 0.7 shard_map.80
  61.6 12.3 %all_to_all.16.loss_ref = bf16[16,16,128]{2,1,0:T(8,128)(2,1)S(1)} all-to-all(bf16[16,16,128]{2,1,0:T(8,128)(2,1)S(1)} %get-tuple-element.23), channel_id=1, replica_groups={{0,32,64,96,128,160,192,224,256,288,320,352,384,416,448,480},{2,34,66,9..., dimensions={0} | all-to-all | bytes 131072 | tf_op jit(solution)/shard_map/all_to_all | solution.py:264
  73.9 0.2 shard_map.81
  74.2 24.2 %all_to_all.17.got_ref = bf16[16,272,128]{2,1,0:T(8,128)(2,1)S(1)} all-to-all(bf16[16,272,128]{2,1,0:T(8,128)(2,1)S(1)} %shard_map.81), channel_id=1, replica_groups={{0,2,4,6,8,10,12,14,16,18,20,22,24,26,28,30},{32,34,36,38,40,42,44,46,4..., dimensions={0} | all-to-all | bytes 2228224 | tf_op jit(solution)/shard_map/all_to_all | solution.py:268
  98.4 0.8 shard_map.82
  99.2 4.9 %collective-permute-start.5 = (f32[72,512]{1,0:T(8,128)S(1)}, f32[72,512]{1,0:T(8,128)S(1)}, u32[]{:S(2)}, u32[]{:S(2)}) collective-permute-start(f32[72,512]{1,0:T(8,128)S(1)} %get-tuple-element.25.give_ref), channel_id=1, source_target_pairs={{0,1},{1,0},{2,3},{3,2},{4,5},{5,4},{6,7},{7,6},{8,9},{9,8},{10,11... | collective-permute-start | bytes 442376 | tf_op jit(solution)/shard_map/ppermute | solution.py:277
  104.1 1.0 collective-permute-done.5.taken_ref
  105.1 1.2 %shard_map.83 = (f32[32,512]{1,0:T(8,128)}, f32[64,512]{1,0:T(8,128)}, f32[1,1]{1,0:T(1,128)}) custom-call(s32[3]{0:T(128)S(1)} %pad_add_fusion.core_ref, f32[64,512]{1,0:T(8,128)S(1)} %get-tuple-element.24.keep_ref, f32[72,512]{1,0:T(8,128)S(1)} %get-tuple-element.25.give_ref, f32[72,512]{1,0:T(8,128)S(1)} %collective-permute-done.5.taken_ref), custom_call_target="tpu_custom_call" | custom-call | tf_op jit(solution)/shard_map/pallas_call | solution.py:278
  (7 shorter events, 0.0 us)
Async XLA Ops:
  1.6 9.7 %collective-permute-start = (bf16[64,512]{1,0:T(8,128)(2,1)S(1)}, bf16[64,512]{1,0:T(8,128)(2,1)S(1)}, u32[]{:S(2)}, u32[]{:S(2)}) collective-permute-start(bf16[64,512]{1,0:T(8,128)(2,1)S(1)} %get-tuple-element.29), channel_id=1, source_target_pairs={{0,1},{1,0},{2,3},{3,2},{4,5},{5,4},{6,7},{7,6},{8,9},{9,8},{10,11... | collective-permute-start | bytes 196616 | tf_op jit(solution)/shard_map/ppermute | solution.py:238
  11.9 18.8 %copy-start = (s32[512]{0:T(512)S(1)}, s32[512]{0:T(512)}, u32[]{:S(2)}) copy-start(s32[512]{0:T(512)} %param.7) | copy-start | bytes 6148
  11.9 18.8 %copy-start.1 = (s32[512]{0:T(512)S(1)}, s32[512]{0:T(512)}, u32[]{:S(2)}) copy-start(s32[512]{0:T(512)} %param.8) | copy-start | bytes 6148
  30.8 21.5 %copy-start.2 = (f32[16]{0:T(128)S(1)}, f32[16]{0:T(128)}, u32[]{:S(2)}) copy-start(f32[16]{0:T(128)} %param.9) | copy-start | bytes 196
  30.8 18.1 %collective-permute-start.1 = (bf16[1040,256]{1,0:T(8,128)(2,1)S(1)}, bf16[1040,256]{1,0:T(8,128)(2,1)S(1)}, u32[]{:S(2)}, u32[]{:S(2)}) collective-permute-start(bf16[1040,256]{1,0:T(8,128)(2,1)S(1)} %get-tuple-element.16), channel_id=1, source_target_pairs={{0,257},{2,259},{4,261},{6,263},{8,265},{10,267},{12,269},{14,271}... | collective-permute-start | bytes 1597448 | tf_op jit(solution)/shard_map/ppermute | solution.py:244
  41.7 10.6 %collective-permute-start.2 = (bf16[1040,256]{1,0:T(8,128)(2,1)S(1)}, bf16[1040,256]{1,0:T(8,128)(2,1)S(1)}, u32[]{:S(2)}, u32[]{:S(2)}) collective-permute-start(bf16[1040,256]{1,0:T(8,128)(2,1)S(1)} %get-tuple-element.17), channel_id=1, source_target_pairs={{0,33},{2,35},{4,37},{6,39},{8,41},{10,43},{12,45},{14,47},{16,49}... | collective-permute-start | bytes 1597448 | tf_op jit(solution)/shard_map/ppermute | solution.py:245
  55.3 18.6 %collective-permute-start.3 = (bf16[16,128,128]{2,1,0:T(8,128)(2,1)S(1)}, bf16[16,128,128]{2,1,0:T(8,128)(2,1)S(1)}, u32[]{:S(2)}, u32[]{:S(2)}) collective-permute-start(bf16[16,128,128]{2,1,0:T(8,128)(2,1)S(1)} %get-tuple-element.21), channel_id=1, source_target_pairs={{0,1},{2,3},{4,5},{6,7},{8,9},{10,11},{12,13},{14,15},{16,17},{18,... | collective-permute-start | bytes 1572872 | tf_op jit(solution)/shard_map/ppermute | solution.py:259
  57.2 16.7 %collective-permute-start.4 = (bf16[16,128,128]{2,1,0:T(8,128)(2,1)S(1)}, bf16[16,128,128]{2,1,0:T(8,128)(2,1)S(1)}, u32[]{:S(2)}, u32[]{:S(2)}) collective-permute-start(bf16[16,128,128]{2,1,0:T(8,128)(2,1)S(1)} %get-tuple-element.22), channel_id=1, source_target_pairs={{0,1},{2,3},{4,5},{6,7},{8,9},{10,11},{12,13},{14,15},{16,17},{18,... | collective-permute-start | bytes 1572872 | tf_op jit(solution)/shard_map/ppermute | solution.py:260
  99.2 5.9 %collective-permute-start.5 = (f32[72,512]{1,0:T(8,128)S(1)}, f32[72,512]{1,0:T(8,128)S(1)}, u32[]{:S(2)}, u32[]{:S(2)}) collective-permute-start(f32[72,512]{1,0:T(8,128)S(1)} %get-tuple-element.25.give_ref), channel_id=1, source_target_pairs={{0,1},{1,0},{2,3},{3,2},{4,5},{5,4},{6,7},{7,6},{8,9},{9,8},{10,11... | collective-permute-start | bytes 442376 | tf_op jit(solution)/shard_map/ppermute | solution.py:277

commit v8 on v7

--- a/solution.py
+++ b/solution.py
@@ -58,91 +58,99 @@
 
 def split_kernel(own_ref, positive_ref, robot_ref, low_ref, high_ref):
     width = own_ref.shape[0]
+    half = low_ref.shape[1]
     positive = positive_ref[...]
-    rows = [positive // LANES, positive % LANES, robot_ref[...]]
-    rows = jnp.concatenate(rows + [jnp.zeros_like(positive)] * (EXTRA - len(rows)), axis=0)
-    rows = rows.astype(F32).astype(BF16)
-    half = low_ref.shape[1]
-    low_ref[:width, :] = own_ref[:, :half]
-    low_ref[width:, :] = rows[:, :half]
-    high_ref[:width, :] = own_ref[:, half:]
-    high_ref[width:, :] = rows[:, half:]
+    robots = [robot_ref[:, :half], robot_ref[:, half:]]
+    padding = [jnp.zeros_like(robots[0])] * (EXTRA - 4)
+    for out_ref, start in ((low_ref, 0), (high_ref, half)):
+        part = positive[:, start : start + half]
+        rows = jnp.concatenate([part // LANES, part % LANES] + robots + padding, axis=0)
+        out_ref[:width, :] = own_ref[:, start : start + half]
+        out_ref[width:, :] = rows.astype(F32).astype(BF16)
 
 
 def transpose_kernel(own_ref, own_t_ref):
     own_t_ref[...] = own_ref[...].T
 
 
-def sides(core_ref, bias_ref, positive_ref, robot_ref, got_rows):
+def sides(start, core_ref, bias_ref, positive_ref, robot_ref, got_rows):
     count = robot_ref.shape[1]
+    step = got_rows.shape[1]
+    part = slice(start, start + step)
     first = core_ref[0] == 0
-    robot = jnp.where(core_ref[0] == core_ref[2], robot_ref[...].astype(F32), got_rows[2:3, :])
+    arrived = jnp.concatenate([got_rows[2:3, :], got_rows[3:4, :]], axis=1)
+    robot = jnp.where(core_ref[0] == core_ref[2], robot_ref[...].astype(F32), arrived)
     bias = jnp.zeros((1, count), F32)
     for index in range(bias_ref.shape[1]):
         bias = jnp.where(robot == index, bias_ref[:, index : index + 1], bias)
     zero = jnp.zeros((1, count), F32)
-    positive = jnp.where(first, positive_ref[...].astype(F32), got_rows[0:1, :] * LANES + got_rows[1:2, :])
     action = (lax.broadcasted_iota(jnp.int32, (1, count), 1) + core_ref[1] * count).astype(F32)
-    rows = [jnp.where(first, zero, bias), jnp.where(first, positive, action)]
-    columns = [jnp.where(first, bias, zero), jnp.where(first, action, positive)]
+    rows = [jnp.where(first, zero, bias), jnp.where(first, positive_ref[...].astype(F32), action)]
     rows = jnp.concatenate(rows + [zero] * 6, axis=0).T
-    return rows[:, 0:1], rows[:, 1:2], columns[0], columns[1]
-
-
-def logits_kernel(scale, core_ref, bias_ref, positive_ref, robot_ref, own_ref, own_t_ref, low_ref, high_ref,
-                  weights_ref, low_grad_ref, high_grad_ref, loss_ref):
+    column_bias = jnp.where(first, bias, zero)[:, part]
+    column_key = jnp.where(first, action[:, part], got_rows[0:1, :] * LANES + got_rows[1:2, :])
+    return rows[:, 0:1], rows[:, 1:2], column_bias, column_key
+
+
+def logits_kernel(scale, start, core_ref, bias_ref, positive_ref, robot_ref, own_ref, own_t_ref, got_ref, before_ref,
+                  weights_ref, grad_ref, loss_ref):
     width = own_ref.shape[0]
-    step = low_ref.shape[1]
-    got_rows = jnp.concatenate([low_ref[width:, :], high_ref[width:, :]], axis=1).astype(F32)
-    row_bias, row_key, column_bias, column_key = sides(core_ref, bias_ref, positive_ref, robot_ref, got_rows)
-    own = own_ref[...]
-    own_t = own_t_ref[...]
-    total = jnp.zeros((1, 1), F32)
-    for start, got_ref, grad_ref in ((0, low_ref, low_grad_ref), (step, high_ref, high_grad_ref)):
-        logits = jnp.dot(own_t, got_ref[:width, :], preferred_element_type=F32) * scale
-        logits = logits + (row_bias + column_bias[:, start : start + step])
-        positive = row_key == column_key[:, start : start + step]
-        margin = jnp.where(positive, -logits, logits)
-        small = jnp.exp(-jnp.abs(margin))
-        above = 1.0 + small
-        inverse = 1.0 / above
-        log = jnp.log(above) + (small - (above - 1.0)) * inverse
-        total = total + jnp.sum(jnp.maximum(margin, 0.0) + log, keepdims=True)
-        sigmoid = jnp.where(margin >= 0.0, inverse, small * inverse)
-        weights = jnp.where(positive, -sigmoid, sigmoid).astype(BF16)
-        weights_ref[:, start : start + step] = weights
-        store_blocks(grad_ref, jnp.dot(own, weights, preferred_element_type=F32), 0)
-    loss_ref[...] = jnp.broadcast_to(total, loss_ref.shape)
-
-
-def second_kernel(low_ref, high_ref, weights_ref, loss_ref, grad_ref, rows_ref):
-    rows_ref[...] = loss_rows(jnp.broadcast_to(loss_ref[0:1, :], rows_ref.shape), rows_ref.shape)
+    got_rows = got_ref[width:, :].astype(F32)
+    row_bias, row_key, column_bias, column_key = sides(start, core_ref, bias_ref, positive_ref, robot_ref, got_rows)
+    logits = jnp.dot(own_t_ref[...], got_ref[:width, :], preferred_element_type=F32) * scale
+    logits = logits + (row_bias + column_bias)
+    positive = row_key == column_key
+    margin = jnp.where(positive, -logits, logits)
+    small = jnp.exp(-jnp.abs(margin))
+    above = 1.0 + small
+    inverse = 1.0 / above
+    log = jnp.log(above) + (small - (above - 1.0)) * inverse
+    sigmoid = jnp.where(margin >= 0.0, inverse, small * inverse)
+    weights = jnp.where(positive, -sigmoid, sigmoid).astype(BF16)
+    weights_ref[...] = weights
+    store_blocks(grad_ref, jnp.dot(own_ref[...], weights, preferred_element_type=F32), 0)
+    total = jnp.sum(jnp.maximum(margin, 0.0) + log, keepdims=True)
+    if before_ref is None:
+        loss_ref[...] = jnp.broadcast_to(total, loss_ref.shape)
+    else:
+        total = jnp.broadcast_to((total + before_ref[0:1, 0:1])[None], loss_ref.shape)
+        loss_ref[...] = loss_rows(total, loss_ref.shape)
+
+
+def low_kernel(scale, *refs):
+    logits_kernel(scale, 0, *refs[:7], None, *refs[7:])
+
+
+def high_kernel(scale, *refs):
+    logits_kernel(scale, refs[6].shape[1], *refs)
+
+
+def received_loss(rows):
+    return rows[0:1] + rows[4:5] + rows[8:9]
+
+
+def second_kernel(low_ref, high_ref, low_weights_ref, high_weights_ref, low_got_ref, high_got_ref, loss_ref, out_ref):
+    blocks = out_ref.shape[0]
     step = low_ref.shape[1]
     width = low_ref.shape[0] - EXTRA
-    by_columns = (((1,), (1,)), ((), ()))
-    for start in range(0, weights_ref.shape[0], step):
-        weights = weights_ref[start : start + step, :]
-        grad = lax.dot_general(low_ref[:width, :], weights[:, :step], by_columns, preferred_element_type=F32)
-        grad += lax.dot_general(high_ref[:width, :], weights[:, step:], by_columns, preferred_element_type=F32)
-        store_blocks(grad_ref, grad, start)
-
-
-def received_loss(rows):
-    return rows[0:1] + rows[4:5] + rows[8:9]
-
-
-def add_kernel(own_ref, low_ref, high_ref, loss_ref, out_ref):
-    blocks, size, _ = own_ref.shape
-    half = size // 2
+    size = width // blocks
     total = loss_ref[0].astype(F32)
     for block in range(1, blocks):
         total = total + loss_ref[block].astype(F32)
     rows = loss_rows(jnp.broadcast_to(received_loss(total), total.shape), total.shape)
     for block in range(blocks):
-        own = own_ref[block].astype(F32)
-        out_ref[block, :half, :] = (own[:half] + low_ref[block].astype(F32)).astype(BF16)
-        out_ref[block, half:size, :] = (own[half:] + high_ref[block].astype(F32)).astype(BF16)
-        out_ref[block, size:, :] = rows
+        out_ref[block, out_ref.shape[1] - EXTRA :, :] = rows
+    by_columns = (((1,), (1,)), ((), ()))
+    for start, got_ref in ((0, low_got_ref), (step, high_got_ref)):
+        half = slice(start, start + step)
+        grad = lax.dot_general(low_ref[:width, :], low_weights_ref[half, :], by_columns, preferred_element_type=F32)
+        grad += lax.dot_general(high_ref[:width, :], high_weights_ref[half, :], by_columns, preferred_element_type=F32)
+        for part in range(step // LANES):
+            at = slice(part * size, (part + 1) * size)
+            columns = grad[:, part * LANES : (part + 1) * LANES].astype(BF16).reshape(blocks, size, LANES)
+            added = columns.astype(F32) + got_ref[:, at, :].astype(F32)
+            first = (start // LANES + part) * size
+            out_ref[:, first : first + size, :] = added.astype(BF16)
 
 
 def sum_kernel(clip_scale, action_scale, core_ref, got_ref, keep_ref, give_ref):
@@ -246,24 +254,25 @@
     own_t = call(transpose_kernel, shape((count, width), BF16), [VMEM])(own)
 
     flops = 2 * width * count * count
-    blocks = shape((n_clip, parts * rows, LANES), BF16)
     half_blocks = shape((n_clip, parts * rows // 2, LANES), BF16)
-    loss_blocks = shape((n_clip, EXTRA, LANES), BF16)
-    weights, low_grad, high_grad, loss = call(
-        functools.partial(logits_kernel, 2.0 / math.sqrt(width)),
-        (shape((count, count), BF16), half_blocks, half_blocks, shape((8, LANES), F32)),
-        [SMEM] + [VMEM] * 7,
-        flops=2 * flops,
-        moved=8 * width * count,
-    )(core, robot_bias[None, :], positive_ids, robot_ids, own, own_t, low, high)
+    scale = 2.0 / math.sqrt(width)
+    fixed = (core, robot_bias[None, :], positive_ids, robot_ids, own, own_t)
+    def results(loss):
+        return (shape((count, count // 2), BF16), half_blocks, loss)
+
+    cost = {"flops": flops, "moved": 4 * width * count}
+    specs = [SMEM] + [VMEM] * 6
+    low_weights, low_grad, loss = call(
+        functools.partial(low_kernel, scale), results(shape((8, LANES), F32)), specs, **cost
+    )(*fixed, low)
     low_got = lax.ppermute(low_grad, both, scatter_pass[0])
+    high_weights, high_grad, loss_sent = call(
+        functools.partial(high_kernel, scale), results(shape((n_clip, EXTRA, LANES), BF16)), specs + [VMEM], **cost
+    )(*fixed, high, loss)
     high_got = lax.ppermute(high_grad, both, scatter_pass[1])
-    second, loss_sent = call(second_kernel, (blocks, loss_blocks), [VMEM] * 4, flops=flops, moved=8 * width * count)(
-        low, high, weights, loss
-    )
     loss_got = exchange(loss_sent, axis_index_groups=actions_first)
-    ready = call(add_kernel, shape((n_clip, parts * rows + EXTRA, LANES), BF16), [VMEM] * 4)(
-        second, low_got, high_got, loss_got
+    ready = call(second_kernel, shape((n_clip, parts * rows + EXTRA, LANES), BF16), [VMEM] * 7, **cost)(
+        low, high, low_weights, high_weights, low_got, high_got, loss_got
     )
     scattered = exchange(ready, axis_index_groups=clips_first)
 

time: 107 us -> 106 us (level)
  waiting for transfers between devices: 10.1 us -> 7.9 us
  blocking collectives: 55.3 us -> 57.1 us
  starting transfers between devices: 32.1 us -> 30.3 us
  Pallas kernels: 7.01 us -> 8.12 us
    ppermute x1, waiting for transfers between devices: 3.45 us -> 1.28 us  [shards(): high = lax.ppermute(high, both, gather_pass[1])]
    ppermute x1, starting transfers between devices: 3.59 us -> 1.92 us  [shards(): high_got = lax.ppermute(high_grad, both, scatter_pass[1])]
    pallas_call x3, Pallas kernels: 3.96 us -> 5.08 us  [the longest x1 2.16 us: shards(): call(functools.partial(high_kernel, scale), results(shape((n_clip, EXTRA,...]
  transfers between devices with their start and end apart: 6 -> 6, of which waited for: 4 -> 4; matrix products, arithmetic and copies ran while one was open for 0% -> 0% of each run, Pallas kernels for 1% -> 2%
where the time goes in v8:
time: 106 us; the launch traced here: 105 us
  blocking collectives  57.1 us (54%)
  starting transfers between devices  30.3 us (29%)
  Pallas kernels  8.12 us (8%)
  waiting for transfers between devices  7.9 us (7%)
    all_to_all x1, blocking collectives, shards(): scattered = exchange(ready, axis_index_groups=clips_first)  25.1 us
    all_to_all x1, blocking collectives, shards(): own = exchange(chunks, axis_index_groups=clips_first).reshape(width, count)  18.8 us
    all_to_all x1, blocking collectives, shards(): loss_got = exchange(loss_sent, axis_index_groups=actions_first)  13.1 us
    ppermute x1, starting transfers between devices, shards(): low = lax.ppermute(low, both, gather_pass[0])  10.9 us
    ppermute x1, starting transfers between devices, shards(): other = lax.ppermute(send, 'act', swap)  8.79 us
    ppermute x1, waiting for transfers between devices, shards(): low = lax.ppermute(low, both, gather_pass[0])  4.86 us
    ppermute x1, starting transfers between devices, shards(): taken = lax.ppermute(give, 'act', swap)  4.19 us
    ppermute x1, starting transfers between devices, shards(): low_got = lax.ppermute(low_grad, both, scatter_pass[0])  2.6 us
  transfers between devices with their start and end apart: 6, of which 4 were waited for; matrix products, arithmetic and copies ran while one was open for 0% of the time, Pallas kernels for 2%

profile of v8, /device:TPU:1, one launch (start us, length us, event | category | flops | bytes accessed | tf_op | source)
XLA Modules:
  0.0 105.3 jit_solution(17954563045286764174)
XLA Ops:
  0.6 0.9 fusion.1
  1.6 8.8 %collective-permute-start = (bf16[64,512]{1,0:T(8,128)(2,1)S(1)}, bf16[64,512]{1,0:T(8,128)(2,1)S(1)}, u32[]{:S(2)}, u32[]{:S(2)}) collective-permute-start(bf16[64,512]{1,0:T(8,128)(2,1)S(1)} %get-tuple-element.29), channel_id=1, source_target_pairs={{0,1},{1,0},{2,3},{3,2},{4,5},{5,4},{6,7},{7,6},{8,9},{9,8},{10,11... | collective-permute-start | bytes 196616 | tf_op jit(solution)/shard_map/ppermute | solution.py:246
  10.4 0.1 pad_add_fusion.core_ref.refs_0_
  10.5 0.8 collective-permute-done.other_ref
  11.2 0.6 shard_map.76
  11.9 18.8 %all_to_all.15 = bf16[16,64,512]{2,1,0:T(8,128)(2,1)S(1)} all-to-all(bf16[16,64,512]{2,1,0:T(8,128)(2,1)S(1)} %shard_map.76), channel_id=1, replica_groups={{0,2,4,6,8,10,12,14,16,18,20,22,24,26,28,30},{32,34,36,38,40,42,44,46,4..., dimensions={0} | all-to-all | bytes 2097152 | tf_op jit(solution)/shard_map/all_to_all | solution.py:249
  30.7 0.1 shard_map.77
  30.8 0.0 copy-start.2
  30.8 10.9 %collective-permute-start.1 = (bf16[1040,256]{1,0:T(8,128)(2,1)S(1)}, bf16[1040,256]{1,0:T(8,128)(2,1)S(1)}, u32[]{:S(2)}, u32[]{:S(2)}) collective-permute-start(bf16[1040,256]{1,0:T(8,128)(2,1)S(1)} %get-tuple-element.16), channel_id=1, source_target_pairs={{0,257},{2,259},{4,261},{6,263},{8,265},{10,267},{12,269},{14,271}... | collective-permute-start | bytes 1597448 | tf_op jit(solution)/shard_map/ppermute | solution.py:252
  41.7 1.9 %collective-permute-start.2 = (bf16[1040,256]{1,0:T(8,128)(2,1)S(1)}, bf16[1040,256]{1,0:T(8,128)(2,1)S(1)}, u32[]{:S(2)}, u32[]{:S(2)}) collective-permute-start(bf16[1040,256]{1,0:T(8,128)(2,1)S(1)} %get-tuple-element.17), channel_id=1, source_target_pairs={{0,33},{2,35},{4,37},{6,39},{8,41},{10,43},{12,45},{14,47},{16,49}... | collective-permute-start | bytes 1597448 | tf_op jit(solution)/shard_map/ppermute | solution.py:253
  43.7 0.3 shard_map.78.refs_5_
  44.0 4.9 %collective-permute-done.1.refs_6_.low_ref = bf16[1040,256]{1,0:T(8,128)(2,1)S(1)} collective-permute-done((bf16[1040,256]{1,0:T(8,128)(2,1)S(1)}, bf16[1040,256]{1,0:T(8,128)(2,1)S(1)}, u32[]{:S(2)}, u32[]{:S(2)}) %collective-permute-start.1) | collective-permute-done | bytes 532512 | tf_op jit(solution)/shard_map/ppermute | solution.py:252
  48.9 2.2 %shard_map.79 = (bf16[512,256]{1,0:T(8,128)(2,1)S(1)}, bf16[16,128,128]{2,1,0:T(8,128)(2,1)S(1)}, f32[8,128]{1,0:T(8,128)S(1)}) custom-call(s32[3]{0:T(128)S(1)} %pad_add_fusion.core_ref.refs_0_, f32[1,16]{1,0:T(1,128)S(1)} %bitcast.25, s32[1,512]{1,0:T(1,128)S(1)} %bitcast.20, s32[1,512]{1,0:T(1,128)S(1)} %bitcast.23, bf16[1024,512]{1,0:T(8,128)(2,1)S(1)} %bitcast.17, ...), custom_call_target="tpu_custom_call" | custom-call | flops 536870912 | bytes 2097152 | tf_op jit(solution)/shard_map/pallas_call | solution.py:265
  51.0 1.3 %collective-permute-done.2.refs_6_.high_ref = bf16[1040,256]{1,0:T(8,128)(2,1)S(1)} collective-permute-done((bf16[1040,256]{1,0:T(8,128)(2,1)S(1)}, bf16[1040,256]{1,0:T(8,128)(2,1)S(1)}, u32[]{:S(2)}, u32[]{:S(2)}) %collective-permute-start.2) | collective-permute-done | bytes 532512 | tf_op jit(solution)/shard_map/ppermute | solution.py:253
  52.3 2.2 %shard_map.80 = (bf16[512,256]{1,0:T(8,128)(2,1)S(1)}, bf16[16,128,128]{2,1,0:T(8,128)(2,1)S(1)}, bf16[16,16,128]{2,1,0:T(8,128)(2,1)S(1)}) custom-call(s32[3]{0:T(128)S(1)} %pad_add_fusion.core_ref.refs_0_, f32[1,16]{1,0:T(1,128)S(1)} %bitcast.26, s32[1,512]{1,0:T(1,128)S(1)} %bitcast.21, s32[1,512]{1,0:T(1,128)S(1)} %bitcast.24, ...), custom_call_target="tpu_custom_call" | custom-call | flops 536870912 | bytes 2097152 | tf_op jit(solution)/shard_map/pallas_call | solution.py:269
  54.5 1.9 %collective-permute-start.4 = (bf16[16,128,128]{2,1,0:T(8,128)(2,1)S(1)}, bf16[16,128,128]{2,1,0:T(8,128)(2,1)S(1)}, u32[]{:S(2)}, u32[]{:S(2)}) collective-permute-start(bf16[16,128,128]{2,1,0:T(8,128)(2,1)S(1)} %get-tuple-element.22), channel_id=1, source_target_pairs={{0,1},{2,3},{4,5},{6,7},{8,9},{10,11},{12,13},{14,15},{16,17},{18,... | collective-permute-start | bytes 1572872 | tf_op jit(solution)/shard_map/ppermute | solution.py:272
  56.4 2.6 %collective-permute-start.3 = (bf16[16,128,128]{2,1,0:T(8,128)(2,1)S(1)}, bf16[16,128,128]{2,1,0:T(8,128)(2,1)S(1)}, u32[]{:S(2)}, u32[]{:S(2)}) collective-permute-start(bf16[16,128,128]{2,1,0:T(8,128)(2,1)S(1)} %get-tuple-element.21), channel_id=1, source_target_pairs={{0,1},{2,3},{4,5},{6,7},{8,9},{10,11},{12,13},{14,15},{16,17},{18,... | collective-permute-start | bytes 1572872 | tf_op jit(solution)/shard_map/ppermute | solution.py:268
  59.0 13.1 %all_to_all.16.loss_ref = bf16[16,16,128]{2,1,0:T(8,128)(2,1)S(1)} all-to-all(bf16[16,16,128]{2,1,0:T(8,128)(2,1)S(1)} %get-tuple-element.23), channel_id=1, replica_groups={{0,32,64,96,128,160,192,224,256,288,320,352,384,416,448,480},{2,34,66,9..., dimensions={0} | all-to-all | bytes 131072 | tf_op jit(solution)/shard_map/all_to_all | solution.py:273
  72.2 0.8 shard_map.81
  72.9 25.1 %all_to_all.17.got_ref = bf16[16,272,128]{2,1,0:T(8,128)(2,1)S(1)} all-to-all(bf16[16,272,128]{2,1,0:T(8,128)(2,1)S(1)} %shard_map.81), channel_id=1, replica_groups={{0,2,4,6,8,10,12,14,16,18,20,22,24,26,28,30},{32,34,36,38,40,42,44,46,4..., dimensions={0} | all-to-all | bytes 2228224 | tf_op jit(solution)/shard_map/all_to_all | solution.py:277
  98.1 0.8 shard_map.82
  98.9 4.2 %collective-permute-start.5 = (f32[72,512]{1,0:T(8,128)S(1)}, f32[72,512]{1,0:T(8,128)S(1)}, u32[]{:S(2)}, u32[]{:S(2)}) collective-permute-start(f32[72,512]{1,0:T(8,128)S(1)} %get-tuple-element.25.give_ref), channel_id=1, source_target_pairs={{0,1},{1,0},{2,3},{3,2},{4,5},{5,4},{6,7},{7,6},{8,9},{9,8},{10,11... | collective-permute-start | bytes 442376 | tf_op jit(solution)/shard_map/ppermute | solution.py:286
  103.1 1.0 collective-permute-done.5.taken_ref
  104.0 1.2 %shard_map.83 = (f32[32,512]{1,0:T(8,128)}, f32[64,512]{1,0:T(8,128)}, f32[1,1]{1,0:T(1,128)}) custom-call(s32[3]{0:T(128)S(1)} %pad_add_fusion.core_ref.refs_0_, f32[64,512]{1,0:T(8,128)S(1)} %get-tuple-element.24.keep_ref, f32[72,512]{1,0:T(8,128)S(1)} %get-tuple-element.25.give_ref, f32[72,512]{1,0:T(8,128)S(1)} %collective-permute-done.5.taken_ref), custom_call_target="tpu_custom_call" | custom-call | tf_op jit(solution)/shard_map/pallas_call | solution.py:287
  (7 shorter events, 0.0 us)
Async XLA Ops:
  1.6 9.7 %collective-permute-start = (bf16[64,512]{1,0:T(8,128)(2,1)S(1)}, bf16[64,512]{1,0:T(8,128)(2,1)S(1)}, u32[]{:S(2)}, u32[]{:S(2)}) collective-permute-start(bf16[64,512]{1,0:T(8,128)(2,1)S(1)} %get-tuple-element.29), channel_id=1, source_target_pairs={{0,1},{1,0},{2,3},{3,2},{4,5},{5,4},{6,7},{7,6},{8,9},{9,8},{10,11... | collective-permute-start | bytes 196616 | tf_op jit(solution)/shard_map/ppermute | solution.py:246
  11.9 18.8 %copy-start = (s32[512]{0:T(512)S(1)}, s32[512]{0:T(512)}, u32[]{:S(2)}) copy-start(s32[512]{0:T(512)} %param.7) | copy-start | bytes 6148
  11.9 18.8 %copy-start.1 = (s32[512]{0:T(512)S(1)}, s32[512]{0:T(512)}, u32[]{:S(2)}) copy-start(s32[512]{0:T(512)} %param.8) | copy-start | bytes 6148
  30.8 18.1 %copy-start.2 = (f32[16]{0:T(128)S(1)}, f32[16]{0:T(128)}, u32[]{:S(2)}) copy-start(f32[16]{0:T(128)} %param.9) | copy-start | bytes 196
  30.8 18.1 %collective-permute-start.1 = (bf16[1040,256]{1,0:T(8,128)(2,1)S(1)}, bf16[1040,256]{1,0:T(8,128)(2,1)S(1)}, u32[]{:S(2)}, u32[]{:S(2)}) collective-permute-start(bf16[1040,256]{1,0:T(8,128)(2,1)S(1)} %get-tuple-element.16), channel_id=1, source_target_pairs={{0,257},{2,259},{4,261},{6,263},{8,265},{10,267},{12,269},{14,271}... | collective-permute-start | bytes 1597448 | tf_op jit(solution)/shard_map/ppermute | solution.py:252
  41.7 10.6 %collective-permute-start.2 = (bf16[1040,256]{1,0:T(8,128)(2,1)S(1)}, bf16[1040,256]{1,0:T(8,128)(2,1)S(1)}, u32[]{:S(2)}, u32[]{:S(2)}) collective-permute-start(bf16[1040,256]{1,0:T(8,128)(2,1)S(1)} %get-tuple-element.17), channel_id=1, source_target_pairs={{0,33},{2,35},{4,37},{6,39},{8,41},{10,43},{12,45},{14,47},{16,49}... | collective-permute-start | bytes 1597448 | tf_op jit(solution)/shard_map/ppermute | solution.py:253
  54.5 17.7 %collective-permute-start.4 = (bf16[16,128,128]{2,1,0:T(8,128)(2,1)S(1)}, bf16[16,128,128]{2,1,0:T(8,128)(2,1)S(1)}, u32[]{:S(2)}, u32[]{:S(2)}) collective-permute-start(bf16[16,128,128]{2,1,0:T(8,128)(2,1)S(1)} %get-tuple-element.22), channel_id=1, source_target_pairs={{0,1},{2,3},{4,5},{6,7},{8,9},{10,11},{12,13},{14,15},{16,17},{18,... | collective-permute-start | bytes 1572872 | tf_op jit(solution)/shard_map/ppermute | solution.py:272
  56.4 15.8 %collective-permute-start.3 = (bf16[16,128,128]{2,1,0:T(8,128)(2,1)S(1)}, bf16[16,128,128]{2,1,0:T(8,128)(2,1)S(1)}, u32[]{:S(2)}, u32[]{:S(2)}) collective-permute-start(bf16[16,128,128]{2,1,0:T(8,128)(2,1)S(1)} %get-tuple-element.21), channel_id=1, source_target_pairs={{0,1},{2,3},{4,5},{6,7},{8,9},{10,11},{12,13},{14,15},{16,17},{18,... | collective-permute-start | bytes 1572872 | tf_op jit(solution)/shard_map/ppermute | solution.py:268
  98.9 5.2 %collective-permute-start.5 = (f32[72,512]{1,0:T(8,128)S(1)}, f32[72,512]{1,0:T(8,128)S(1)}, u32[]{:S(2)}, u32[]{:S(2)}) collective-permute-start(f32[72,512]{1,0:T(8,128)S(1)} %get-tuple-element.25.give_ref), channel_id=1, source_target_pairs={{0,1},{1,0},{2,3},{3,2},{4,5},{5,4},{6,7},{7,6},{8,9},{9,8},{10,11... | collective-permute-start | bytes 442376 | tf_op jit(solution)/shard_map/ppermute | solution.py:286

commit v9 on v8

--- a/solution.py
+++ b/solution.py
@@ -36,24 +36,6 @@
 
 def block_of(index, blocks):
     return (index // (blocks // 2) + index) % 2
-
-
-def chunk_kernel(core_ref, mine_ref, other_ref, out_ref):
-    blocks = out_ref.shape[0]
-    half = mine_ref.shape[0] // 2
-    mine = mine_ref[...]
-    other = other_ref[...]
-
-    @pl.when(core_ref[0] == 0)
-    def _():
-        pair = jnp.concatenate([mine[:half], other[:half]], axis=0)
-        for block in range(blocks):
-            out_ref[block] = pair
-
-    @pl.when(core_ref[0] != 0)
-    def _():
-        for block in range(blocks):
-            out_ref[block] = mine if block_of(block, blocks) else other
 
 
 def split_kernel(own_ref, positive_ref, robot_ref, low_ref, high_ref):
@@ -97,19 +79,23 @@
     width = own_ref.shape[0]
     got_rows = got_ref[width:, :].astype(F32)
     row_bias, row_key, column_bias, column_key = sides(start, core_ref, bias_ref, positive_ref, robot_ref, got_rows)
-    logits = jnp.dot(own_t_ref[...], got_ref[:width, :], preferred_element_type=F32) * scale
-    logits = logits + (row_bias + column_bias)
-    positive = row_key == column_key
-    margin = jnp.where(positive, -logits, logits)
-    small = jnp.exp(-jnp.abs(margin))
-    above = 1.0 + small
-    inverse = 1.0 / above
-    log = jnp.log(above) + (small - (above - 1.0)) * inverse
-    sigmoid = jnp.where(margin >= 0.0, inverse, small * inverse)
-    weights = jnp.where(positive, -sigmoid, sigmoid).astype(BF16)
-    weights_ref[...] = weights
-    store_blocks(grad_ref, jnp.dot(own_ref[...], weights, preferred_element_type=F32), 0)
-    total = jnp.sum(jnp.maximum(margin, 0.0) + log, keepdims=True)
+    got = got_ref[:width, :]
+    total = jnp.zeros((1, got.shape[1]), F32)
+    for row in range(0, own_t_ref.shape[0], LANES):
+        part = slice(row, row + LANES)
+        logits = jnp.dot(own_t_ref[part, :], got, preferred_element_type=F32) * scale
+        logits = logits + (row_bias[part] + column_bias)
+        positive = row_key[part] == column_key
+        margin = jnp.where(positive, -logits, logits)
+        small = jnp.exp(-jnp.abs(margin))
+        above = 1.0 + small
+        inverse = 1.0 / above
+        log = jnp.log(above) + (small - (above - 1.0)) * inverse
+        sigmoid = jnp.where(margin >= 0.0, inverse, small * inverse)
+        weights_ref[part, :] = jnp.where(positive, -sigmoid, sigmoid).astype(BF16)
+        total = total + jnp.sum(jnp.maximum(margin, 0.0) + log, axis=0, keepdims=True)
+    store_blocks(grad_ref, jnp.dot(own_ref[...], weights_ref[...], preferred_element_type=F32), 0)
+    total = jnp.sum(total, keepdims=True)
     if before_ref is None:
         loss_ref[...] = jnp.broadcast_to(total, loss_ref.shape)
     else:
@@ -129,28 +115,37 @@
     return rows[0:1] + rows[4:5] + rows[8:9]
 
 
-def second_kernel(low_ref, high_ref, low_weights_ref, high_weights_ref, low_got_ref, high_got_ref, loss_ref, out_ref):
-    blocks = out_ref.shape[0]
+def add_second(start, low_ref, high_ref, low_weights_ref, high_weights_ref, got_ref, out_ref):
+    blocks, got_size, _ = got_ref.shape
     step = low_ref.shape[1]
     width = low_ref.shape[0] - EXTRA
     size = width // blocks
+    by_columns = (((1,), (1,)), ((), ()))
+    half = slice(start, start + step)
+    grad = lax.dot_general(low_ref[:width, :], low_weights_ref[half, :], by_columns, preferred_element_type=F32)
+    grad += lax.dot_general(high_ref[:width, :], high_weights_ref[half, :], by_columns, preferred_element_type=F32)
+    first = start // step * got_size
+    for part in range(step // LANES):
+        at = slice(part * size, (part + 1) * size)
+        columns = grad[:, part * LANES : (part + 1) * LANES].astype(BF16).reshape(blocks, size, LANES)
+        added = columns.astype(F32) + got_ref[:, at, :].astype(F32)
+        out_ref[:, first + part * size : first + (part + 1) * size, :] = added.astype(BF16)
+
+
+def second_kernel(low_ref, high_ref, low_weights_ref, high_weights_ref, got_ref, loss_ref, out_ref, rows_ref):
+    add_second(0, low_ref, high_ref, low_weights_ref, high_weights_ref, got_ref, out_ref)
     total = loss_ref[0].astype(F32)
-    for block in range(1, blocks):
+    for block in range(1, loss_ref.shape[0]):
         total = total + loss_ref[block].astype(F32)
-    rows = loss_rows(jnp.broadcast_to(received_loss(total), total.shape), total.shape)
+    rows_ref[...] = loss_rows(jnp.broadcast_to(received_loss(total), total.shape), total.shape)
+
+
+def third_kernel(low_ref, high_ref, low_weights_ref, high_weights_ref, got_ref, before_ref, rows_ref, out_ref):
+    blocks, before, _ = before_ref.shape
     for block in range(blocks):
-        out_ref[block, out_ref.shape[1] - EXTRA :, :] = rows
-    by_columns = (((1,), (1,)), ((), ()))
-    for start, got_ref in ((0, low_got_ref), (step, high_got_ref)):
-        half = slice(start, start + step)
-        grad = lax.dot_general(low_ref[:width, :], low_weights_ref[half, :], by_columns, preferred_element_type=F32)
-        grad += lax.dot_general(high_ref[:width, :], high_weights_ref[half, :], by_columns, preferred_element_type=F32)
-        for part in range(step // LANES):
-            at = slice(part * size, (part + 1) * size)
-            columns = grad[:, part * LANES : (part + 1) * LANES].astype(BF16).reshape(blocks, size, LANES)
-            added = columns.astype(F32) + got_ref[:, at, :].astype(F32)
-            first = (start // LANES + part) * size
-            out_ref[:, first : first + size, :] = added.astype(BF16)
+        out_ref[block, :before, :] = before_ref[block]
+        out_ref[block, out_ref.shape[1] - EXTRA :, :] = rows_ref[...]
+    add_second(low_ref.shape[1], low_ref, high_ref, low_weights_ref, high_weights_ref, got_ref, out_ref)
 
 
 def sum_kernel(clip_scale, action_scale, core_ref, got_ref, keep_ref, give_ref):
@@ -244,7 +239,9 @@
     send = jnp.where(first_core, actions, clip_twice).astype(BF16)
     mine = jnp.where(first_core, clip_twice, actions).astype(BF16)
     other = lax.ppermute(send, "act", swap)
-    chunks = call(chunk_kernel, shape((n_clip, rows, count), BF16), [SMEM, VMEM, VMEM])(core, mine, other)
+    pair = jnp.concatenate([mine[:half], other[:half]], axis=0)
+    takes_mine = block_of(jnp.arange(n_clip), n_clip)[:, None, None] == 1
+    chunks = jnp.where(first_core, pair[None], jnp.where(takes_mine, mine[None], other[None]))
     positive_ids, robot_ids = positive_ids[None, :], robot_ids[None, :]
     own = exchange(chunks, axis_index_groups=clips_first).reshape(width, count)
     halves = shape((width + EXTRA, count // 2), BF16)
@@ -271,8 +268,12 @@
     )(*fixed, high, loss)
     high_got = lax.ppermute(high_grad, both, scatter_pass[1])
     loss_got = exchange(loss_sent, axis_index_groups=actions_first)
-    ready = call(second_kernel, shape((n_clip, parts * rows + EXTRA, LANES), BF16), [VMEM] * 7, **cost)(
-        low, high, low_weights, high_weights, low_got, high_got, loss_got
+    operands = (low, high, low_weights, high_weights)
+    begun, loss_sum = call(second_kernel, (half_blocks, shape((EXTRA, LANES), BF16)), [VMEM] * 6, **cost)(
+        *operands, low_got, loss_got
+    )
+    ready = call(third_kernel, shape((n_clip, parts * rows + EXTRA, LANES), BF16), [VMEM] * 7, **cost)(
+        *operands, high_got, begun, loss_sum
     )
     scattered = exchange(ready, axis_index_groups=clips_first)
 

time: 106 us -> 104 us (0.981)
  waiting for transfers between devices: 7.9 us -> 6.6 us
  starting transfers between devices: 30.3 us -> 31.5 us
  Pallas kernels: 8.12 us -> 7 us
    ppermute x1, starting transfers between devices: 1.92 us -> 3.58 us  [shards(): high_got = lax.ppermute(high_grad, both, scatter_pass[1])]
    all_to_all x1, blocking collectives: 25.1 us -> 23.7 us  [shards(): scattered = exchange(ready, axis_index_groups=clips_first)]
    ppermute x1, waiting for transfers between devices: 1.28 us -> 0.01 us  [shards(): high = lax.ppermute(high, both, gather_pass[1])]
  transfers between devices with their start and end apart: 6 -> 6, of which waited for: 4 -> 3; matrix products, arithmetic and copies ran while one was open for 0% -> 0% of each run, Pallas kernels for 2% -> 4%
where the time goes in v9:
time: 104 us; the launch traced here: 103 us
  blocking collectives  56.2 us (54%)
  starting transfers between devices  31.5 us (30%)
  Pallas kernels  7 us (7%)
  waiting for transfers between devices  6.6 us (6%)
  other arithmetic  1.18 us (1%)
    all_to_all x1, blocking collectives, shards(): scattered = exchange(ready, axis_index_groups=clips_first)  23.7 us
    all_to_all x1, blocking collectives, shards(): own = exchange(chunks, axis_index_groups=clips_first).reshape(width, count)  18.8 us
    all_to_all x1, blocking collectives, shards(): loss_got = exchange(loss_sent, axis_index_groups=actions_first)  13.6 us
    ppermute x1, starting transfers between devices, shards(): low = lax.ppermute(low, both, gather_pass[0])  10.9 us
    ppermute x1, starting transfers between devices, shards(): other = lax.ppermute(send, 'act', swap)  8.79 us
    ppermute x1, waiting for transfers between devices, shards(): low = lax.ppermute(low, both, gather_pass[0])  4.75 us
    ppermute x1, starting transfers between devices, shards(): taken = lax.ppermute(give, 'act', swap)  4.34 us
    ppermute x1, starting transfers between devices, shards(): high_got = lax.ppermute(high_grad, both, scatter_pass[1])  3.58 us
  transfers between devices with their start and end apart: 6, of which 3 were waited for; matrix products, arithmetic and copies ran while one was open for 0% of the time, Pallas kernels for 4%

profile of v9, /device:TPU:1, one launch (start us, length us, event | category | flops | bytes accessed | tf_op | source)
XLA Modules:
  0.0 103.3 jit_solution(15560359558422640813)
XLA Ops:
  0.6 0.9 fusion
  1.6 8.8 %collective-permute-start = (bf16[64,512]{1,0:T(8,128)(2,1)S(1)}, bf16[64,512]{1,0:T(8,128)(2,1)S(1)}, u32[]{:S(2)}, u32[]{:S(2)}) collective-permute-start(bf16[64,512]{1,0:T(8,128)(2,1)S(1)} %get-tuple-element.34), channel_id=1, source_target_pairs={{0,1},{1,0},{2,3},{3,2},{4,5},{5,4},{6,7},{7,6},{8,9},{9,8},{10,11... | collective-permute-start | bytes 196616 | tf_op jit(solution)/shard_map/ppermute | solution.py:241
  10.4 0.9 collective-permute-done
  11.3 0.2 select_select_fusion
  11.4 0.0 copy-start.1
  11.5 18.8 %all_to_all.15 = bf16[16,64,512]{2,1,0:T(8,128)(2,1)S(1)} all-to-all(bf16[16,64,512]{2,1,0:T(8,128)(2,1)S(1)} %select_select_fusion), channel_id=1, replica_groups={{0,2,4,6,8,10,12,14,16,18,20,22,24,26,28,30},{32,34,36,38,40,42,44,46,4..., dimensions={0} | all-to-all | bytes 2097152 | tf_op jit(solution)/shard_map/all_to_all | solution.py:246
  30.3 0.1 shard_map.76
  30.3 10.9 %collective-permute-start.1 = (bf16[1040,256]{1,0:T(8,128)(2,1)S(1)}, bf16[1040,256]{1,0:T(8,128)(2,1)S(1)}, u32[]{:S(2)}, u32[]{:S(2)}) collective-permute-start(bf16[1040,256]{1,0:T(8,128)(2,1)S(1)} %get-tuple-element.18), channel_id=1, source_target_pairs={{0,257},{2,259},{4,261},{6,263},{8,265},{10,267},{12,269},{14,271}... | collective-permute-start | bytes 1597448 | tf_op jit(solution)/shard_map/ppermute | solution.py:249
  41.3 1.9 %collective-permute-start.2 = (bf16[1040,256]{1,0:T(8,128)(2,1)S(1)}, bf16[1040,256]{1,0:T(8,128)(2,1)S(1)}, u32[]{:S(2)}, u32[]{:S(2)}) collective-permute-start(bf16[1040,256]{1,0:T(8,128)(2,1)S(1)} %get-tuple-element.19), channel_id=1, source_target_pairs={{0,33},{2,35},{4,37},{6,39},{8,41},{10,43},{12,45},{14,47},{16,49}... | collective-permute-start | bytes 1597448 | tf_op jit(solution)/shard_map/ppermute | solution.py:250
  43.2 0.1 pad_add_fusion.refs_0_.core_ref
  43.3 0.3 shard_map.77.refs_5_
  43.7 4.7 %collective-permute-done.1.refs_6_.low_ref = bf16[1040,256]{1,0:T(8,128)(2,1)S(1)} collective-permute-done((bf16[1040,256]{1,0:T(8,128)(2,1)S(1)}, bf16[1040,256]{1,0:T(8,128)(2,1)S(1)}, u32[]{:S(2)}, u32[]{:S(2)}) %collective-permute-start.1) | collective-permute-done | bytes 532512 | tf_op jit(solution)/shard_map/ppermute | solution.py:249
  48.4 1.8 %shard_map.78 = (bf16[512,256]{1,0:T(8,128)(2,1)S(1)}, bf16[16,128,128]{2,1,0:T(8,128)(2,1)S(1)}, f32[8,128]{1,0:T(8,128)S(1)}) custom-call(s32[3]{0:T(128)S(1)} %pad_add_fusion.refs_0_.core_ref, f32[1,16]{1,0:T(1,128)S(1)} %bitcast.25, s32[1,512]{1,0:T(1,128)S(1)} %bitcast.20, s32[1,512]{1,0:T(1,128)S(1)} %bitcast.23, bf16[1024,512]{1,0:T(8,128)(2,1)S(1)} %bitcast.17, ...), custom_call_target="tpu_custom_call" | custom-call | flops 536870912 | bytes 2097152 | tf_op jit(solution)/shard_map/pallas_call | solution.py:262
  50.2 1.9 %collective-permute-start.4 = (bf16[16,128,128]{2,1,0:T(8,128)(2,1)S(1)}, bf16[16,128,128]{2,1,0:T(8,128)(2,1)S(1)}, u32[]{:S(2)}, u32[]{:S(2)}) collective-permute-start(bf16[16,128,128]{2,1,0:T(8,128)(2,1)S(1)} %get-tuple-element.24), channel_id=1, source_target_pairs={{0,1},{2,3},{4,5},{6,7},{8,9},{10,11},{12,13},{14,15},{16,17},{18,... | collective-permute-start | bytes 1572872 | tf_op jit(solution)/shard_map/ppermute | solution.py:265
  52.2 1.8 %shard_map.79 = (bf16[512,256]{1,0:T(8,128)(2,1)S(1)}, bf16[16,128,128]{2,1,0:T(8,128)(2,1)S(1)}, bf16[16,16,128]{2,1,0:T(8,128)(2,1)S(1)}) custom-call(s32[3]{0:T(128)S(1)} %pad_add_fusion.refs_0_.core_ref, f32[1,16]{1,0:T(1,128)S(1)} %bitcast.26, s32[1,512]{1,0:T(1,128)S(1)} %bitcast.21, s32[1,512]{1,0:T(1,128)S(1)} %bitcast.24, ...), custom_call_target="tpu_custom_call" | custom-call | flops 536870912 | bytes 2097152 | tf_op jit(solution)/shard_map/pallas_call | solution.py:266
  54.0 3.6 %collective-permute-start.3 = (bf16[16,128,128]{2,1,0:T(8,128)(2,1)S(1)}, bf16[16,128,128]{2,1,0:T(8,128)(2,1)S(1)}, u32[]{:S(2)}, u32[]{:S(2)}) collective-permute-start(bf16[16,128,128]{2,1,0:T(8,128)(2,1)S(1)} %get-tuple-element.23), channel_id=1, source_target_pairs={{0,1},{2,3},{4,5},{6,7},{8,9},{10,11},{12,13},{14,15},{16,17},{18,... | collective-permute-start | bytes 1572872 | tf_op jit(solution)/shard_map/ppermute | solution.py:269
  57.6 13.6 %all_to_all.16.loss_ref = bf16[16,16,128]{2,1,0:T(8,128)(2,1)S(1)} all-to-all(bf16[16,16,128]{2,1,0:T(8,128)(2,1)S(1)} %get-tuple-element.25), channel_id=1, replica_groups={{0,32,64,96,128,160,192,224,256,288,320,352,384,416,448,480},{2,34,66,9..., dimensions={0} | all-to-all | bytes 131072 | tf_op jit(solution)/shard_map/all_to_all | solution.py:270
  71.2 0.5 shard_map.80
  71.7 0.5 shard_map.81
  72.2 23.7 %all_to_all.17.got_ref = bf16[16,272,128]{2,1,0:T(8,128)(2,1)S(1)} all-to-all(bf16[16,272,128]{2,1,0:T(8,128)(2,1)S(1)} %shard_map.81), channel_id=1, replica_groups={{0,2,4,6,8,10,12,14,16,18,20,22,24,26,28,30},{32,34,36,38,40,42,44,46,4..., dimensions={0} | all-to-all | bytes 2228224 | tf_op jit(solution)/shard_map/all_to_all | solution.py:278
  96.0 0.8 shard_map.82
  96.7 4.3 %collective-permute-start.5 = (f32[72,512]{1,0:T(8,128)S(1)}, f32[72,512]{1,0:T(8,128)S(1)}, u32[]{:S(2)}, u32[]{:S(2)}) collective-permute-start(f32[72,512]{1,0:T(8,128)S(1)} %get-tuple-element.29.give_ref), channel_id=1, source_target_pairs={{0,1},{1,0},{2,3},{3,2},{4,5},{5,4},{6,7},{7,6},{8,9},{9,8},{10,11... | collective-permute-start | bytes 442376 | tf_op jit(solution)/shard_map/ppermute | solution.py:287
  101.1 1.0 collective-permute-done.5.taken_ref
  102.1 1.2 %shard_map.83 = (f32[32,512]{1,0:T(8,128)}, f32[64,512]{1,0:T(8,128)}, f32[1,1]{1,0:T(1,128)}) custom-call(s32[3]{0:T(128)S(1)} %pad_add_fusion.refs_0_.core_ref, f32[64,512]{1,0:T(8,128)S(1)} %get-tuple-element.28.keep_ref, f32[72,512]{1,0:T(8,128)S(1)} %get-tuple-element.29.give_ref, f32[72,512]{1,0:T(8,128)S(1)} %collective-permute-done.5.taken_ref), custom_call_target="tpu_custom_call" | custom-call | tf_op jit(solution)/shard_map/pallas_call | solution.py:288
  (12 shorter events, 0.0 us)
Async XLA Ops:
  1.6 9.7 %collective-permute-start = (bf16[64,512]{1,0:T(8,128)(2,1)S(1)}, bf16[64,512]{1,0:T(8,128)(2,1)S(1)}, u32[]{:S(2)}, u32[]{:S(2)}) collective-permute-start(bf16[64,512]{1,0:T(8,128)(2,1)S(1)} %get-tuple-element.34), channel_id=1, source_target_pairs={{0,1},{1,0},{2,3},{3,2},{4,5},{5,4},{6,7},{7,6},{8,9},{9,8},{10,11... | collective-permute-start | bytes 196616 | tf_op jit(solution)/shard_map/ppermute | solution.py:241
  11.4 18.8 %copy-start = (s32[512]{0:T(512)S(1)}, s32[512]{0:T(512)}, u32[]{:S(2)}) copy-start(s32[512]{0:T(512)} %param.7) | copy-start | bytes 6148
  11.4 18.8 %copy-start.1 = (s32[512]{0:T(512)S(1)}, s32[512]{0:T(512)}, u32[]{:S(2)}) copy-start(s32[512]{0:T(512)} %param.8) | copy-start | bytes 6148
  30.3 18.1 %copy-start.2 = (f32[16]{0:T(128)S(1)}, f32[16]{0:T(128)}, u32[]{:S(2)}) copy-start(f32[16]{0:T(128)} %param.9) | copy-start | bytes 196
  30.3 18.1 %collective-permute-start.1 = (bf16[1040,256]{1,0:T(8,128)(2,1)S(1)}, bf16[1040,256]{1,0:T(8,128)(2,1)S(1)}, u32[]{:S(2)}, u32[]{:S(2)}) collective-permute-start(bf16[1040,256]{1,0:T(8,128)(2,1)S(1)} %get-tuple-element.18), channel_id=1, source_target_pairs={{0,257},{2,259},{4,261},{6,263},{8,265},{10,267},{12,269},{14,271}... | collective-permute-start | bytes 1597448 | tf_op jit(solution)/shard_map/ppermute | solution.py:249
  41.3 10.9 %collective-permute-start.2 = (bf16[1040,256]{1,0:T(8,128)(2,1)S(1)}, bf16[1040,256]{1,0:T(8,128)(2,1)S(1)}, u32[]{:S(2)}, u32[]{:S(2)}) collective-permute-start(bf16[1040,256]{1,0:T(8,128)(2,1)S(1)} %get-tuple-element.19), channel_id=1, source_target_pairs={{0,33},{2,35},{4,37},{6,39},{8,41},{10,43},{12,45},{14,47},{16,49}... | collective-permute-start | bytes 1597448 | tf_op jit(solution)/shard_map/ppermute | solution.py:250
  50.2 21.0 %collective-permute-start.4 = (bf16[16,128,128]{2,1,0:T(8,128)(2,1)S(1)}, bf16[16,128,128]{2,1,0:T(8,128)(2,1)S(1)}, u32[]{:S(2)}, u32[]{:S(2)}) collective-permute-start(bf16[16,128,128]{2,1,0:T(8,128)(2,1)S(1)} %get-tuple-element.24), channel_id=1, source_target_pairs={{0,1},{2,3},{4,5},{6,7},{8,9},{10,11},{12,13},{14,15},{16,17},{18,... | collective-permute-start | bytes 1572872 | tf_op jit(solution)/shard_map/ppermute | solution.py:265
  54.0 17.7 %collective-permute-start.3 = (bf16[16,128,128]{2,1,0:T(8,128)(2,1)S(1)}, bf16[16,128,128]{2,1,0:T(8,128)(2,1)S(1)}, u32[]{:S(2)}, u32[]{:S(2)}) collective-permute-start(bf16[16,128,128]{2,1,0:T(8,128)(2,1)S(1)} %get-tuple-element.23), channel_id=1, source_target_pairs={{0,1},{2,3},{4,5},{6,7},{8,9},{10,11},{12,13},{14,15},{16,17},{18,... | collective-permute-start | bytes 1572872 | tf_op jit(solution)/shard_map/ppermute | solution.py:269
  96.7 5.3 %collective-permute-start.5 = (f32[72,512]{1,0:T(8,128)S(1)}, f32[72,512]{1,0:T(8,128)S(1)}, u32[]{:S(2)}, u32[]{:S(2)}) collective-permute-start(f32[72,512]{1,0:T(8,128)S(1)} %get-tuple-element.29.give_ref), channel_id=1, source_target_pairs={{0,1},{1,0},{2,3},{3,2},{4,5},{5,4},{6,7},{7,6},{8,9},{9,8},{10,11... | collective-permute-start | bytes 442376 | tf_op jit(solution)/shard_map/ppermute | solution.py:287

commit v10 on v9

--- a/solution.py
+++ b/solution.py
@@ -13,7 +13,7 @@
 LANES = 128
 EXTRA = 16
 VMEM = pl.BlockSpec(memory_space=pltpu.VMEM)
-SMEM = pl.BlockSpec(memory_space=pltpu.SMEM)
+ANY = pl.BlockSpec(memory_space=pl.ANY)
 
 
 def loss_rows(value, shape):
@@ -36,6 +36,14 @@
 
 def block_of(index, blocks):
     return (index // (blocks // 2) + index) % 2
+
+
+def place(n_clip):
+    act = lax.axis_index("act")
+    core = lax.rem(act, 2)
+    clip = lax.axis_index("clip")
+    kind = lax.rem(lax.div(clip, n_clip // 2) + clip, 2)
+    return core, kind, act - core + kind
 
 
 def split_kernel(own_ref, positive_ref, robot_ref, low_ref, high_ref):
@@ -55,18 +63,19 @@
     own_t_ref[...] = own_ref[...].T
 
 
-def sides(start, core_ref, bias_ref, positive_ref, robot_ref, got_rows):
+def sides(n_clip, start, bias_ref, positive_ref, robot_ref, got_rows):
     count = robot_ref.shape[1]
     step = got_rows.shape[1]
     part = slice(start, start + step)
-    first = core_ref[0] == 0
+    core, kind, index = place(n_clip)
+    first = core == 0
     arrived = jnp.concatenate([got_rows[2:3, :], got_rows[3:4, :]], axis=1)
-    robot = jnp.where(core_ref[0] == core_ref[2], robot_ref[...].astype(F32), arrived)
+    robot = jnp.where(core == kind, robot_ref[...].astype(F32), arrived)
     bias = jnp.zeros((1, count), F32)
-    for index in range(bias_ref.shape[1]):
-        bias = jnp.where(robot == index, bias_ref[:, index : index + 1], bias)
+    for each in range(bias_ref.shape[1]):
+        bias = jnp.where(robot == each, bias_ref[:, each : each + 1], bias)
     zero = jnp.zeros((1, count), F32)
-    action = (lax.broadcasted_iota(jnp.int32, (1, count), 1) + core_ref[1] * count).astype(F32)
+    action = (lax.broadcasted_iota(jnp.int32, (1, count), 1) + index * count).astype(F32)
     rows = [jnp.where(first, zero, bias), jnp.where(first, positive_ref[...].astype(F32), action)]
     rows = jnp.concatenate(rows + [zero] * 6, axis=0).T
     column_bias = jnp.where(first, bias, zero)[:, part]
@@ -74,11 +83,11 @@
     return rows[:, 0:1], rows[:, 1:2], column_bias, column_key
 
 
-def logits_kernel(scale, start, core_ref, bias_ref, positive_ref, robot_ref, own_ref, own_t_ref, got_ref, before_ref,
+def logits_kernel(n_clip, scale, start, bias_ref, positive_ref, robot_ref, own_ref, own_t_ref, got_ref, before_ref,
                   weights_ref, grad_ref, loss_ref):
     width = own_ref.shape[0]
     got_rows = got_ref[width:, :].astype(F32)
-    row_bias, row_key, column_bias, column_key = sides(start, core_ref, bias_ref, positive_ref, robot_ref, got_rows)
+    row_bias, row_key, column_bias, column_key = sides(n_clip, start, bias_ref, positive_ref, robot_ref, got_rows)
     got = got_ref[:width, :]
     total = jnp.zeros((1, got.shape[1]), F32)
     for row in range(0, own_t_ref.shape[0], LANES):
@@ -103,12 +112,12 @@
         loss_ref[...] = loss_rows(total, loss_ref.shape)
 
 
-def low_kernel(scale, *refs):
-    logits_kernel(scale, 0, *refs[:7], None, *refs[7:])
-
-
-def high_kernel(scale, *refs):
-    logits_kernel(scale, refs[6].shape[1], *refs)
+def low_kernel(n_clip, scale, *refs):
+    logits_kernel(n_clip, scale, 0, *refs[:6], None, *refs[6:])
+
+
+def high_kernel(n_clip, scale, *refs):
+    logits_kernel(n_clip, scale, refs[5].shape[1], *refs)
 
 
 def received_loss(rows):
@@ -148,10 +157,11 @@
     add_second(low_ref.shape[1], low_ref, high_ref, low_weights_ref, high_weights_ref, got_ref, out_ref)
 
 
-def sum_kernel(clip_scale, action_scale, core_ref, got_ref, keep_ref, give_ref):
+def sum_kernel(clip_scale, action_scale, got_ref, keep_ref, give_ref):
     blocks = got_ref.shape[0]
     rows, count = keep_ref.shape
     half = rows // 2
+    core = place(blocks)[0]
 
     def over(kind):
         chosen = [block for block in range(blocks) if block_of(block, blocks) == kind]
@@ -169,39 +179,46 @@
         columns = slice(part * LANES, (part + 1) * LANES)
         at = slice(part * rows, (part + 1) * rows)
 
-        @pl.when(core_ref[0] == 0)
+        @pl.when(core == 0)
         def _():
             keep_ref[:half, columns] = both[at][:half] * clip_scale
             give_ref[:half, columns] = both[at][half:] * clip_scale
 
-        @pl.when(core_ref[0] != 0)
+        @pl.when(core != 0)
         def _():
             keep_ref[:, columns] = upper[at] * action_scale
             give_ref[:rows, columns] = lower[at] * action_scale
 
 
-def last_kernel(loss_scale, core_ref, keep_ref, give_ref, taken_ref, clip_ref, action_ref, loss_ref):
+def last_kernel(n_clip, loss_scale, keep_ref, give_ref, taken_ref, clip_ref, action_ref, loss_ref, sent):
     rows = keep_ref.shape[0]
     half = clip_ref.shape[0]
+    core = place(n_clip)[0]
+
+    def write(clip, action):
+        copies = [pltpu.make_async_copy(clip, clip_ref, sent.at[0]), pltpu.make_async_copy(action, action_ref, sent.at[1])]
+        for copy in copies:
+            copy.start()
+        for copy in copies:
+            copy.wait()
+
+    @pl.when(core == 0)
+    def _():
+        write(keep_ref.at[:half, :], taken_ref.at[:rows, :])
+
+    @pl.when(core != 0)
+    def _():
+        write(taken_ref.at[:half, :], keep_ref)
+
     loss_ref[...] = (give_ref[rows : rows + 1, :1] + taken_ref[rows : rows + 1, :1]) * loss_scale
 
-    @pl.when(core_ref[0] == 0)
-    def _():
-        clip_ref[...] = keep_ref[:half, :]
-        action_ref[...] = taken_ref[:rows, :]
-
-    @pl.when(core_ref[0] != 0)
-    def _():
-        clip_ref[...] = taken_ref[:half, :]
-        action_ref[...] = keep_ref[...]
-
-
-def call(kernel, out_shape, in_specs, scratch=(), flops=0, moved=0):
+
+def call(kernel, out_shape, in_specs, out_specs=None, scratch=(), flops=0, moved=0):
     return pl.pallas_call(
         kernel,
         out_shape=out_shape,
         in_specs=in_specs,
-        out_specs=jax.tree.map(lambda _: VMEM, out_shape),
+        out_specs=jax.tree.map(lambda _: VMEM, out_shape) if out_specs is None else out_specs,
         scratch_shapes=scratch,
         compiler_params=pltpu.CompilerParams(vmem_limit_bytes=12 * 1024 * 1024),
         cost_estimate=pl.CostEstimate(flops=flops, bytes_accessed=moved, transcendentals=0),
@@ -230,8 +247,6 @@
     width = rows * n_clip
     parts = count // LANES
     act = lax.axis_index("act")
-    kind = block_of(lax.axis_index("clip"), n_clip)
-    core = jnp.stack([act % 2, act - act % 2 + kind, kind]).astype(jnp.int32)
     shape = jax.ShapeDtypeStruct
 
     first_core = act % 2 == 0
@@ -253,18 +268,18 @@
     flops = 2 * width * count * count
     half_blocks = shape((n_clip, parts * rows // 2, LANES), BF16)
     scale = 2.0 / math.sqrt(width)
-    fixed = (core, robot_bias[None, :], positive_ids, robot_ids, own, own_t)
+    fixed = (robot_bias[None, :], positive_ids, robot_ids, own, own_t)
     def results(loss):
         return (shape((count, count // 2), BF16), half_blocks, loss)
 
     cost = {"flops": flops, "moved": 4 * width * count}
-    specs = [SMEM] + [VMEM] * 6
+    specs = [VMEM] * 6
     low_weights, low_grad, loss = call(
-        functools.partial(low_kernel, scale), results(shape((8, LANES), F32)), specs, **cost
+        functools.partial(low_kernel, n_clip, scale), results(shape((8, LANES), F32)), specs, **cost
     )(*fixed, low)
     low_got = lax.ppermute(low_grad, both, scatter_pass[0])
     high_weights, high_grad, loss_sent = call(
-        functools.partial(high_kernel, scale), results(shape((n_clip, EXTRA, LANES), BF16)), specs + [VMEM], **cost
+        functools.partial(high_kernel, n_clip, scale), results(shape((n_clip, EXTRA, LANES), BF16)), specs + [VMEM], **cost
     )(*fixed, high, loss)
     high_got = lax.ppermute(high_grad, both, scatter_pass[1])
     loss_got = exchange(loss_sent, axis_index_groups=actions_first)
@@ -282,14 +297,16 @@
     keep, give = call(
         functools.partial(sum_kernel, 1.0 / math.sqrt(total_actions), 1.0 / math.sqrt(total_clips)),
         (shape((rows, count), F32), shape((rows + 8, count), F32)),
-        [SMEM, VMEM],
-    )(core, scattered)
+        [VMEM],
+    )(scattered)
     taken = lax.ppermute(give, "act", swap)
     clip_grad, action_grad, loss = call(
-        functools.partial(last_kernel, 1.0 / (total_clips * total_actions)),
+        functools.partial(last_kernel, n_clip, 1.0 / (total_clips * total_actions)),
         (shape((half, count), F32), shape((rows, count), F32), shape((1, 1), F32)),
-        [SMEM] + [VMEM] * 3,
-    )(core, keep, give, taken)
+        [VMEM] * 3,
+        (ANY, ANY, VMEM),
+        [pltpu.SemaphoreType.DMA((2,))],
+    )(keep, give, taken)
     return clip_grad, action_grad, loss.reshape(())
 
 

time: 104 us -> 102 us (0.981)
  Pallas kernels: 7 us -> 5.31 us
    pallas_call x3, Pallas kernels: 4.83 us -> 3.72 us  [the longest x1 1.27 us: shards(): call(functools.partial(low_kernel, n_clip, scale), results(shape((8, LANE...]
  transfers between devices with their start and end apart: 6 -> 6, of which waited for: 3 -> 4; matrix products, arithmetic and copies ran while one was open for 0% -> 0% of each run, Pallas kernels for 4% -> 3%
where the time goes in v10:
time: 102 us
  blocking collectives  56.2 us (55%)
  starting transfers between devices  31.2 us (31%)
  waiting for transfers between devices  6.95 us (7%)
  Pallas kernels  5.31 us (5%)
  other arithmetic  1.1 us (1%)
    all_to_all x1, blocking collectives, shards(): scattered = exchange(ready, axis_index_groups=clips_first)  23.7 us
    all_to_all x1, blocking collectives, shards(): own = exchange(chunks, axis_index_groups=clips_first).reshape(width, count)  18.8 us
    all_to_all x1, blocking collectives, shards(): loss_got = exchange(loss_sent, axis_index_groups=actions_first)  13.6 us
    ppermute x1, starting transfers between devices, shards(): low = lax.ppermute(low, both, gather_pass[0])  10.9 us
    ppermute x1, starting transfers between devices, shards(): other = lax.ppermute(send, 'act', swap)  8.79 us
    ppermute x1, waiting for transfers between devices, shards(): low = lax.ppermute(low, both, gather_pass[0])  4.86 us
    ppermute x1, starting transfers between devices, shards(): taken = lax.ppermute(give, 'act', swap)  4.34 us
    ppermute x1, starting transfers between devices, shards(): high_got = lax.ppermute(high_grad, both, scatter_pass[1])  3.35 us
  transfers between devices with their start and end apart: 6, of which 4 were waited for; matrix products, arithmetic and copies ran while one was open for 0% of the time, Pallas kernels for 3%

profile of v10, /device:TPU:1, one launch (start us, length us, event | category | flops | bytes accessed | tf_op | source)
XLA Modules:
  0.0 101.6 jit_solution(10526628325710062735)
XLA Ops:
  0.6 0.9 fusion
  1.6 8.8 %collective-permute-start = (bf16[64,512]{1,0:T(8,128)(2,1)S(1)}, bf16[64,512]{1,0:T(8,128)(2,1)S(1)}, u32[]{:S(2)}, u32[]{:S(2)}) collective-permute-start(bf16[64,512]{1,0:T(8,128)(2,1)S(1)} %get-tuple-element.34), channel_id=1, source_target_pairs={{0,1},{1,0},{2,3},{3,2},{4,5},{5,4},{6,7},{7,6},{8,9},{9,8},{10,11... | collective-permute-start | bytes 196616 | tf_op jit(solution)/shard_map/ppermute | solution.py:256
  10.4 0.9 collective-permute-done
  11.3 0.2 select_select_fusion
  11.4 18.8 %all_to_all.15 = bf16[16,64,512]{2,1,0:T(8,128)(2,1)S(1)} all-to-all(bf16[16,64,512]{2,1,0:T(8,128)(2,1)S(1)} %select_select_fusion), channel_id=1, replica_groups={{0,2,4,6,8,10,12,14,16,18,20,22,24,26,28,30},{32,34,36,38,40,42,44,46,4..., dimensions={0} | all-to-all | bytes 2097152 | tf_op jit(solution)/shard_map/all_to_all | solution.py:261
  30.3 0.1 shard_map.76
  30.3 0.0 copy-start.2
  30.3 10.9 %collective-permute-start.1 = (bf16[1040,256]{1,0:T(8,128)(2,1)S(1)}, bf16[1040,256]{1,0:T(8,128)(2,1)S(1)}, u32[]{:S(2)}, u32[]{:S(2)}) collective-permute-start(bf16[1040,256]{1,0:T(8,128)(2,1)S(1)} %get-tuple-element.18), channel_id=1, source_target_pairs={{0,257},{2,259},{4,261},{6,263},{8,265},{10,267},{12,269},{14,271}... | collective-permute-start | bytes 1597448 | tf_op jit(solution)/shard_map/ppermute | solution.py:264
  41.3 1.9 %collective-permute-start.2 = (bf16[1040,256]{1,0:T(8,128)(2,1)S(1)}, bf16[1040,256]{1,0:T(8,128)(2,1)S(1)}, u32[]{:S(2)}, u32[]{:S(2)}) collective-permute-start(bf16[1040,256]{1,0:T(8,128)(2,1)S(1)} %get-tuple-element.19), channel_id=1, source_target_pairs={{0,33},{2,35},{4,37},{6,39},{8,41},{10,43},{12,45},{14,47},{16,49}... | collective-permute-start | bytes 1597448 | tf_op jit(solution)/shard_map/ppermute | solution.py:265
  43.2 0.3 shard_map.77.refs_4_
  43.6 4.9 %collective-permute-done.1.refs_5_.low_ref = bf16[1040,256]{1,0:T(8,128)(2,1)S(1)} collective-permute-done((bf16[1040,256]{1,0:T(8,128)(2,1)S(1)}, bf16[1040,256]{1,0:T(8,128)(2,1)S(1)}, u32[]{:S(2)}, u32[]{:S(2)}) %collective-permute-start.1) | collective-permute-done | bytes 532512 | tf_op jit(solution)/shard_map/ppermute | solution.py:264
  48.4 1.3 %shard_map.78 = (bf16[512,256]{1,0:T(8,128)(2,1)S(1)}, bf16[16,128,128]{2,1,0:T(8,128)(2,1)S(1)}, f32[8,128]{1,0:T(8,128)S(1)}) custom-call(f32[1,16]{1,0:T(1,128)S(1)} %bitcast.22, s32[1,512]{1,0:T(1,128)S(1)} %bitcast.17, s32[1,512]{1,0:T(1,128)S(1)} %bitcast.20, bf16[1024,512]{1,0:T(8,128)(2,1)S(1)} %bitcast.14, bf16[512,1024]{1,0:T(8,128)(2,1)S(1)} %shard_map.77.refs_4_, ...), custom_call_target="tpu_custom_call" | custom-call | flops 536870912 | bytes 2097152 | tf_op jit(solution)/shard_map/pallas_call | solution.py:277
  49.7 1.9 %collective-permute-start.4 = (bf16[16,128,128]{2,1,0:T(8,128)(2,1)S(1)}, bf16[16,128,128]{2,1,0:T(8,128)(2,1)S(1)}, u32[]{:S(2)}, u32[]{:S(2)}) collective-permute-start(bf16[16,128,128]{2,1,0:T(8,128)(2,1)S(1)} %get-tuple-element.24), channel_id=1, source_target_pairs={{0,1},{2,3},{4,5},{6,7},{8,9},{10,11},{12,13},{14,15},{16,17},{18,... | collective-permute-start | bytes 1572872 | tf_op jit(solution)/shard_map/ppermute | solution.py:280
  51.6 0.2 collective-permute-done.2.refs_5_.high_ref
  51.9 1.2 %shard_map.79 = (bf16[512,256]{1,0:T(8,128)(2,1)S(1)}, bf16[16,128,128]{2,1,0:T(8,128)(2,1)S(1)}, bf16[16,16,128]{2,1,0:T(8,128)(2,1)S(1)}) custom-call(f32[1,16]{1,0:T(1,128)S(1)} %bitcast.23, s32[1,512]{1,0:T(1,128)S(1)} %bitcast.18, s32[1,512]{1,0:T(1,128)S(1)} %bitcast.21, bf16[1024,512]{1,0:T(8,128)(2,1)S(1)} %bitcast.15, ...), custom_call_target="tpu_custom_call" | custom-call | flops 536870912 | bytes 2097152 | tf_op jit(solution)/shard_map/pallas_call | solution.py:281
  53.1 3.4 %collective-permute-start.3 = (bf16[16,128,128]{2,1,0:T(8,128)(2,1)S(1)}, bf16[16,128,128]{2,1,0:T(8,128)(2,1)S(1)}, u32[]{:S(2)}, u32[]{:S(2)}) collective-permute-start(bf16[16,128,128]{2,1,0:T(8,128)(2,1)S(1)} %get-tuple-element.23), channel_id=1, source_target_pairs={{0,1},{2,3},{4,5},{6,7},{8,9},{10,11},{12,13},{14,15},{16,17},{18,... | collective-permute-start | bytes 1572872 | tf_op jit(solution)/shard_map/ppermute | solution.py:284
  56.5 13.6 %all_to_all.16.loss_ref = bf16[16,16,128]{2,1,0:T(8,128)(2,1)S(1)} all-to-all(bf16[16,16,128]{2,1,0:T(8,128)(2,1)S(1)} %get-tuple-element.25), channel_id=1, replica_groups={{0,32,64,96,128,160,192,224,256,288,320,352,384,416,448,480},{2,34,66,9..., dimensions={0} | all-to-all | bytes 131072 | tf_op jit(solution)/shard_map/all_to_all | solution.py:285
  70.1 0.5 shard_map.80
  70.6 0.5 shard_map.81
  71.1 23.7 %all_to_all.17.got_ref = bf16[16,272,128]{2,1,0:T(8,128)(2,1)S(1)} all-to-all(bf16[16,272,128]{2,1,0:T(8,128)(2,1)S(1)} %shard_map.81), channel_id=1, replica_groups={{0,2,4,6,8,10,12,14,16,18,20,22,24,26,28,30},{32,34,36,38,40,42,44,46,4..., dimensions={0} | all-to-all | bytes 2228224 | tf_op jit(solution)/shard_map/all_to_all | solution.py:293
  94.9 0.2 shard_map.82
  95.1 4.3 %collective-permute-start.5 = (f32[72,512]{1,0:T(8,128)S(1)}, f32[72,512]{1,0:T(8,128)S(1)}, u32[]{:S(2)}, u32[]{:S(2)}) collective-permute-start(f32[72,512]{1,0:T(8,128)S(1)} %get-tuple-element.29.give_ref), channel_id=1, source_target_pairs={{0,1},{1,0},{2,3},{3,2},{4,5},{5,4},{6,7},{7,6},{8,9},{9,8},{10,11... | collective-permute-start | bytes 442376 | tf_op jit(solution)/shard_map/ppermute | solution.py:302
  99.4 1.0 collective-permute-done.5.taken_ref
  100.4 1.2 %shard_map.83 = (f32[32,512]{1,0:T(8,128)}, f32[64,512]{1,0:T(8,128)}, f32[1,1]{1,0:T(1,128)}) custom-call(f32[64,512]{1,0:T(8,128)S(1)} %get-tuple-element.28.keep_ref, f32[72,512]{1,0:T(8,128)S(1)} %get-tuple-element.29.give_ref, f32[72,512]{1,0:T(8,128)S(1)} %collective-permute-done.5.taken_ref), custom_call_target="tpu_custom_call" | custom-call | tf_op jit(solution)/shard_map/pallas_call | solution.py:303
  (11 shorter events, 0.0 us)
Async XLA Ops:
  1.6 9.7 %collective-permute-start = (bf16[64,512]{1,0:T(8,128)(2,1)S(1)}, bf16[64,512]{1,0:T(8,128)(2,1)S(1)}, u32[]{:S(2)}, u32[]{:S(2)}) collective-permute-start(bf16[64,512]{1,0:T(8,128)(2,1)S(1)} %get-tuple-element.34), channel_id=1, source_target_pairs={{0,1},{1,0},{2,3},{3,2},{4,5},{5,4},{6,7},{7,6},{8,9},{9,8},{10,11... | collective-permute-start | bytes 196616 | tf_op jit(solution)/shard_map/ppermute | solution.py:256
  11.4 18.8 %copy-start = (s32[512]{0:T(512)S(1)}, s32[512]{0:T(512)}, u32[]{:S(2)}) copy-start(s32[512]{0:T(512)} %param.7) | copy-start | bytes 6148
  11.4 18.8 %copy-start.1 = (s32[512]{0:T(512)S(1)}, s32[512]{0:T(512)}, u32[]{:S(2)}) copy-start(s32[512]{0:T(512)} %param.8) | copy-start | bytes 6148
  30.3 18.1 %copy-start.2 = (f32[16]{0:T(128)S(1)}, f32[16]{0:T(128)}, u32[]{:S(2)}) copy-start(f32[16]{0:T(128)} %param.9) | copy-start | bytes 196
  30.3 18.1 %collective-permute-start.1 = (bf16[1040,256]{1,0:T(8,128)(2,1)S(1)}, bf16[1040,256]{1,0:T(8,128)(2,1)S(1)}, u32[]{:S(2)}, u32[]{:S(2)}) collective-permute-start(bf16[1040,256]{1,0:T(8,128)(2,1)S(1)} %get-tuple-element.18), channel_id=1, source_target_pairs={{0,257},{2,259},{4,261},{6,263},{8,265},{10,267},{12,269},{14,271}... | collective-permute-start | bytes 1597448 | tf_op jit(solution)/shard_map/ppermute | solution.py:264
  41.3 10.6 %collective-permute-start.2 = (bf16[1040,256]{1,0:T(8,128)(2,1)S(1)}, bf16[1040,256]{1,0:T(8,128)(2,1)S(1)}, u32[]{:S(2)}, u32[]{:S(2)}) collective-permute-start(bf16[1040,256]{1,0:T(8,128)(2,1)S(1)} %get-tuple-element.19), channel_id=1, source_target_pairs={{0,33},{2,35},{4,37},{6,39},{8,41},{10,43},{12,45},{14,47},{16,49}... | collective-permute-start | bytes 1597448 | tf_op jit(solution)/shard_map/ppermute | solution.py:265
  49.7 20.4 %collective-permute-start.4 = (bf16[16,128,128]{2,1,0:T(8,128)(2,1)S(1)}, bf16[16,128,128]{2,1,0:T(8,128)(2,1)S(1)}, u32[]{:S(2)}, u32[]{:S(2)}) collective-permute-start(bf16[16,128,128]{2,1,0:T(8,128)(2,1)S(1)} %get-tuple-element.24), channel_id=1, source_target_pairs={{0,1},{2,3},{4,5},{6,7},{8,9},{10,11},{12,13},{14,15},{16,17},{18,... | collective-permute-start | bytes 1572872 | tf_op jit(solution)/shard_map/ppermute | solution.py:280
  53.1 17.5 %collective-permute-start.3 = (bf16[16,128,128]{2,1,0:T(8,128)(2,1)S(1)}, bf16[16,128,128]{2,1,0:T(8,128)(2,1)S(1)}, u32[]{:S(2)}, u32[]{:S(2)}) collective-permute-start(bf16[16,128,128]{2,1,0:T(8,128)(2,1)S(1)} %get-tuple-element.23), channel_id=1, source_target_pairs={{0,1},{2,3},{4,5},{6,7},{8,9},{10,11},{12,13},{14,15},{16,17},{18,... | collective-permute-start | bytes 1572872 | tf_op jit(solution)/shard_map/ppermute | solution.py:284
  95.1 5.3 %collective-permute-start.5 = (f32[72,512]{1,0:T(8,128)S(1)}, f32[72,512]{1,0:T(8,128)S(1)}, u32[]{:S(2)}, u32[]{:S(2)}) collective-permute-start(f32[72,512]{1,0:T(8,128)S(1)} %get-tuple-element.29.give_ref), channel_id=1, source_target_pairs={{0,1},{1,0},{2,3},{3,2},{4,5},{5,4},{6,7},{7,6},{8,9},{9,8},{10,11... | collective-permute-start | bytes 442376 | tf_op jit(solution)/shard_map/ppermute | solution.py:302

commit v11 on v10

--- a/solution.py
+++ b/solution.py
@@ -124,37 +124,28 @@
     return rows[0:1] + rows[4:5] + rows[8:9]
 
 
-def add_second(start, low_ref, high_ref, low_weights_ref, high_weights_ref, got_ref, out_ref):
-    blocks, got_size, _ = got_ref.shape
+def second_kernel(low_ref, high_ref, low_weights_ref, high_weights_ref, low_got_ref, high_got_ref, loss_ref, out_ref):
+    blocks = out_ref.shape[0]
     step = low_ref.shape[1]
     width = low_ref.shape[0] - EXTRA
     size = width // blocks
+    total = loss_ref[0].astype(F32)
+    for block in range(1, blocks):
+        total = total + loss_ref[block].astype(F32)
+    rows = loss_rows(jnp.broadcast_to(received_loss(total), total.shape), total.shape)
+    for block in range(blocks):
+        out_ref[block, out_ref.shape[1] - EXTRA :, :] = rows
     by_columns = (((1,), (1,)), ((), ()))
-    half = slice(start, start + step)
-    grad = lax.dot_general(low_ref[:width, :], low_weights_ref[half, :], by_columns, preferred_element_type=F32)
-    grad += lax.dot_general(high_ref[:width, :], high_weights_ref[half, :], by_columns, preferred_element_type=F32)
-    first = start // step * got_size
-    for part in range(step // LANES):
-        at = slice(part * size, (part + 1) * size)
-        columns = grad[:, part * LANES : (part + 1) * LANES].astype(BF16).reshape(blocks, size, LANES)
-        added = columns.astype(F32) + got_ref[:, at, :].astype(F32)
-        out_ref[:, first + part * size : first + (part + 1) * size, :] = added.astype(BF16)
-
-
-def second_kernel(low_ref, high_ref, low_weights_ref, high_weights_ref, got_ref, loss_ref, out_ref, rows_ref):
-    add_second(0, low_ref, high_ref, low_weights_ref, high_weights_ref, got_ref, out_ref)
-    total = loss_ref[0].astype(F32)
-    for block in range(1, loss_ref.shape[0]):
-        total = total + loss_ref[block].astype(F32)
-    rows_ref[...] = loss_rows(jnp.broadcast_to(received_loss(total), total.shape), total.shape)
-
-
-def third_kernel(low_ref, high_ref, low_weights_ref, high_weights_ref, got_ref, before_ref, rows_ref, out_ref):
-    blocks, before, _ = before_ref.shape
-    for block in range(blocks):
-        out_ref[block, :before, :] = before_ref[block]
-        out_ref[block, out_ref.shape[1] - EXTRA :, :] = rows_ref[...]
-    add_second(low_ref.shape[1], low_ref, high_ref, low_weights_ref, high_weights_ref, got_ref, out_ref)
+    for start, got_ref in ((0, low_got_ref), (step, high_got_ref)):
+        half = slice(start, start + step)
+        grad = lax.dot_general(low_ref[:width, :], low_weights_ref[half, :], by_columns, preferred_element_type=F32)
+        grad += lax.dot_general(high_ref[:width, :], high_weights_ref[half, :], by_columns, preferred_element_type=F32)
+        for part in range(step // LANES):
+            at = slice(part * size, (part + 1) * size)
+            columns = grad[:, part * LANES : (part + 1) * LANES].astype(BF16).reshape(blocks, size, LANES)
+            added = columns.astype(F32) + got_ref[:, at, :].astype(F32)
+            first = (start // LANES + part) * size
+            out_ref[:, first : first + size, :] = added.astype(BF16)
 
 
 def sum_kernel(clip_scale, action_scale, got_ref, keep_ref, give_ref):
@@ -284,11 +275,9 @@
     high_got = lax.ppermute(high_grad, both, scatter_pass[1])
     loss_got = exchange(loss_sent, axis_index_groups=actions_first)
     operands = (low, high, low_weights, high_weights)
-    begun, loss_sum = call(second_kernel, (half_blocks, shape((EXTRA, LANES), BF16)), [VMEM] * 6, **cost)(
-        *operands, low_got, loss_got
-    )
-    ready = call(third_kernel, shape((n_clip, parts * rows + EXTRA, LANES), BF16), [VMEM] * 7, **cost)(
-        *operands, high_got, begun, loss_sum
+    low_got, loss_got = lax.optimization_barrier((low_got, loss_got))
+    ready = call(second_kernel, shape((n_clip, parts * rows + EXTRA, LANES), BF16), [VMEM] * 7, **cost)(
+        *operands, low_got, high_got, loss_got
     )
     scattered = exchange(ready, axis_index_groups=clips_first)
 

time: 102 us -> 102 us (level)
  no operation moved by 1% of the time
where the time goes in v11:
time: 102 us; the launch traced here: 101 us
  blocking collectives  56.2 us (55%)
  starting transfers between devices  31.2 us (31%)
  waiting for transfers between devices  6.95 us (7%)
  Pallas kernels  5.09 us (5%)
  other arithmetic  1.1 us (1%)
    all_to_all x1, blocking collectives, shards(): scattered = exchange(ready, axis_index_groups=clips_first)  23.7 us
    all_to_all x1, blocking collectives, shards(): own = exchange(chunks, axis_index_groups=clips_first).reshape(width, count)  18.8 us
    all_to_all x1, blocking collectives, shards(): loss_got = exchange(loss_sent, axis_index_groups=actions_first)  13.6 us
    ppermute x1, starting transfers between devices, shards(): low = lax.ppermute(low, both, gather_pass[0])  10.9 us
    ppermute x1, starting transfers between devices, shards(): other = lax.ppermute(send, 'act', swap)  8.79 us
    ppermute x1, waiting for transfers between devices, shards(): low = lax.ppermute(low, both, gather_pass[0])  4.86 us
    ppermute x1, starting transfers between devices, shards(): taken = lax.ppermute(give, 'act', swap)  4.34 us
    ppermute x1, starting transfers between devices, shards(): high_got = lax.ppermute(high_grad, both, scatter_pass[1])  3.35 us
  transfers between devices with their start and end apart: 6, of which 4 were waited for; matrix products, arithmetic and copies ran while one was open for 0% of the time, Pallas kernels for 3%

profile of v11, /device:TPU:1, one launch (start us, length us, event | category | flops | bytes accessed | tf_op | source)
XLA Modules:
  0.0 101.4 jit_solution(7351512149297830631)
XLA Ops:
  0.6 0.9 fusion
  1.6 8.8 %collective-permute-start = (bf16[64,512]{1,0:T(8,128)(2,1)S(1)}, bf16[64,512]{1,0:T(8,128)(2,1)S(1)}, u32[]{:S(2)}, u32[]{:S(2)}) collective-permute-start(bf16[64,512]{1,0:T(8,128)(2,1)S(1)} %get-tuple-element.34), channel_id=1, source_target_pairs={{0,1},{1,0},{2,3},{3,2},{4,5},{5,4},{6,7},{7,6},{8,9},{9,8},{10,11... | collective-permute-start | bytes 196616 | tf_op jit(solution)/shard_map/ppermute | solution.py:247
  10.4 0.9 collective-permute-done
  11.3 0.2 select_select_fusion
  11.4 0.0 copy-start
  11.4 18.8 %all_to_all.15 = bf16[16,64,512]{2,1,0:T(8,128)(2,1)S(1)} all-to-all(bf16[16,64,512]{2,1,0:T(8,128)(2,1)S(1)} %select_select_fusion), channel_id=1, replica_groups={{0,2,4,6,8,10,12,14,16,18,20,22,24,26,28,30},{32,34,36,38,40,42,44,46,4..., dimensions={0} | all-to-all | bytes 2097152 | tf_op jit(solution)/shard_map/all_to_all | solution.py:252
  30.3 0.1 shard_map.76
  30.3 0.0 copy-start.2
  30.3 10.9 %collective-permute-start.1 = (bf16[1040,256]{1,0:T(8,128)(2,1)S(1)}, bf16[1040,256]{1,0:T(8,128)(2,1)S(1)}, u32[]{:S(2)}, u32[]{:S(2)}) collective-permute-start(bf16[1040,256]{1,0:T(8,128)(2,1)S(1)} %get-tuple-element.18), channel_id=1, source_target_pairs={{0,257},{2,259},{4,261},{6,263},{8,265},{10,267},{12,269},{14,271}... | collective-permute-start | bytes 1597448 | tf_op jit(solution)/shard_map/ppermute | solution.py:255
  41.3 1.9 %collective-permute-start.2 = (bf16[1040,256]{1,0:T(8,128)(2,1)S(1)}, bf16[1040,256]{1,0:T(8,128)(2,1)S(1)}, u32[]{:S(2)}, u32[]{:S(2)}) collective-permute-start(bf16[1040,256]{1,0:T(8,128)(2,1)S(1)} %get-tuple-element.19), channel_id=1, source_target_pairs={{0,33},{2,35},{4,37},{6,39},{8,41},{10,43},{12,45},{14,47},{16,49}... | collective-permute-start | bytes 1597448 | tf_op jit(solution)/shard_map/ppermute | solution.py:256
  43.2 0.3 shard_map.77.refs_4_
  43.6 4.9 %collective-permute-done.1.refs_5_.low_ref = bf16[1040,256]{1,0:T(8,128)(2,1)S(1)} collective-permute-done((bf16[1040,256]{1,0:T(8,128)(2,1)S(1)}, bf16[1040,256]{1,0:T(8,128)(2,1)S(1)}, u32[]{:S(2)}, u32[]{:S(2)}) %collective-permute-start.1) | collective-permute-done | bytes 532512 | tf_op jit(solution)/shard_map/ppermute | solution.py:255
  48.4 1.3 %shard_map.78 = (bf16[512,256]{1,0:T(8,128)(2,1)S(1)}, bf16[16,128,128]{2,1,0:T(8,128)(2,1)S(1)}, f32[8,128]{1,0:T(8,128)S(1)}) custom-call(f32[1,16]{1,0:T(1,128)S(1)} %bitcast.22, s32[1,512]{1,0:T(1,128)S(1)} %bitcast.17, s32[1,512]{1,0:T(1,128)S(1)} %bitcast.20, bf16[1024,512]{1,0:T(8,128)(2,1)S(1)} %bitcast.14, bf16[512,1024]{1,0:T(8,128)(2,1)S(1)} %shard_map.77.refs_4_, ...), custom_call_target="tpu_custom_call" | custom-call | flops 536870912 | bytes 2097152 | tf_op jit(solution)/shard_map/pallas_call | solution.py:268
  49.7 1.9 %collective-permute-start.3 = (bf16[16,128,128]{2,1,0:T(8,128)(2,1)S(1)}, bf16[16,128,128]{2,1,0:T(8,128)(2,1)S(1)}, u32[]{:S(2)}, u32[]{:S(2)}) collective-permute-start(bf16[16,128,128]{2,1,0:T(8,128)(2,1)S(1)} %get-tuple-element.23), channel_id=1, source_target_pairs={{0,1},{2,3},{4,5},{6,7},{8,9},{10,11},{12,13},{14,15},{16,17},{18,... | collective-permute-start | bytes 1572872 | tf_op jit(solution)/shard_map/ppermute | solution.py:271
  51.6 0.2 collective-permute-done.2.refs_5_.high_ref
  51.9 1.2 %shard_map.79 = (bf16[512,256]{1,0:T(8,128)(2,1)S(1)}, bf16[16,128,128]{2,1,0:T(8,128)(2,1)S(1)}, bf16[16,16,128]{2,1,0:T(8,128)(2,1)S(1)}) custom-call(f32[1,16]{1,0:T(1,128)S(1)} %bitcast.23, s32[1,512]{1,0:T(1,128)S(1)} %bitcast.18, s32[1,512]{1,0:T(1,128)S(1)} %bitcast.21, bf16[1024,512]{1,0:T(8,128)(2,1)S(1)} %bitcast.15, ...), custom_call_target="tpu_custom_call" | custom-call | flops 536870912 | bytes 2097152 | tf_op jit(solution)/shard_map/pallas_call | solution.py:272
  53.1 3.4 %collective-permute-start.4 = (bf16[16,128,128]{2,1,0:T(8,128)(2,1)S(1)}, bf16[16,128,128]{2,1,0:T(8,128)(2,1)S(1)}, u32[]{:S(2)}, u32[]{:S(2)}) collective-permute-start(bf16[16,128,128]{2,1,0:T(8,128)(2,1)S(1)} %get-tuple-element.26), channel_id=1, source_target_pairs={{0,1},{2,3},{4,5},{6,7},{8,9},{10,11},{12,13},{14,15},{16,17},{18,... | collective-permute-start | bytes 1572872 | tf_op jit(solution)/shard_map/ppermute | solution.py:275
  56.5 13.6 %all_to_all.16.loss_ref = bf16[16,16,128]{2,1,0:T(8,128)(2,1)S(1)} all-to-all(bf16[16,16,128]{2,1,0:T(8,128)(2,1)S(1)} %get-tuple-element.24), channel_id=1, replica_groups={{0,32,64,96,128,160,192,224,256,288,320,352,384,416,448,480},{2,34,66,9..., dimensions={0} | all-to-all | bytes 131072 | tf_op jit(solution)/shard_map/all_to_all | solution.py:276
  70.1 0.8 shard_map.80
  70.9 23.7 %all_to_all.17.got_ref = bf16[16,272,128]{2,1,0:T(8,128)(2,1)S(1)} all-to-all(bf16[16,272,128]{2,1,0:T(8,128)(2,1)S(1)} %shard_map.80), channel_id=1, replica_groups={{0,2,4,6,8,10,12,14,16,18,20,22,24,26,28,30},{32,34,36,38,40,42,44,46,4..., dimensions={0} | all-to-all | bytes 2228224 | tf_op jit(solution)/shard_map/all_to_all | solution.py:282
  94.6 0.2 shard_map.81
  94.8 4.3 %collective-permute-start.5 = (f32[72,512]{1,0:T(8,128)S(1)}, f32[72,512]{1,0:T(8,128)S(1)}, u32[]{:S(2)}, u32[]{:S(2)}) collective-permute-start(f32[72,512]{1,0:T(8,128)S(1)} %get-tuple-element.29.give_ref), channel_id=1, source_target_pairs={{0,1},{1,0},{2,3},{3,2},{4,5},{5,4},{6,7},{7,6},{8,9},{9,8},{10,11... | collective-permute-start | bytes 442376 | tf_op jit(solution)/shard_map/ppermute | solution.py:291
  99.2 1.0 collective-permute-done.5.taken_ref
  100.2 1.2 %shard_map.82 = (f32[32,512]{1,0:T(8,128)}, f32[64,512]{1,0:T(8,128)}, f32[1,1]{1,0:T(1,128)}) custom-call(f32[64,512]{1,0:T(8,128)S(1)} %get-tuple-element.28.keep_ref, f32[72,512]{1,0:T(8,128)S(1)} %get-tuple-element.29.give_ref, f32[72,512]{1,0:T(8,128)S(1)} %collective-permute-done.5.taken_ref), custom_call_target="tpu_custom_call" | custom-call | tf_op jit(solution)/shard_map/pallas_call | solution.py:292
  (10 shorter events, 0.0 us)
Async XLA Ops:
  1.6 9.7 %collective-permute-start = (bf16[64,512]{1,0:T(8,128)(2,1)S(1)}, bf16[64,512]{1,0:T(8,128)(2,1)S(1)}, u32[]{:S(2)}, u32[]{:S(2)}) collective-permute-start(bf16[64,512]{1,0:T(8,128)(2,1)S(1)} %get-tuple-element.34), channel_id=1, source_target_pairs={{0,1},{1,0},{2,3},{3,2},{4,5},{5,4},{6,7},{7,6},{8,9},{9,8},{10,11... | collective-permute-start | bytes 196616 | tf_op jit(solution)/shard_map/ppermute | solution.py:247
  11.4 18.8 %copy-start = (s32[512]{0:T(512)S(1)}, s32[512]{0:T(512)}, u32[]{:S(2)}) copy-start(s32[512]{0:T(512)} %param.7) | copy-start | bytes 6148
  11.4 18.8 %copy-start.1 = (s32[512]{0:T(512)S(1)}, s32[512]{0:T(512)}, u32[]{:S(2)}) copy-start(s32[512]{0:T(512)} %param.8) | copy-start | bytes 6148
  30.3 18.1 %copy-start.2 = (f32[16]{0:T(128)S(1)}, f32[16]{0:T(128)}, u32[]{:S(2)}) copy-start(f32[16]{0:T(128)} %param.9) | copy-start | bytes 196
  30.3 18.1 %collective-permute-start.1 = (bf16[1040,256]{1,0:T(8,128)(2,1)S(1)}, bf16[1040,256]{1,0:T(8,128)(2,1)S(1)}, u32[]{:S(2)}, u32[]{:S(2)}) collective-permute-start(bf16[1040,256]{1,0:T(8,128)(2,1)S(1)} %get-tuple-element.18), channel_id=1, source_target_pairs={{0,257},{2,259},{4,261},{6,263},{8,265},{10,267},{12,269},{14,271}... | collective-permute-start | bytes 1597448 | tf_op jit(solution)/shard_map/ppermute | solution.py:255
  41.3 10.6 %collective-permute-start.2 = (bf16[1040,256]{1,0:T(8,128)(2,1)S(1)}, bf16[1040,256]{1,0:T(8,128)(2,1)S(1)}, u32[]{:S(2)}, u32[]{:S(2)}) collective-permute-start(bf16[1040,256]{1,0:T(8,128)(2,1)S(1)} %get-tuple-element.19), channel_id=1, source_target_pairs={{0,33},{2,35},{4,37},{6,39},{8,41},{10,43},{12,45},{14,47},{16,49}... | collective-permute-start | bytes 1597448 | tf_op jit(solution)/shard_map/ppermute | solution.py:256
  49.7 20.4 %collective-permute-start.3 = (bf16[16,128,128]{2,1,0:T(8,128)(2,1)S(1)}, bf16[16,128,128]{2,1,0:T(8,128)(2,1)S(1)}, u32[]{:S(2)}, u32[]{:S(2)}) collective-permute-start(bf16[16,128,128]{2,1,0:T(8,128)(2,1)S(1)} %get-tuple-element.23), channel_id=1, source_target_pairs={{0,1},{2,3},{4,5},{6,7},{8,9},{10,11},{12,13},{14,15},{16,17},{18,... | collective-permute-start | bytes 1572872 | tf_op jit(solution)/shard_map/ppermute | solution.py:271
  53.1 17.0 %collective-permute-start.4 = (bf16[16,128,128]{2,1,0:T(8,128)(2,1)S(1)}, bf16[16,128,128]{2,1,0:T(8,128)(2,1)S(1)}, u32[]{:S(2)}, u32[]{:S(2)}) collective-permute-start(bf16[16,128,128]{2,1,0:T(8,128)(2,1)S(1)} %get-tuple-element.26), channel_id=1, source_target_pairs={{0,1},{2,3},{4,5},{6,7},{8,9},{10,11},{12,13},{14,15},{16,17},{18,... | collective-permute-start | bytes 1572872 | tf_op jit(solution)/shard_map/ppermute | solution.py:275
  94.8 5.3 %collective-permute-start.5 = (f32[72,512]{1,0:T(8,128)S(1)}, f32[72,512]{1,0:T(8,128)S(1)}, u32[]{:S(2)}, u32[]{:S(2)}) collective-permute-start(f32[72,512]{1,0:T(8,128)S(1)} %get-tuple-element.29.give_ref), channel_id=1, source_target_pairs={{0,1},{1,0},{2,3},{3,2},{4,5},{5,4},{6,7},{7,6},{8,9},{9,8},{10,11... | collective-permute-start | bytes 442376 | tf_op jit(solution)/shard_map/ppermute | solution.py:291

commit v12 on v11

--- a/solution.py
+++ b/solution.py
@@ -181,13 +181,15 @@
             give_ref[:rows, columns] = lower[at] * action_scale
 
 
-def last_kernel(n_clip, loss_scale, keep_ref, give_ref, taken_ref, clip_ref, action_ref, loss_ref, sent):
+def last_kernel(n_clip, loss_scale, keep_ref, give_ref, taken_ref, clip_ref, action_ref, loss_ref, loss, sent):
     rows = keep_ref.shape[0]
     half = clip_ref.shape[0]
     core = place(n_clip)[0]
+    loss[...] = (give_ref[rows : rows + 1, :1] + taken_ref[rows : rows + 1, :1]) * loss_scale
 
     def write(clip, action):
-        copies = [pltpu.make_async_copy(clip, clip_ref, sent.at[0]), pltpu.make_async_copy(action, action_ref, sent.at[1])]
+        pairs = [(clip, clip_ref), (action, action_ref), (loss, loss_ref)]
+        copies = [pltpu.make_async_copy(source, target, sent.at[i]) for i, (source, target) in enumerate(pairs)]
         for copy in copies:
             copy.start()
         for copy in copies:
@@ -200,8 +202,6 @@
     @pl.when(core != 0)
     def _():
         write(taken_ref.at[:half, :], keep_ref)
-
-    loss_ref[...] = (give_ref[rows : rows + 1, :1] + taken_ref[rows : rows + 1, :1]) * loss_scale
 
 
 def call(kernel, out_shape, in_specs, out_specs=None, scratch=(), flops=0, moved=0):
@@ -293,8 +293,8 @@
         functools.partial(last_kernel, n_clip, 1.0 / (total_clips * total_actions)),
         (shape((half, count), F32), shape((rows, count), F32), shape((1, 1), F32)),
         [VMEM] * 3,
-        (ANY, ANY, VMEM),
-        [pltpu.SemaphoreType.DMA((2,))],
+        (ANY, ANY, ANY),
+        [pltpu.VMEM((1, 1), F32), pltpu.SemaphoreType.DMA((3,))],
     )(keep, give, taken)
     return clip_grad, action_grad, loss.reshape(())
 

time: 102 us -> 101 us (level)
  no operation moved by 1% of the time
where the time goes in v12:
time: 101 us
  blocking collectives  56.2 us (56%)
  starting transfers between devices  31.2 us (31%)
  waiting for transfers between devices  6.95 us (7%)
  Pallas kernels  4.59 us (5%)
  other arithmetic  1.1 us (1%)
    all_to_all x1, blocking collectives, shards(): scattered = exchange(ready, axis_index_groups=clips_first)  23.7 us
    all_to_all x1, blocking collectives, shards(): own = exchange(chunks, axis_index_groups=clips_first).reshape(width, count)  18.8 us
    all_to_all x1, blocking collectives, shards(): loss_got = exchange(loss_sent, axis_index_groups=actions_first)  13.6 us
    ppermute x1, starting transfers between devices, shards(): low = lax.ppermute(low, both, gather_pass[0])  10.9 us
    ppermute x1, starting transfers between devices, shards(): other = lax.ppermute(send, 'act', swap)  8.79 us
    ppermute x1, waiting for transfers between devices, shards(): low = lax.ppermute(low, both, gather_pass[0])  4.86 us
    ppermute x1, starting transfers between devices, shards(): taken = lax.ppermute(give, 'act', swap)  4.34 us
    ppermute x1, starting transfers between devices, shards(): high_got = lax.ppermute(high_grad, both, scatter_pass[1])  3.35 us
  transfers between devices with their start and end apart: 6, of which 4 were waited for; matrix products, arithmetic and copies ran while one was open for 0% of the time, Pallas kernels for 3%

profile of v12, /device:TPU:1, one launch (start us, length us, event | category | flops | bytes accessed | tf_op | source)
XLA Modules:
  0.0 100.9 jit_solution(6234457756943466072)
XLA Ops:
  0.6 0.9 fusion
  1.6 8.8 %collective-permute-start = (bf16[64,512]{1,0:T(8,128)(2,1)S(1)}, bf16[64,512]{1,0:T(8,128)(2,1)S(1)}, u32[]{:S(2)}, u32[]{:S(2)}) collective-permute-start(bf16[64,512]{1,0:T(8,128)(2,1)S(1)} %get-tuple-element.34), channel_id=1, source_target_pairs={{0,1},{1,0},{2,3},{3,2},{4,5},{5,4},{6,7},{7,6},{8,9},{9,8},{10,11... | collective-permute-start | bytes 196616 | tf_op jit(solution)/shard_map/ppermute | solution.py:247
  10.4 0.9 collective-permute-done
  11.3 0.2 select_select_fusion
  11.4 0.0 copy-start
  11.4 18.8 %all_to_all.15 = bf16[16,64,512]{2,1,0:T(8,128)(2,1)S(1)} all-to-all(bf16[16,64,512]{2,1,0:T(8,128)(2,1)S(1)} %select_select_fusion), channel_id=1, replica_groups={{0,2,4,6,8,10,12,14,16,18,20,22,24,26,28,30},{32,34,36,38,40,42,44,46,4..., dimensions={0} | all-to-all | bytes 2097152 | tf_op jit(solution)/shard_map/all_to_all | solution.py:252
  30.3 0.1 shard_map.76
  30.3 0.0 copy-start.2
  30.3 10.9 %collective-permute-start.1 = (bf16[1040,256]{1,0:T(8,128)(2,1)S(1)}, bf16[1040,256]{1,0:T(8,128)(2,1)S(1)}, u32[]{:S(2)}, u32[]{:S(2)}) collective-permute-start(bf16[1040,256]{1,0:T(8,128)(2,1)S(1)} %get-tuple-element.18), channel_id=1, source_target_pairs={{0,257},{2,259},{4,261},{6,263},{8,265},{10,267},{12,269},{14,271}... | collective-permute-start | bytes 1597448 | tf_op jit(solution)/shard_map/ppermute | solution.py:255
  41.3 1.9 %collective-permute-start.2 = (bf16[1040,256]{1,0:T(8,128)(2,1)S(1)}, bf16[1040,256]{1,0:T(8,128)(2,1)S(1)}, u32[]{:S(2)}, u32[]{:S(2)}) collective-permute-start(bf16[1040,256]{1,0:T(8,128)(2,1)S(1)} %get-tuple-element.19), channel_id=1, source_target_pairs={{0,33},{2,35},{4,37},{6,39},{8,41},{10,43},{12,45},{14,47},{16,49}... | collective-permute-start | bytes 1597448 | tf_op jit(solution)/shard_map/ppermute | solution.py:256
  43.2 0.3 shard_map.77.refs_4_
  43.6 4.9 %collective-permute-done.1.refs_5_.low_ref = bf16[1040,256]{1,0:T(8,128)(2,1)S(1)} collective-permute-done((bf16[1040,256]{1,0:T(8,128)(2,1)S(1)}, bf16[1040,256]{1,0:T(8,128)(2,1)S(1)}, u32[]{:S(2)}, u32[]{:S(2)}) %collective-permute-start.1) | collective-permute-done | bytes 532512 | tf_op jit(solution)/shard_map/ppermute | solution.py:255
  48.4 1.3 %shard_map.78 = (bf16[512,256]{1,0:T(8,128)(2,1)S(1)}, bf16[16,128,128]{2,1,0:T(8,128)(2,1)S(1)}, f32[8,128]{1,0:T(8,128)S(1)}) custom-call(f32[1,16]{1,0:T(1,128)S(1)} %bitcast.22, s32[1,512]{1,0:T(1,128)S(1)} %bitcast.17, s32[1,512]{1,0:T(1,128)S(1)} %bitcast.20, bf16[1024,512]{1,0:T(8,128)(2,1)S(1)} %bitcast.14, bf16[512,1024]{1,0:T(8,128)(2,1)S(1)} %shard_map.77.refs_4_, ...), custom_call_target="tpu_custom_call" | custom-call | flops 536870912 | bytes 2097152 | tf_op jit(solution)/shard_map/pallas_call | solution.py:268
  49.7 1.9 %collective-permute-start.3 = (bf16[16,128,128]{2,1,0:T(8,128)(2,1)S(1)}, bf16[16,128,128]{2,1,0:T(8,128)(2,1)S(1)}, u32[]{:S(2)}, u32[]{:S(2)}) collective-permute-start(bf16[16,128,128]{2,1,0:T(8,128)(2,1)S(1)} %get-tuple-element.23), channel_id=1, source_target_pairs={{0,1},{2,3},{4,5},{6,7},{8,9},{10,11},{12,13},{14,15},{16,17},{18,... | collective-permute-start | bytes 1572872 | tf_op jit(solution)/shard_map/ppermute | solution.py:271
  51.6 0.2 collective-permute-done.2.refs_5_.high_ref
  51.9 1.2 %shard_map.79 = (bf16[512,256]{1,0:T(8,128)(2,1)S(1)}, bf16[16,128,128]{2,1,0:T(8,128)(2,1)S(1)}, bf16[16,16,128]{2,1,0:T(8,128)(2,1)S(1)}) custom-call(f32[1,16]{1,0:T(1,128)S(1)} %bitcast.23, s32[1,512]{1,0:T(1,128)S(1)} %bitcast.18, s32[1,512]{1,0:T(1,128)S(1)} %bitcast.21, bf16[1024,512]{1,0:T(8,128)(2,1)S(1)} %bitcast.15, ...), custom_call_target="tpu_custom_call" | custom-call | flops 536870912 | bytes 2097152 | tf_op jit(solution)/shard_map/pallas_call | solution.py:272
  53.1 3.4 %collective-permute-start.4 = (bf16[16,128,128]{2,1,0:T(8,128)(2,1)S(1)}, bf16[16,128,128]{2,1,0:T(8,128)(2,1)S(1)}, u32[]{:S(2)}, u32[]{:S(2)}) collective-permute-start(bf16[16,128,128]{2,1,0:T(8,128)(2,1)S(1)} %get-tuple-element.26), channel_id=1, source_target_pairs={{0,1},{2,3},{4,5},{6,7},{8,9},{10,11},{12,13},{14,15},{16,17},{18,... | collective-permute-start | bytes 1572872 | tf_op jit(solution)/shard_map/ppermute | solution.py:275
  56.5 13.6 %all_to_all.16.loss_ref = bf16[16,16,128]{2,1,0:T(8,128)(2,1)S(1)} all-to-all(bf16[16,16,128]{2,1,0:T(8,128)(2,1)S(1)} %get-tuple-element.24), channel_id=1, replica_groups={{0,32,64,96,128,160,192,224,256,288,320,352,384,416,448,480},{2,34,66,9..., dimensions={0} | all-to-all | bytes 131072 | tf_op jit(solution)/shard_map/all_to_all | solution.py:276
  70.1 0.8 shard_map.80
  70.9 23.7 %all_to_all.17.got_ref = bf16[16,272,128]{2,1,0:T(8,128)(2,1)S(1)} all-to-all(bf16[16,272,128]{2,1,0:T(8,128)(2,1)S(1)} %shard_map.80), channel_id=1, replica_groups={{0,2,4,6,8,10,12,14,16,18,20,22,24,26,28,30},{32,34,36,38,40,42,44,46,4..., dimensions={0} | all-to-all | bytes 2228224 | tf_op jit(solution)/shard_map/all_to_all | solution.py:282
  94.6 0.2 shard_map.81
  94.8 4.3 %collective-permute-start.5 = (f32[72,512]{1,0:T(8,128)S(1)}, f32[72,512]{1,0:T(8,128)S(1)}, u32[]{:S(2)}, u32[]{:S(2)}) collective-permute-start(f32[72,512]{1,0:T(8,128)S(1)} %get-tuple-element.29.give_ref), channel_id=1, source_target_pairs={{0,1},{1,0},{2,3},{3,2},{4,5},{5,4},{6,7},{7,6},{8,9},{9,8},{10,11... | collective-permute-start | bytes 442376 | tf_op jit(solution)/shard_map/ppermute | solution.py:291
  99.2 1.0 collective-permute-done.5.taken_ref
  100.2 0.7 shard_map.82
  (10 shorter events, 0.0 us)
Async XLA Ops:
  1.6 9.7 %collective-permute-start = (bf16[64,512]{1,0:T(8,128)(2,1)S(1)}, bf16[64,512]{1,0:T(8,128)(2,1)S(1)}, u32[]{:S(2)}, u32[]{:S(2)}) collective-permute-start(bf16[64,512]{1,0:T(8,128)(2,1)S(1)} %get-tuple-element.34), channel_id=1, source_target_pairs={{0,1},{1,0},{2,3},{3,2},{4,5},{5,4},{6,7},{7,6},{8,9},{9,8},{10,11... | collective-permute-start | bytes 196616 | tf_op jit(solution)/shard_map/ppermute | solution.py:247
  11.4 18.8 %copy-start = (s32[512]{0:T(512)S(1)}, s32[512]{0:T(512)}, u32[]{:S(2)}) copy-start(s32[512]{0:T(512)} %param.7) | copy-start | bytes 6148
  11.4 18.8 %copy-start.1 = (s32[512]{0:T(512)S(1)}, s32[512]{0:T(512)}, u32[]{:S(2)}) copy-start(s32[512]{0:T(512)} %param.8) | copy-start | bytes 6148
  30.3 18.1 %copy-start.2 = (f32[16]{0:T(128)S(1)}, f32[16]{0:T(128)}, u32[]{:S(2)}) copy-start(f32[16]{0:T(128)} %param.9) | copy-start | bytes 196
  30.3 18.1 %collective-permute-start.1 = (bf16[1040,256]{1,0:T(8,128)(2,1)S(1)}, bf16[1040,256]{1,0:T(8,128)(2,1)S(1)}, u32[]{:S(2)}, u32[]{:S(2)}) collective-permute-start(bf16[1040,256]{1,0:T(8,128)(2,1)S(1)} %get-tuple-element.18), channel_id=1, source_target_pairs={{0,257},{2,259},{4,261},{6,263},{8,265},{10,267},{12,269},{14,271}... | collective-permute-start | bytes 1597448 | tf_op jit(solution)/shard_map/ppermute | solution.py:255
  41.3 10.6 %collective-permute-start.2 = (bf16[1040,256]{1,0:T(8,128)(2,1)S(1)}, bf16[1040,256]{1,0:T(8,128)(2,1)S(1)}, u32[]{:S(2)}, u32[]{:S(2)}) collective-permute-start(bf16[1040,256]{1,0:T(8,128)(2,1)S(1)} %get-tuple-element.19), channel_id=1, source_target_pairs={{0,33},{2,35},{4,37},{6,39},{8,41},{10,43},{12,45},{14,47},{16,49}... | collective-permute-start | bytes 1597448 | tf_op jit(solution)/shard_map/ppermute | solution.py:256
  49.7 20.4 %collective-permute-start.3 = (bf16[16,128,128]{2,1,0:T(8,128)(2,1)S(1)}, bf16[16,128,128]{2,1,0:T(8,128)(2,1)S(1)}, u32[]{:S(2)}, u32[]{:S(2)}) collective-permute-start(bf16[16,128,128]{2,1,0:T(8,128)(2,1)S(1)} %get-tuple-element.23), channel_id=1, source_target_pairs={{0,1},{2,3},{4,5},{6,7},{8,9},{10,11},{12,13},{14,15},{16,17},{18,... | collective-permute-start | bytes 1572872 | tf_op jit(solution)/shard_map/ppermute | solution.py:271
  53.1 17.0 %collective-permute-start.4 = (bf16[16,128,128]{2,1,0:T(8,128)(2,1)S(1)}, bf16[16,128,128]{2,1,0:T(8,128)(2,1)S(1)}, u32[]{:S(2)}, u32[]{:S(2)}) collective-permute-start(bf16[16,128,128]{2,1,0:T(8,128)(2,1)S(1)} %get-tuple-element.26), channel_id=1, source_target_pairs={{0,1},{2,3},{4,5},{6,7},{8,9},{10,11},{12,13},{14,15},{16,17},{18,... | collective-permute-start | bytes 1572872 | tf_op jit(solution)/shard_map/ppermute | solution.py:275
  94.8 5.3 %collective-permute-start.5 = (f32[72,512]{1,0:T(8,128)S(1)}, f32[72,512]{1,0:T(8,128)S(1)}, u32[]{:S(2)}, u32[]{:S(2)}) collective-permute-start(f32[72,512]{1,0:T(8,128)S(1)} %get-tuple-element.29.give_ref), channel_id=1, source_target_pairs={{0,1},{1,0},{2,3},{3,2},{4,5},{5,4},{6,7},{7,6},{8,9},{9,8},{10,11... | collective-permute-start | bytes 442376 | tf_op jit(solution)/shard_map/ppermute | solution.py:291

commit v13 on v12

--- a/solution.py
+++ b/solution.py
@@ -36,6 +36,10 @@
 
 def block_of(index, blocks):
     return (index // (blocks // 2) + index) % 2
+
+
+def member(position):
+    return position ^ 12
 
 
 def place(n_clip):
@@ -155,7 +159,7 @@
     core = place(blocks)[0]
 
     def over(kind):
-        chosen = [block for block in range(blocks) if block_of(block, blocks) == kind]
+        chosen = [block for block in range(blocks) if block_of(member(block), blocks) == kind]
         total = got_ref[chosen[0]].astype(F32)
         for block in chosen[1:]:
             total = total + got_ref[block].astype(F32)
@@ -220,8 +224,9 @@
     both = ("clip", "act")
     pairs = n_act // 2
     near = n_clip // 2
-    along_act = [[[k * n_act + 2 * m + c for m in range(pairs)] for k in range(n_clip)] for c in range(2)]
-    along_clip = [[[k * n_act + 2 * m + c for k in range(n_clip)] for m in range(pairs)] for c in range(2)]
+    order = [member(i) for i in range(n_clip)]
+    along_act = [[[k * n_act + 2 * m + c for m in order] for k in range(n_clip)] for c in range(2)]
+    along_clip = [[[k * n_act + 2 * m + c for k in order] for m in range(pairs)] for c in range(2)]
     clips_first = along_act[0] + along_clip[1]
     actions_first = along_clip[0] + along_act[1]
     swap = [(i, i ^ 1) for i in range(n_act)]
@@ -246,7 +251,7 @@
     mine = jnp.where(first_core, clip_twice, actions).astype(BF16)
     other = lax.ppermute(send, "act", swap)
     pair = jnp.concatenate([mine[:half], other[:half]], axis=0)
-    takes_mine = block_of(jnp.arange(n_clip), n_clip)[:, None, None] == 1
+    takes_mine = block_of(member(jnp.arange(n_clip)), n_clip)[:, None, None] == 1
     chunks = jnp.where(first_core, pair[None], jnp.where(takes_mine, mine[None], other[None]))
     positive_ids, robot_ids = positive_ids[None, :], robot_ids[None, :]
     own = exchange(chunks, axis_index_groups=clips_first).reshape(width, count)

time: 101 us -> 95.5 us (0.946)
  starting transfers between devices: 31.2 us -> 26.4 us
    ppermute x1, starting transfers between devices: 10.9 us -> 6.51 us  [shards(): low = lax.ppermute(low, both, gather_pass[0])]
    all_to_all x1, blocking collectives: 23.7 us -> 21.6 us  [shards(): scattered = exchange(ready, axis_index_groups=clips_first)]
    all_to_all x1, blocking collectives: 18.8 us -> 20.3 us  [shards(): own = exchange(chunks, axis_index_groups=clips_first).reshape(width, count)]
where the time goes in v13:
time: 95.5 us; the launch traced here: 95.1 us
  blocking collectives  55.2 us (58%)
  starting transfers between devices  26.4 us (28%)
  waiting for transfers between devices  6.94 us (7%)
  Pallas kernels  4.59 us (5%)
  other arithmetic  1.11 us (1%)
    all_to_all x1, blocking collectives, shards(): scattered = exchange(ready, axis_index_groups=clips_first)  21.6 us
    all_to_all x1, blocking collectives, shards(): own = exchange(chunks, axis_index_groups=clips_first).reshape(width, count)  20.3 us
    all_to_all x1, blocking collectives, shards(): loss_got = exchange(loss_sent, axis_index_groups=actions_first)  13.3 us
    ppermute x1, starting transfers between devices, shards(): other = lax.ppermute(send, 'act', swap)  8.79 us
    ppermute x1, starting transfers between devices, shards(): low = lax.ppermute(low, both, gather_pass[0])  6.51 us
    ppermute x1, waiting for transfers between devices, shards(): low = lax.ppermute(low, both, gather_pass[0])  4.86 us
    ppermute x1, starting transfers between devices, shards(): taken = lax.ppermute(give, 'act', swap)  3.93 us
    ppermute x1, starting transfers between devices, shards(): high_got = lax.ppermute(high_grad, both, scatter_pass[1])  3.35 us
  transfers between devices with their start and end apart: 6, of which 4 were waited for; matrix products, arithmetic and copies ran while one was open for 0% of the time, Pallas kernels for 3%

profile of v13, /device:TPU:1, one launch (start us, length us, event | category | flops | bytes accessed | tf_op | source)
XLA Modules:
  0.0 95.1 jit_solution(2349631558799469561)
XLA Ops:
  0.6 0.9 fusion
  1.6 8.8 %collective-permute-start = (bf16[64,512]{1,0:T(8,128)(2,1)S(1)}, bf16[64,512]{1,0:T(8,128)(2,1)S(1)}, u32[]{:S(2)}, u32[]{:S(2)}) collective-permute-start(bf16[64,512]{1,0:T(8,128)(2,1)S(1)} %get-tuple-element.34), channel_id=1, source_target_pairs={{0,1},{1,0},{2,3},{3,2},{4,5},{5,4},{6,7},{7,6},{8,9},{9,8},{10,11... | collective-permute-start | bytes 196616 | tf_op jit(solution)/shard_map/ppermute | solution.py:252
  10.4 0.8 collective-permute-done
  11.3 0.2 select_select_fusion
  11.4 0.0 copy-start
  11.4 20.3 %all_to_all.15 = bf16[16,64,512]{2,1,0:T(8,128)(2,1)S(1)} all-to-all(bf16[16,64,512]{2,1,0:T(8,128)(2,1)S(1)} %select_select_fusion), channel_id=1, replica_groups={{24,26,28,30,16,18,20,22,8,10,12,14,0,2,4,6},{56,58,60,62,48,50,52,54,4..., dimensions={0} | all-to-all | bytes 2097152 | tf_op jit(solution)/shard_map/all_to_all | solution.py:257
  31.8 0.1 shard_map.76
  31.9 0.0 copy-start.2
  31.9 6.5 %collective-permute-start.1 = (bf16[1040,256]{1,0:T(8,128)(2,1)S(1)}, bf16[1040,256]{1,0:T(8,128)(2,1)S(1)}, u32[]{:S(2)}, u32[]{:S(2)}) collective-permute-start(bf16[1040,256]{1,0:T(8,128)(2,1)S(1)} %get-tuple-element.18), channel_id=1, source_target_pairs={{0,257},{2,259},{4,261},{6,263},{8,265},{10,267},{12,269},{14,271}... | collective-permute-start | bytes 1597448 | tf_op jit(solution)/shard_map/ppermute | solution.py:260
  38.4 1.9 %collective-permute-start.2 = (bf16[1040,256]{1,0:T(8,128)(2,1)S(1)}, bf16[1040,256]{1,0:T(8,128)(2,1)S(1)}, u32[]{:S(2)}, u32[]{:S(2)}) collective-permute-start(bf16[1040,256]{1,0:T(8,128)(2,1)S(1)} %get-tuple-element.19), channel_id=1, source_target_pairs={{0,33},{2,35},{4,37},{6,39},{8,41},{10,43},{12,45},{14,47},{16,49}... | collective-permute-start | bytes 1597448 | tf_op jit(solution)/shard_map/ppermute | solution.py:261
  40.3 0.3 shard_map.77.refs_4_
  40.7 4.9 %collective-permute-done.1.refs_5_.low_ref = bf16[1040,256]{1,0:T(8,128)(2,1)S(1)} collective-permute-done((bf16[1040,256]{1,0:T(8,128)(2,1)S(1)}, bf16[1040,256]{1,0:T(8,128)(2,1)S(1)}, u32[]{:S(2)}, u32[]{:S(2)}) %collective-permute-start.1) | collective-permute-done | bytes 532512 | tf_op jit(solution)/shard_map/ppermute | solution.py:260
  45.5 1.3 %shard_map.78 = (bf16[512,256]{1,0:T(8,128)(2,1)S(1)}, bf16[16,128,128]{2,1,0:T(8,128)(2,1)S(1)}, f32[8,128]{1,0:T(8,128)S(1)}) custom-call(f32[1,16]{1,0:T(1,128)S(1)} %bitcast.22, s32[1,512]{1,0:T(1,128)S(1)} %bitcast.17, s32[1,512]{1,0:T(1,128)S(1)} %bitcast.20, bf16[1024,512]{1,0:T(8,128)(2,1)S(1)} %bitcast.14, bf16[512,1024]{1,0:T(8,128)(2,1)S(1)} %shard_map.77.refs_4_, ...), custom_call_target="tpu_custom_call" | custom-call | flops 536870912 | bytes 2097152 | tf_op jit(solution)/shard_map/pallas_call | solution.py:273
  46.8 1.9 %collective-permute-start.3 = (bf16[16,128,128]{2,1,0:T(8,128)(2,1)S(1)}, bf16[16,128,128]{2,1,0:T(8,128)(2,1)S(1)}, u32[]{:S(2)}, u32[]{:S(2)}) collective-permute-start(bf16[16,128,128]{2,1,0:T(8,128)(2,1)S(1)} %get-tuple-element.23), channel_id=1, source_target_pairs={{0,1},{2,3},{4,5},{6,7},{8,9},{10,11},{12,13},{14,15},{16,17},{18,... | collective-permute-start | bytes 1572872 | tf_op jit(solution)/shard_map/ppermute | solution.py:276
  48.7 0.2 collective-permute-done.2.refs_5_.high_ref
  49.0 1.2 %shard_map.79 = (bf16[512,256]{1,0:T(8,128)(2,1)S(1)}, bf16[16,128,128]{2,1,0:T(8,128)(2,1)S(1)}, bf16[16,16,128]{2,1,0:T(8,128)(2,1)S(1)}) custom-call(f32[1,16]{1,0:T(1,128)S(1)} %bitcast.23, s32[1,512]{1,0:T(1,128)S(1)} %bitcast.18, s32[1,512]{1,0:T(1,128)S(1)} %bitcast.21, bf16[1024,512]{1,0:T(8,128)(2,1)S(1)} %bitcast.15, ...), custom_call_target="tpu_custom_call" | custom-call | flops 536870912 | bytes 2097152 | tf_op jit(solution)/shard_map/pallas_call | solution.py:277
  50.2 3.4 %collective-permute-start.4 = (bf16[16,128,128]{2,1,0:T(8,128)(2,1)S(1)}, bf16[16,128,128]{2,1,0:T(8,128)(2,1)S(1)}, u32[]{:S(2)}, u32[]{:S(2)}) collective-permute-start(bf16[16,128,128]{2,1,0:T(8,128)(2,1)S(1)} %get-tuple-element.26), channel_id=1, source_target_pairs={{0,1},{2,3},{4,5},{6,7},{8,9},{10,11},{12,13},{14,15},{16,17},{18,... | collective-permute-start | bytes 1572872 | tf_op jit(solution)/shard_map/ppermute | solution.py:280
  53.6 13.3 %all_to_all.16.loss_ref = bf16[16,16,128]{2,1,0:T(8,128)(2,1)S(1)} all-to-all(bf16[16,16,128]{2,1,0:T(8,128)(2,1)S(1)} %get-tuple-element.24), channel_id=1, replica_groups={{384,416,448,480,256,288,320,352,128,160,192,224,0,32,64,96},{386,418,4..., dimensions={0} | all-to-all | bytes 131072 | tf_op jit(solution)/shard_map/all_to_all | solution.py:281
  66.9 0.8 shard_map.80
  67.6 21.6 %all_to_all.17.got_ref = bf16[16,272,128]{2,1,0:T(8,128)(2,1)S(1)} all-to-all(bf16[16,272,128]{2,1,0:T(8,128)(2,1)S(1)} %shard_map.80), channel_id=1, replica_groups={{24,26,28,30,16,18,20,22,8,10,12,14,0,2,4,6},{56,58,60,62,48,50,52,54,4..., dimensions={0} | all-to-all | bytes 2228224 | tf_op jit(solution)/shard_map/all_to_all | solution.py:287
  89.2 0.2 shard_map.81
  89.4 3.9 %collective-permute-start.5 = (f32[72,512]{1,0:T(8,128)S(1)}, f32[72,512]{1,0:T(8,128)S(1)}, u32[]{:S(2)}, u32[]{:S(2)}) collective-permute-start(f32[72,512]{1,0:T(8,128)S(1)} %get-tuple-element.29.give_ref), channel_id=1, source_target_pairs={{0,1},{1,0},{2,3},{3,2},{4,5},{5,4},{6,7},{7,6},{8,9},{9,8},{10,11... | collective-permute-start | bytes 442376 | tf_op jit(solution)/shard_map/ppermute | solution.py:296
  93.4 1.0 %collective-permute-done.5.taken_ref = f32[72,512]{1,0:T(8,128)S(1)} collective-permute-done((f32[72,512]{1,0:T(8,128)S(1)}, f32[72,512]{1,0:T(8,128)S(1)}, u32[]{:S(2)}, u32[]{:S(2)}) %collective-permute-start.5) | collective-permute-done | bytes 147488 | tf_op jit(solution)/shard_map/ppermute | solution.py:296
  94.4 0.7 shard_map.82
  (10 shorter events, 0.0 us)
Async XLA Ops:
  1.6 9.7 %collective-permute-start = (bf16[64,512]{1,0:T(8,128)(2,1)S(1)}, bf16[64,512]{1,0:T(8,128)(2,1)S(1)}, u32[]{:S(2)}, u32[]{:S(2)}) collective-permute-start(bf16[64,512]{1,0:T(8,128)(2,1)S(1)} %get-tuple-element.34), channel_id=1, source_target_pairs={{0,1},{1,0},{2,3},{3,2},{4,5},{5,4},{6,7},{7,6},{8,9},{9,8},{10,11... | collective-permute-start | bytes 196616 | tf_op jit(solution)/shard_map/ppermute | solution.py:252
  11.4 20.4 %copy-start = (s32[512]{0:T(512)S(1)}, s32[512]{0:T(512)}, u32[]{:S(2)}) copy-start(s32[512]{0:T(512)} %param.7) | copy-start | bytes 6148
  11.4 20.3 %copy-start.1 = (s32[512]{0:T(512)S(1)}, s32[512]{0:T(512)}, u32[]{:S(2)}) copy-start(s32[512]{0:T(512)} %param.8) | copy-start | bytes 6148
  31.9 13.7 %copy-start.2 = (f32[16]{0:T(128)S(1)}, f32[16]{0:T(128)}, u32[]{:S(2)}) copy-start(f32[16]{0:T(128)} %param.9) | copy-start | bytes 196
  31.9 13.7 %collective-permute-start.1 = (bf16[1040,256]{1,0:T(8,128)(2,1)S(1)}, bf16[1040,256]{1,0:T(8,128)(2,1)S(1)}, u32[]{:S(2)}, u32[]{:S(2)}) collective-permute-start(bf16[1040,256]{1,0:T(8,128)(2,1)S(1)} %get-tuple-element.18), channel_id=1, source_target_pairs={{0,257},{2,259},{4,261},{6,263},{8,265},{10,267},{12,269},{14,271}... | collective-permute-start | bytes 1597448 | tf_op jit(solution)/shard_map/ppermute | solution.py:260
  38.4 10.6 %collective-permute-start.2 = (bf16[1040,256]{1,0:T(8,128)(2,1)S(1)}, bf16[1040,256]{1,0:T(8,128)(2,1)S(1)}, u32[]{:S(2)}, u32[]{:S(2)}) collective-permute-start(bf16[1040,256]{1,0:T(8,128)(2,1)S(1)} %get-tuple-element.19), channel_id=1, source_target_pairs={{0,33},{2,35},{4,37},{6,39},{8,41},{10,43},{12,45},{14,47},{16,49}... | collective-permute-start | bytes 1597448 | tf_op jit(solution)/shard_map/ppermute | solution.py:261
  46.8 20.1 %collective-permute-start.3 = (bf16[16,128,128]{2,1,0:T(8,128)(2,1)S(1)}, bf16[16,128,128]{2,1,0:T(8,128)(2,1)S(1)}, u32[]{:S(2)}, u32[]{:S(2)}) collective-permute-start(bf16[16,128,128]{2,1,0:T(8,128)(2,1)S(1)} %get-tuple-element.23), channel_id=1, source_target_pairs={{0,1},{2,3},{4,5},{6,7},{8,9},{10,11},{12,13},{14,15},{16,17},{18,... | collective-permute-start | bytes 1572872 | tf_op jit(solution)/shard_map/ppermute | solution.py:276
  50.2 16.6 %collective-permute-start.4 = (bf16[16,128,128]{2,1,0:T(8,128)(2,1)S(1)}, bf16[16,128,128]{2,1,0:T(8,128)(2,1)S(1)}, u32[]{:S(2)}, u32[]{:S(2)}) collective-permute-start(bf16[16,128,128]{2,1,0:T(8,128)(2,1)S(1)} %get-tuple-element.26), channel_id=1, source_target_pairs={{0,1},{2,3},{4,5},{6,7},{8,9},{10,11},{12,13},{14,15},{16,17},{18,... | collective-permute-start | bytes 1572872 | tf_op jit(solution)/shard_map/ppermute | solution.py:280
  89.4 4.9 %collective-permute-start.5 = (f32[72,512]{1,0:T(8,128)S(1)}, f32[72,512]{1,0:T(8,128)S(1)}, u32[]{:S(2)}, u32[]{:S(2)}) collective-permute-start(f32[72,512]{1,0:T(8,128)S(1)} %get-tuple-element.29.give_ref), channel_id=1, source_target_pairs={{0,1},{1,0},{2,3},{3,2},{4,5},{5,4},{6,7},{7,6},{8,9},{9,8},{10,11... | collective-permute-start | bytes 442376 | tf_op jit(solution)/shard_map/ppermute | solution.py:296

commit v14 on v13

--- a/solution.py
+++ b/solution.py
@@ -11,6 +11,7 @@
 BF16 = jnp.bfloat16
 F32 = jnp.float32
 LANES = 128
+ORDER = (13, 12, 14, 15, 11, 10, 9, 6, 8, 7, 4, 5, 3, 2, 1, 0)
 EXTRA = 16
 VMEM = pl.BlockSpec(memory_space=pltpu.VMEM)
 ANY = pl.BlockSpec(memory_space=pl.ANY)
@@ -39,7 +40,7 @@
 
 
 def member(position):
-    return position ^ 12
+    return ORDER[position]
 
 
 def place(n_clip):
@@ -251,7 +252,7 @@
     mine = jnp.where(first_core, clip_twice, actions).astype(BF16)
     other = lax.ppermute(send, "act", swap)
     pair = jnp.concatenate([mine[:half], other[:half]], axis=0)
-    takes_mine = block_of(member(jnp.arange(n_clip)), n_clip)[:, None, None] == 1
+    takes_mine = jnp.array([block_of(k, n_clip) == 1 for k in order])[:, None, None]
     chunks = jnp.where(first_core, pair[None], jnp.where(takes_mine, mine[None], other[None]))
     positive_ids, robot_ids = positive_ids[None, :], robot_ids[None, :]
     own = exchange(chunks, axis_index_groups=clips_first).reshape(width, count)

time: 95.5 us -> 94.7 us (level)
  starting transfers between devices: 26.4 us -> 23.9 us
    ppermute x1, starting transfers between devices: 6.51 us -> 4.15 us  [shards(): low = lax.ppermute(low, both, gather_pass[0])]
  transfers between devices with their start and end apart: 6 -> 6, of which waited for: 4 -> 3; matrix products, arithmetic and copies ran while one was open for 0% -> 0% of each run, Pallas kernels for 3% -> 3%
where the time goes in v14:
time: 94.7 us; the launch traced here: 94.3 us
  blocking collectives  55.6 us (59%)
  starting transfers between devices  23.9 us (25%)
  waiting for transfers between devices  7.56 us (8%)
  Pallas kernels  4.59 us (5%)
  other arithmetic  1.75 us (2%)
    all_to_all x1, blocking collectives, shards(): scattered = exchange(ready, axis_index_groups=clips_first)  22.2 us
    all_to_all x1, blocking collectives, shards(): own = exchange(chunks, axis_index_groups=clips_first).reshape(width, count)  20.3 us
    all_to_all x1, blocking collectives, shards(): loss_got = exchange(loss_sent, axis_index_groups=actions_first)  13.1 us
    ppermute x1, starting transfers between devices, shards(): other = lax.ppermute(send, 'act', swap)  8.79 us
    ppermute x1, waiting for transfers between devices, shards(): low = lax.ppermute(low, both, gather_pass[0])  5.7 us
    ppermute x1, starting transfers between devices, shards(): low = lax.ppermute(low, both, gather_pass[0])  4.15 us
    ppermute x1, starting transfers between devices, shards(): high_got = lax.ppermute(high_grad, both, scatter_pass[1])  3.59 us
    ppermute x1, starting transfers between devices, shards(): taken = lax.ppermute(give, 'act', swap)  3.56 us
  transfers between devices with their start and end apart: 6, of which 3 were waited for; matrix products, arithmetic and copies ran while one was open for 0% of the time, Pallas kernels for 3%

profile of v14, /device:TPU:1, one launch (start us, length us, event | category | flops | bytes accessed | tf_op | source)
XLA Modules:
  0.0 94.3 jit_solution(14949906431005535321)
XLA Ops:
  0.6 0.9 fusion
  1.6 8.8 %collective-permute-start = (bf16[64,512]{1,0:T(8,128)(2,1)S(1)}, bf16[64,512]{1,0:T(8,128)(2,1)S(1)}, u32[]{:S(2)}, u32[]{:S(2)}) collective-permute-start(bf16[64,512]{1,0:T(8,128)(2,1)S(1)} %get-tuple-element.34), channel_id=1, source_target_pairs={{0,1},{1,0},{2,3},{3,2},{4,5},{5,4},{6,7},{7,6},{8,9},{9,8},{10,11... | collective-permute-start | bytes 196616 | tf_op jit(solution)/shard_map/ppermute | solution.py:253
  10.4 0.9 collective-permute-done
  11.3 0.8 select_select_fusion
  12.1 0.0 copy-start
  12.1 0.0 copy-start.1
  12.1 20.3 %all_to_all.15 = bf16[16,64,512]{2,1,0:T(8,128)(2,1)S(1)} all-to-all(bf16[16,64,512]{2,1,0:T(8,128)(2,1)S(1)} %select_select_fusion), channel_id=1, replica_groups={{26,24,28,30,22,20,18,12,16,14,8,10,6,4,2,0},{58,56,60,62,54,52,50,44,4..., dimensions={0} | all-to-all | bytes 2097152 | tf_op jit(solution)/shard_map/all_to_all | solution.py:258
  32.4 0.1 shard_map.85
  32.5 0.0 copy-start.2
  32.5 4.1 %collective-permute-start.1 = (bf16[1040,256]{1,0:T(8,128)(2,1)S(1)}, bf16[1040,256]{1,0:T(8,128)(2,1)S(1)}, u32[]{:S(2)}, u32[]{:S(2)}) collective-permute-start(bf16[1040,256]{1,0:T(8,128)(2,1)S(1)} %get-tuple-element.18), channel_id=1, source_target_pairs={{0,257},{2,259},{4,261},{6,263},{8,265},{10,267},{12,269},{14,271}... | collective-permute-start | bytes 1597448 | tf_op jit(solution)/shard_map/ppermute | solution.py:261
  36.7 1.9 %collective-permute-start.2 = (bf16[1040,256]{1,0:T(8,128)(2,1)S(1)}, bf16[1040,256]{1,0:T(8,128)(2,1)S(1)}, u32[]{:S(2)}, u32[]{:S(2)}) collective-permute-start(bf16[1040,256]{1,0:T(8,128)(2,1)S(1)} %get-tuple-element.19), channel_id=1, source_target_pairs={{0,33},{2,35},{4,37},{6,39},{8,41},{10,43},{12,45},{14,47},{16,49}... | collective-permute-start | bytes 1597448 | tf_op jit(solution)/shard_map/ppermute | solution.py:262
  38.6 0.3 shard_map.86.refs_4_
  39.0 5.7 %collective-permute-done.1.refs_5_.low_ref = bf16[1040,256]{1,0:T(8,128)(2,1)S(1)} collective-permute-done((bf16[1040,256]{1,0:T(8,128)(2,1)S(1)}, bf16[1040,256]{1,0:T(8,128)(2,1)S(1)}, u32[]{:S(2)}, u32[]{:S(2)}) %collective-permute-start.1) | collective-permute-done | bytes 532512 | tf_op jit(solution)/shard_map/ppermute | solution.py:261
  44.7 1.3 %shard_map.87 = (bf16[512,256]{1,0:T(8,128)(2,1)S(1)}, bf16[16,128,128]{2,1,0:T(8,128)(2,1)S(1)}, f32[8,128]{1,0:T(8,128)S(1)}) custom-call(f32[1,16]{1,0:T(1,128)S(1)} %bitcast.22, s32[1,512]{1,0:T(1,128)S(1)} %bitcast.17, s32[1,512]{1,0:T(1,128)S(1)} %bitcast.20, bf16[1024,512]{1,0:T(8,128)(2,1)S(1)} %bitcast.14, bf16[512,1024]{1,0:T(8,128)(2,1)S(1)} %shard_map.86.refs_4_, ...), custom_call_target="tpu_custom_call" | custom-call | flops 536870912 | bytes 2097152 | tf_op jit(solution)/shard_map/pallas_call | solution.py:274
  45.9 1.9 %collective-permute-start.3 = (bf16[16,128,128]{2,1,0:T(8,128)(2,1)S(1)}, bf16[16,128,128]{2,1,0:T(8,128)(2,1)S(1)}, u32[]{:S(2)}, u32[]{:S(2)}) collective-permute-start(bf16[16,128,128]{2,1,0:T(8,128)(2,1)S(1)} %get-tuple-element.23), channel_id=1, source_target_pairs={{0,1},{2,3},{4,5},{6,7},{8,9},{10,11},{12,13},{14,15},{16,17},{18,... | collective-permute-start | bytes 1572872 | tf_op jit(solution)/shard_map/ppermute | solution.py:277
  47.9 1.2 %shard_map.88 = (bf16[512,256]{1,0:T(8,128)(2,1)S(1)}, bf16[16,128,128]{2,1,0:T(8,128)(2,1)S(1)}, bf16[16,16,128]{2,1,0:T(8,128)(2,1)S(1)}) custom-call(f32[1,16]{1,0:T(1,128)S(1)} %bitcast.23, s32[1,512]{1,0:T(1,128)S(1)} %bitcast.18, s32[1,512]{1,0:T(1,128)S(1)} %bitcast.21, bf16[1024,512]{1,0:T(8,128)(2,1)S(1)} %bitcast.15, ...), custom_call_target="tpu_custom_call" | custom-call | flops 536870912 | bytes 2097152 | tf_op jit(solution)/shard_map/pallas_call | solution.py:278
  49.1 3.6 %collective-permute-start.4 = (bf16[16,128,128]{2,1,0:T(8,128)(2,1)S(1)}, bf16[16,128,128]{2,1,0:T(8,128)(2,1)S(1)}, u32[]{:S(2)}, u32[]{:S(2)}) collective-permute-start(bf16[16,128,128]{2,1,0:T(8,128)(2,1)S(1)} %get-tuple-element.26), channel_id=1, source_target_pairs={{0,1},{2,3},{4,5},{6,7},{8,9},{10,11},{12,13},{14,15},{16,17},{18,... | collective-permute-start | bytes 1572872 | tf_op jit(solution)/shard_map/ppermute | solution.py:281
  52.7 13.1 %all_to_all.16.loss_ref = bf16[16,16,128]{2,1,0:T(8,128)(2,1)S(1)} all-to-all(bf16[16,16,128]{2,1,0:T(8,128)(2,1)S(1)} %get-tuple-element.24), channel_id=1, replica_groups={{416,384,448,480,352,320,288,192,256,224,128,160,96,64,32,0},{418,386,4..., dimensions={0} | all-to-all | bytes 131072 | tf_op jit(solution)/shard_map/all_to_all | solution.py:282
  65.9 0.8 shard_map.89
  66.6 22.2 %all_to_all.17.got_ref = bf16[16,272,128]{2,1,0:T(8,128)(2,1)S(1)} all-to-all(bf16[16,272,128]{2,1,0:T(8,128)(2,1)S(1)} %shard_map.89), channel_id=1, replica_groups={{26,24,28,30,22,20,18,12,16,14,8,10,6,4,2,0},{58,56,60,62,54,52,50,44,4..., dimensions={0} | all-to-all | bytes 2228224 | tf_op jit(solution)/shard_map/all_to_all | solution.py:288
  88.8 0.2 shard_map.90
  89.0 3.6 %collective-permute-start.5 = (f32[72,512]{1,0:T(8,128)S(1)}, f32[72,512]{1,0:T(8,128)S(1)}, u32[]{:S(2)}, u32[]{:S(2)}) collective-permute-start(f32[72,512]{1,0:T(8,128)S(1)} %get-tuple-element.29.give_ref), channel_id=1, source_target_pairs={{0,1},{1,0},{2,3},{3,2},{4,5},{5,4},{6,7},{7,6},{8,9},{9,8},{10,11... | collective-permute-start | bytes 442376 | tf_op jit(solution)/shard_map/ppermute | solution.py:297
  92.6 1.0 %collective-permute-done.5.taken_ref = f32[72,512]{1,0:T(8,128)S(1)} collective-permute-done((f32[72,512]{1,0:T(8,128)S(1)}, f32[72,512]{1,0:T(8,128)S(1)}, u32[]{:S(2)}, u32[]{:S(2)}) %collective-permute-start.5) | collective-permute-done | bytes 147488 | tf_op jit(solution)/shard_map/ppermute | solution.py:297
  93.6 0.7 shard_map.91
  (9 shorter events, 0.0 us)
Async XLA Ops:
  1.6 9.7 %collective-permute-start = (bf16[64,512]{1,0:T(8,128)(2,1)S(1)}, bf16[64,512]{1,0:T(8,128)(2,1)S(1)}, u32[]{:S(2)}, u32[]{:S(2)}) collective-permute-start(bf16[64,512]{1,0:T(8,128)(2,1)S(1)} %get-tuple-element.34), channel_id=1, source_target_pairs={{0,1},{1,0},{2,3},{3,2},{4,5},{5,4},{6,7},{7,6},{8,9},{9,8},{10,11... | collective-permute-start | bytes 196616 | tf_op jit(solution)/shard_map/ppermute | solution.py:253
  12.1 20.4 %copy-start = (s32[512]{0:T(512)S(1)}, s32[512]{0:T(512)}, u32[]{:S(2)}) copy-start(s32[512]{0:T(512)} %param.8) | copy-start | bytes 6148
  12.1 20.3 %copy-start.1 = (s32[512]{0:T(512)S(1)}, s32[512]{0:T(512)}, u32[]{:S(2)}) copy-start(s32[512]{0:T(512)} %param.9) | copy-start | bytes 6148
  32.5 12.1 %copy-start.2 = (f32[16]{0:T(128)S(1)}, f32[16]{0:T(128)}, u32[]{:S(2)}) copy-start(f32[16]{0:T(128)} %param.10) | copy-start | bytes 196
  32.5 12.1 %collective-permute-start.1 = (bf16[1040,256]{1,0:T(8,128)(2,1)S(1)}, bf16[1040,256]{1,0:T(8,128)(2,1)S(1)}, u32[]{:S(2)}, u32[]{:S(2)}) collective-permute-start(bf16[1040,256]{1,0:T(8,128)(2,1)S(1)} %get-tuple-element.18), channel_id=1, source_target_pairs={{0,257},{2,259},{4,261},{6,263},{8,265},{10,267},{12,269},{14,271}... | collective-permute-start | bytes 1597448 | tf_op jit(solution)/shard_map/ppermute | solution.py:261
  36.7 11.2 %collective-permute-start.2 = (bf16[1040,256]{1,0:T(8,128)(2,1)S(1)}, bf16[1040,256]{1,0:T(8,128)(2,1)S(1)}, u32[]{:S(2)}, u32[]{:S(2)}) collective-permute-start(bf16[1040,256]{1,0:T(8,128)(2,1)S(1)} %get-tuple-element.19), channel_id=1, source_target_pairs={{0,33},{2,35},{4,37},{6,39},{8,41},{10,43},{12,45},{14,47},{16,49}... | collective-permute-start | bytes 1597448 | tf_op jit(solution)/shard_map/ppermute | solution.py:262
  45.9 19.9 %collective-permute-start.3 = (bf16[16,128,128]{2,1,0:T(8,128)(2,1)S(1)}, bf16[16,128,128]{2,1,0:T(8,128)(2,1)S(1)}, u32[]{:S(2)}, u32[]{:S(2)}) collective-permute-start(bf16[16,128,128]{2,1,0:T(8,128)(2,1)S(1)} %get-tuple-element.23), channel_id=1, source_target_pairs={{0,1},{2,3},{4,5},{6,7},{8,9},{10,11},{12,13},{14,15},{16,17},{18,... | collective-permute-start | bytes 1572872 | tf_op jit(solution)/shard_map/ppermute | solution.py:277
  49.1 16.7 %collective-permute-start.4 = (bf16[16,128,128]{2,1,0:T(8,128)(2,1)S(1)}, bf16[16,128,128]{2,1,0:T(8,128)(2,1)S(1)}, u32[]{:S(2)}, u32[]{:S(2)}) collective-permute-start(bf16[16,128,128]{2,1,0:T(8,128)(2,1)S(1)} %get-tuple-element.26), channel_id=1, source_target_pairs={{0,1},{2,3},{4,5},{6,7},{8,9},{10,11},{12,13},{14,15},{16,17},{18,... | collective-permute-start | bytes 1572872 | tf_op jit(solution)/shard_map/ppermute | solution.py:281
  89.0 4.6 %collective-permute-start.5 = (f32[72,512]{1,0:T(8,128)S(1)}, f32[72,512]{1,0:T(8,128)S(1)}, u32[]{:S(2)}, u32[]{:S(2)}) collective-permute-start(f32[72,512]{1,0:T(8,128)S(1)} %get-tuple-element.29.give_ref), channel_id=1, source_target_pairs={{0,1},{1,0},{2,3},{3,2},{4,5},{5,4},{6,7},{7,6},{8,9},{9,8},{10,11... | collective-permute-start | bytes 442376 | tf_op jit(solution)/shard_map/ppermute | solution.py:297

commit v15 on v14

--- a/solution.py
+++ b/solution.py
@@ -232,7 +232,7 @@
     actions_first = along_clip[0] + along_act[1]
     swap = [(i, i ^ 1) for i in range(n_act)]
     gather_pass, scatter_pass = [], []
-    for neighbour in (lambda k: (k + near) % n_clip, lambda k: k ^ 1):
+    for neighbour in (lambda k: k ^ 1, lambda k: (k + near) % n_clip):
         there = [(k * n_act + 2 * m, neighbour(k) * n_act + 2 * m + 1) for k in range(n_clip) for m in range(pairs)]
         here = [(k * n_act + 2 * m, k * n_act + 2 * m + 1) for k in range(n_clip) for m in range(pairs)]
         gather_pass.append(there + [(b, a) for a, b in here])

time: 94.7 us -> 94.5 us (level)
  no operation moved by 1% of the time
where the time goes in v15:
time: 94.5 us; the launch traced here: 94.1 us
  blocking collectives  55.6 us (59%)
  starting transfers between devices  23.6 us (25%)
  waiting for transfers between devices  7.7 us (8%)
  Pallas kernels  4.59 us (5%)
  other arithmetic  1.75 us (2%)
    all_to_all x1, blocking collectives, shards(): scattered = exchange(ready, axis_index_groups=clips_first)  22.2 us
    all_to_all x1, blocking collectives, shards(): own = exchange(chunks, axis_index_groups=clips_first).reshape(width, count)  20.3 us
    all_to_all x1, blocking collectives, shards(): loss_got = exchange(loss_sent, axis_index_groups=actions_first)  13.1 us
    ppermute x1, starting transfers between devices, shards(): other = lax.ppermute(send, 'act', swap)  8.79 us
    ppermute x1, waiting for transfers between devices, shards(): low = lax.ppermute(low, both, gather_pass[0])  5.84 us
    ppermute x1, starting transfers between devices, shards(): low = lax.ppermute(low, both, gather_pass[0])  4.15 us
    ppermute x1, starting transfers between devices, shards(): high_got = lax.ppermute(high_grad, both, scatter_pass[1])  3.45 us
    ppermute x1, starting transfers between devices, shards(): taken = lax.ppermute(give, 'act', swap)  3.38 us
  transfers between devices with their start and end apart: 6, of which 3 were waited for; matrix products, arithmetic and copies ran while one was open for 0% of the time, Pallas kernels for 3%

profile of v15, /device:TPU:1, one launch (start us, length us, event | category | flops | bytes accessed | tf_op | source)
XLA Modules:
  0.0 94.1 jit_solution(6013037139326445026)
XLA Ops:
  0.6 0.9 fusion
  1.6 8.8 %collective-permute-start = (bf16[64,512]{1,0:T(8,128)(2,1)S(1)}, bf16[64,512]{1,0:T(8,128)(2,1)S(1)}, u32[]{:S(2)}, u32[]{:S(2)}) collective-permute-start(bf16[64,512]{1,0:T(8,128)(2,1)S(1)} %get-tuple-element.34), channel_id=1, source_target_pairs={{0,1},{1,0},{2,3},{3,2},{4,5},{5,4},{6,7},{7,6},{8,9},{9,8},{10,11... | collective-permute-start | bytes 196616 | tf_op jit(solution)/shard_map/ppermute | solution.py:253
  10.4 0.9 collective-permute-done
  11.3 0.8 select_select_fusion
  12.1 0.0 copy-start
  12.1 0.0 copy-start.1
  12.1 20.3 %all_to_all.15 = bf16[16,64,512]{2,1,0:T(8,128)(2,1)S(1)} all-to-all(bf16[16,64,512]{2,1,0:T(8,128)(2,1)S(1)} %select_select_fusion), channel_id=1, replica_groups={{26,24,28,30,22,20,18,12,16,14,8,10,6,4,2,0},{58,56,60,62,54,52,50,44,4..., dimensions={0} | all-to-all | bytes 2097152 | tf_op jit(solution)/shard_map/all_to_all | solution.py:258
  32.4 0.1 shard_map.85
  32.5 0.0 copy-start.2
  32.5 4.1 %collective-permute-start.1 = (bf16[1040,256]{1,0:T(8,128)(2,1)S(1)}, bf16[1040,256]{1,0:T(8,128)(2,1)S(1)}, u32[]{:S(2)}, u32[]{:S(2)}) collective-permute-start(bf16[1040,256]{1,0:T(8,128)(2,1)S(1)} %get-tuple-element.18), channel_id=1, source_target_pairs={{0,33},{2,35},{4,37},{6,39},{8,41},{10,43},{12,45},{14,47},{16,49}... | collective-permute-start | bytes 1597448 | tf_op jit(solution)/shard_map/ppermute | solution.py:261
  36.7 1.9 %collective-permute-start.2 = (bf16[1040,256]{1,0:T(8,128)(2,1)S(1)}, bf16[1040,256]{1,0:T(8,128)(2,1)S(1)}, u32[]{:S(2)}, u32[]{:S(2)}) collective-permute-start(bf16[1040,256]{1,0:T(8,128)(2,1)S(1)} %get-tuple-element.19), channel_id=1, source_target_pairs={{0,257},{2,259},{4,261},{6,263},{8,265},{10,267},{12,269},{14,271}... | collective-permute-start | bytes 1597448 | tf_op jit(solution)/shard_map/ppermute | solution.py:262
  38.6 0.3 shard_map.86.refs_4_
  39.0 5.8 %collective-permute-done.1.refs_5_.low_ref = bf16[1040,256]{1,0:T(8,128)(2,1)S(1)} collective-permute-done((bf16[1040,256]{1,0:T(8,128)(2,1)S(1)}, bf16[1040,256]{1,0:T(8,128)(2,1)S(1)}, u32[]{:S(2)}, u32[]{:S(2)}) %collective-permute-start.1) | collective-permute-done | bytes 532512 | tf_op jit(solution)/shard_map/ppermute | solution.py:261
  44.8 1.3 %shard_map.87 = (bf16[512,256]{1,0:T(8,128)(2,1)S(1)}, bf16[16,128,128]{2,1,0:T(8,128)(2,1)S(1)}, f32[8,128]{1,0:T(8,128)S(1)}) custom-call(f32[1,16]{1,0:T(1,128)S(1)} %bitcast.22, s32[1,512]{1,0:T(1,128)S(1)} %bitcast.17, s32[1,512]{1,0:T(1,128)S(1)} %bitcast.20, bf16[1024,512]{1,0:T(8,128)(2,1)S(1)} %bitcast.14, bf16[512,1024]{1,0:T(8,128)(2,1)S(1)} %shard_map.86.refs_4_, ...), custom_call_target="tpu_custom_call" | custom-call | flops 536870912 | bytes 2097152 | tf_op jit(solution)/shard_map/pallas_call | solution.py:274
  46.1 1.9 %collective-permute-start.3 = (bf16[16,128,128]{2,1,0:T(8,128)(2,1)S(1)}, bf16[16,128,128]{2,1,0:T(8,128)(2,1)S(1)}, u32[]{:S(2)}, u32[]{:S(2)}) collective-permute-start(bf16[16,128,128]{2,1,0:T(8,128)(2,1)S(1)} %get-tuple-element.23), channel_id=1, source_target_pairs={{0,1},{2,3},{4,5},{6,7},{8,9},{10,11},{12,13},{14,15},{16,17},{18,... | collective-permute-start | bytes 1572872 | tf_op jit(solution)/shard_map/ppermute | solution.py:277
  48.0 1.2 %shard_map.88 = (bf16[512,256]{1,0:T(8,128)(2,1)S(1)}, bf16[16,128,128]{2,1,0:T(8,128)(2,1)S(1)}, bf16[16,16,128]{2,1,0:T(8,128)(2,1)S(1)}) custom-call(f32[1,16]{1,0:T(1,128)S(1)} %bitcast.23, s32[1,512]{1,0:T(1,128)S(1)} %bitcast.18, s32[1,512]{1,0:T(1,128)S(1)} %bitcast.21, bf16[1024,512]{1,0:T(8,128)(2,1)S(1)} %bitcast.15, ...), custom_call_target="tpu_custom_call" | custom-call | flops 536870912 | bytes 2097152 | tf_op jit(solution)/shard_map/pallas_call | solution.py:278
  49.3 3.4 %collective-permute-start.4 = (bf16[16,128,128]{2,1,0:T(8,128)(2,1)S(1)}, bf16[16,128,128]{2,1,0:T(8,128)(2,1)S(1)}, u32[]{:S(2)}, u32[]{:S(2)}) collective-permute-start(bf16[16,128,128]{2,1,0:T(8,128)(2,1)S(1)} %get-tuple-element.26), channel_id=1, source_target_pairs={{0,1},{2,3},{4,5},{6,7},{8,9},{10,11},{12,13},{14,15},{16,17},{18,... | collective-permute-start | bytes 1572872 | tf_op jit(solution)/shard_map/ppermute | solution.py:281
  52.7 13.1 %all_to_all.16.loss_ref = bf16[16,16,128]{2,1,0:T(8,128)(2,1)S(1)} all-to-all(bf16[16,16,128]{2,1,0:T(8,128)(2,1)S(1)} %get-tuple-element.24), channel_id=1, replica_groups={{416,384,448,480,352,320,288,192,256,224,128,160,96,64,32,0},{418,386,4..., dimensions={0} | all-to-all | bytes 131072 | tf_op jit(solution)/shard_map/all_to_all | solution.py:282
  65.9 0.8 shard_map.89
  66.6 22.2 %all_to_all.17.got_ref = bf16[16,272,128]{2,1,0:T(8,128)(2,1)S(1)} all-to-all(bf16[16,272,128]{2,1,0:T(8,128)(2,1)S(1)} %shard_map.89), channel_id=1, replica_groups={{26,24,28,30,22,20,18,12,16,14,8,10,6,4,2,0},{58,56,60,62,54,52,50,44,4..., dimensions={0} | all-to-all | bytes 2228224 | tf_op jit(solution)/shard_map/all_to_all | solution.py:288
  88.8 0.2 shard_map.90
  89.0 3.4 %collective-permute-start.5 = (f32[72,512]{1,0:T(8,128)S(1)}, f32[72,512]{1,0:T(8,128)S(1)}, u32[]{:S(2)}, u32[]{:S(2)}) collective-permute-start(f32[72,512]{1,0:T(8,128)S(1)} %get-tuple-element.29.give_ref), channel_id=1, source_target_pairs={{0,1},{1,0},{2,3},{3,2},{4,5},{5,4},{6,7},{7,6},{8,9},{9,8},{10,11... | collective-permute-start | bytes 442376 | tf_op jit(solution)/shard_map/ppermute | solution.py:297
  92.4 1.0 %collective-permute-done.5.taken_ref = f32[72,512]{1,0:T(8,128)S(1)} collective-permute-done((f32[72,512]{1,0:T(8,128)S(1)}, f32[72,512]{1,0:T(8,128)S(1)}, u32[]{:S(2)}, u32[]{:S(2)}) %collective-permute-start.5) | collective-permute-done | bytes 147488 | tf_op jit(solution)/shard_map/ppermute | solution.py:297
  93.4 0.7 shard_map.91
  (9 shorter events, 0.0 us)
Async XLA Ops:
  1.6 9.7 %collective-permute-start = (bf16[64,512]{1,0:T(8,128)(2,1)S(1)}, bf16[64,512]{1,0:T(8,128)(2,1)S(1)}, u32[]{:S(2)}, u32[]{:S(2)}) collective-permute-start(bf16[64,512]{1,0:T(8,128)(2,1)S(1)} %get-tuple-element.34), channel_id=1, source_target_pairs={{0,1},{1,0},{2,3},{3,2},{4,5},{5,4},{6,7},{7,6},{8,9},{9,8},{10,11... | collective-permute-start | bytes 196616 | tf_op jit(solution)/shard_map/ppermute | solution.py:253
  12.1 20.4 %copy-start = (s32[512]{0:T(512)S(1)}, s32[512]{0:T(512)}, u32[]{:S(2)}) copy-start(s32[512]{0:T(512)} %param.8) | copy-start | bytes 6148
  12.1 20.3 %copy-start.1 = (s32[512]{0:T(512)S(1)}, s32[512]{0:T(512)}, u32[]{:S(2)}) copy-start(s32[512]{0:T(512)} %param.9) | copy-start | bytes 6148
  32.5 12.3 %copy-start.2 = (f32[16]{0:T(128)S(1)}, f32[16]{0:T(128)}, u32[]{:S(2)}) copy-start(f32[16]{0:T(128)} %param.10) | copy-start | bytes 196
  32.5 12.3 %collective-permute-start.1 = (bf16[1040,256]{1,0:T(8,128)(2,1)S(1)}, bf16[1040,256]{1,0:T(8,128)(2,1)S(1)}, u32[]{:S(2)}, u32[]{:S(2)}) collective-permute-start(bf16[1040,256]{1,0:T(8,128)(2,1)S(1)} %get-tuple-element.18), channel_id=1, source_target_pairs={{0,33},{2,35},{4,37},{6,39},{8,41},{10,43},{12,45},{14,47},{16,49}... | collective-permute-start | bytes 1597448 | tf_op jit(solution)/shard_map/ppermute | solution.py:261
  36.7 11.3 %collective-permute-start.2 = (bf16[1040,256]{1,0:T(8,128)(2,1)S(1)}, bf16[1040,256]{1,0:T(8,128)(2,1)S(1)}, u32[]{:S(2)}, u32[]{:S(2)}) collective-permute-start(bf16[1040,256]{1,0:T(8,128)(2,1)S(1)} %get-tuple-element.19), channel_id=1, source_target_pairs={{0,257},{2,259},{4,261},{6,263},{8,265},{10,267},{12,269},{14,271}... | collective-permute-start | bytes 1597448 | tf_op jit(solution)/shard_map/ppermute | solution.py:262
  46.1 19.8 %collective-permute-start.3 = (bf16[16,128,128]{2,1,0:T(8,128)(2,1)S(1)}, bf16[16,128,128]{2,1,0:T(8,128)(2,1)S(1)}, u32[]{:S(2)}, u32[]{:S(2)}) collective-permute-start(bf16[16,128,128]{2,1,0:T(8,128)(2,1)S(1)} %get-tuple-element.23), channel_id=1, source_target_pairs={{0,1},{2,3},{4,5},{6,7},{8,9},{10,11},{12,13},{14,15},{16,17},{18,... | collective-permute-start | bytes 1572872 | tf_op jit(solution)/shard_map/ppermute | solution.py:277
  49.3 16.6 %collective-permute-start.4 = (bf16[16,128,128]{2,1,0:T(8,128)(2,1)S(1)}, bf16[16,128,128]{2,1,0:T(8,128)(2,1)S(1)}, u32[]{:S(2)}, u32[]{:S(2)}) collective-permute-start(bf16[16,128,128]{2,1,0:T(8,128)(2,1)S(1)} %get-tuple-element.26), channel_id=1, source_target_pairs={{0,1},{2,3},{4,5},{6,7},{8,9},{10,11},{12,13},{14,15},{16,17},{18,... | collective-permute-start | bytes 1572872 | tf_op jit(solution)/shard_map/ppermute | solution.py:281
  89.0 4.4 %collective-permute-start.5 = (f32[72,512]{1,0:T(8,128)S(1)}, f32[72,512]{1,0:T(8,128)S(1)}, u32[]{:S(2)}, u32[]{:S(2)}) collective-permute-start(f32[72,512]{1,0:T(8,128)S(1)} %get-tuple-element.29.give_ref), channel_id=1, source_target_pairs={{0,1},{1,0},{2,3},{3,2},{4,5},{5,4},{6,7},{7,6},{8,9},{9,8},{10,11... | collective-permute-start | bytes 442376 | tf_op jit(solution)/shard_map/ppermute | solution.py:297
